TPU v7x, 32 devices: a whole 2x2x4 slice. The times are simulated.
32 devices in a mesh: loop: 4 (over x, core), groups: 8 (over z, y).
Axes of the slice: x: 2, y: 2, z: 4, core: 2. Of those that a mesh axis runs over, the one named last changes fastest.
Arguments:
- states: bfloat16 [4096, 1024], P(('loop', 'groups')), may hold values from -64 to 64
- premises: bfloat16 [4096, 1024], P(('loop', 'groups')), may hold values from -1 to 1
- counts: int32 [4, 8], P('loop', 'groups'), may hold values from 64 to 128, as said below
- partner_mask: int32 [4], P('loop'), may hold values from 0 to 7, as said below
- send_rows: int32 [4, 8, 16], P('loop', 'groups'), may hold values from 0 to 63
- hard_idx: int32 [4096], P(('loop', 'groups')), may hold values from 0 to 15
Outputs:
- loss: float32 [], replicated
- grad_states: bfloat16 [4096, 1024], P(('loop', 'groups'))
- grad_premises: bfloat16 [4096, 1024], P(('loop', 'groups'))
Inputs may be any that keep to these rules, and one draw needn't show every extreme that they name: `counts`: at least 64 valid pairs on every device; some device has all slots valid. `partner_mask`: loop index 0 has the value 8 // 2.
All inputs are finite; a program needn't handle non-finite values.
Results may differ from a plain program's by a relative error of at most 0.0034.
Values may be sent and summed in bfloat16 or wider, within the bound.
No kernel may reach another device: no remote copies, remote signals or barrier semaphores. Data moves between devices by JAX's collectives and lax.ppermute only.
A program may use at most 64 MiB of HBM per device.

v0:
```python
import jax
import jax.numpy as jnp
from jax import lax
from jax.sharding import PartitionSpec as P

SCALE = 3.0


def from_partner(block, axis, apart):
    count = lax.axis_size(axis)
    route = []
    for low in range(count):
        high = low | 1 << apart
        if high != low and high < count:
            route += [(low, high), (high, low)]
    return lax.ppermute(block, axis, route)


def from_behind(value, axis, steps):
    count = lax.axis_size(axis)
    pairs = [(source, (source + steps) % count) for source in range(count)]
    return lax.ppermute(value, axis, pairs)


def body(states, premises, counts, partner_mask, send_rows, hard_idx):
    rows = states.shape[0]
    offer = send_rows.shape[2]
    loop_size = lax.axis_size("loop")
    group_size = lax.axis_size("groups")
    here = lax.axis_index("loop")
    slots = jnp.arange(rows, dtype=jnp.int32)
    valid = slots < counts[0, 0]
    vflt = valid.astype(jnp.float32)
    keys, counts_all = (
        lax.all_gather(premises, "loop", axis=0, tiled=True),
        lax.all_gather(counts, "loop", axis=0, tiled=True),
    )
    column = jnp.arange(loop_size * rows, dtype=jnp.int32)
    limits = jnp.repeat(counts_all[:, 0], rows)
    key_ok = column % rows < limits
    scores = SCALE * jnp.einsum("pd,kd->pk", states, keys, preferred_element_type=jnp.float32)
    masked = jnp.where(key_ok[None, :], scores, -jnp.inf)
    top = jnp.max(masked, axis=1)
    lse = top + jnp.log(jnp.sum(jnp.exp(masked - top[:, None]), axis=1))
    own_block = lax.dynamic_slice_in_dim(scores, here * rows, rows, 1)
    pos = jnp.diagonal(own_block)
    offered = premises[send_rows[0, 0]]
    bits = group_size.bit_length() - 1
    pool = offered
    for level in range(bits):
        other = from_partner(pool, "groups", level)
        pool = jnp.where(partner_mask[0] >> level & 1 == 1, other, pool)
    hard = pool[hard_idx]
    states_f = states.astype(jnp.float32)
    hard_f = hard.astype(jnp.float32)
    tval = SCALE * jnp.sum(states_f * hard_f, axis=-1)
    qval = jnp.where(valid, jax.nn.sigmoid(tval - pos), 0.0)
    terms = jnp.where(valid, lse - pos + jax.nn.softplus(tval - pos), 0.0)
    loss = lax.psum(jnp.sum(terms), ("loop", "groups")) / (loop_size * group_size * rows)
    prob = jnp.where(valid[:, None], jnp.exp(masked - lse[:, None]), 0.0).astype(jnp.bfloat16)
    dstate = jnp.dot(prob, keys, preferred_element_type=jnp.float32)
    grad_states = SCALE * (
        dstate + qval[:, None] * hard_f - (vflt + qval)[:, None] * premises.astype(jnp.float32)
    )

    def visit(step, carry):
        block = jnp.remainder(here - step, loop_size)
        columns = lax.dynamic_slice_in_dim(prob, block * rows, rows, 1)
        carry = carry + jnp.einsum("pk,pd->kd", columns, states, preferred_element_type=jnp.float32)
        return from_behind(carry.astype(jnp.bfloat16), "loop", 1).astype(carry.dtype)

    dprem = lax.fori_loop(0, loop_size, visit, jnp.zeros(states.shape, jnp.float32))
    pick = jax.nn.one_hot(hard_idx, offer, dtype=jnp.float32)
    back = SCALE * jnp.dot(pick.T, qval[:, None] * states_f, precision=lax.Precision.HIGHEST)
    back_home = back
    for level in range(bits):
        other = from_partner(back_home, "groups", level)
        back_home = jnp.where(partner_mask[0] >> level & 1 == 1, other, back_home)
    place = jax.nn.one_hot(send_rows[0, 0], rows, dtype=jnp.float32)
    dhard = jnp.dot(place.T, back_home, precision=lax.Precision.HIGHEST)
    grad_premises = dprem - SCALE * (vflt + qval)[:, None] * states_f + dhard
    return (loss, grad_states.astype(jnp.bfloat16), grad_premises.astype(jnp.bfloat16))


def solution(mesh):
    return jax.shard_map(
        body,
        mesh=mesh,
        in_specs=(
            P(("loop", "groups"), None),
            P(("loop", "groups"), None),
            P("loop", "groups"),
            P("loop"),
            P("loop", "groups", None),
            P(("loop", "groups")),
        ),
        out_specs=(P(), P(("loop", "groups"), None), P(("loop", "groups"), None)),
        check_vma=False,
    )
```

profile of v0, /device:TPU:0, one launch (start us, length us, event | category | flops | bytes accessed | tf_op | source)
XLA Modules:
  0.0 117.5 jit_solution(1754814726871664779)
XLA Ops:
  7.2 0.0 all-gather.2.cloned.1.call-start
  7.2 0.7 all-gather.2.cloned.1.call-update
  8.6 0.6 gather_fusion.1
  9.2 0.0 copy-start.5
  9.2 0.6 copy-done.5
  9.9 0.6 dynamic-slice
  10.5 0.7 bitcast_dynamic-update-slice_fusion
  11.2 3.0 %collective-permute-start.1 = (bf16[16,1024]{1,0:T(8,128)(2,1)S(1)}, bf16[16,1024]{1,0:T(8,128)(2,1)S(1)}, u32[]{:S(2)}, u32[]{:S(2)}) collective-permute-start(bf16[16,1024]{1,0:T(8,128)(2,1)S(1)} %gather_fusion.1), channel_id=1, source_target_pairs={{0,1},{1,0},{2,3},{3,2},{4,5},{5,4},{6,7},{7,6},{8,9},{9,8},{10,11... | collective-permute-start | bytes 98312 | tf_op jit(solution)/shard_map/ppermute | solution.py:16
  14.2 4.9 %all-reduce = s32[4]{0:T(128)S(1)} all-reduce(s32[4]{0:T(128)S(1)} %bitcast_dynamic-update-slice_fusion), channel_id=1, replica_groups=mesh['loop'=4,'groups'=8] {'loop'}, use_global_device_ids=true, to_apply=%add | all-reduce | flops 4 | bytes 32
  19.1 0.1 fusion.15
  19.2 0.6 copy-done.4
  20.4 0.0 collective-permute-done.1
  20.4 1.6 %collective-permute-start.2 = (bf16[16,1024]{1,0:T(8,128)(2,1)S(1)}, bf16[16,1024]{1,0:T(8,128)(2,1)S(1)}, u32[]{:S(2)}, u32[]{:S(2)}) collective-permute-start(bf16[16,1024]{1,0:T(8,128)(2,1)S(1)} %broadcast_select_fusion.1), channel_id=1, source_target_pairs={{0,2},{2,0},{1,3},{3,1},{4,6},{6,4},{5,7},{7,5},{8,10},{10,8},{9,1... | collective-permute-start | bytes 98312 | tf_op jit(solution)/shard_map/ppermute | solution.py:16
  22.1 2.3 %collective-permute-done.2 = bf16[16,1024]{1,0:T(8,128)(2,1)S(1)} collective-permute-done((bf16[16,1024]{1,0:T(8,128)(2,1)S(1)}, bf16[16,1024]{1,0:T(8,128)(2,1)S(1)}, u32[]{:S(2)}, u32[]{:S(2)}) %collective-permute-start.2) | collective-permute-done | bytes 32800 | tf_op jit(solution)/shard_map/ppermute | solution.py:16
  24.4 2.7 %collective-permute-start.3 = (bf16[16,1024]{1,0:T(8,128)(2,1)S(1)}, bf16[16,1024]{1,0:T(8,128)(2,1)S(1)}, u32[]{:S(2)}, u32[]{:S(2)}) collective-permute-start(bf16[16,1024]{1,0:T(8,128)(2,1)S(1)} %broadcast_select_fusion.3), channel_id=1, source_target_pairs={{0,4},{4,0},{1,5},{5,1},{2,6},{6,2},{3,7},{7,3},{8,12},{12,8},{9,1... | collective-permute-start | bytes 98312 | tf_op jit(solution)/shard_map/ppermute | solution.py:16
  27.1 2.2 %collective-permute-done.3 = bf16[16,1024]{1,0:T(8,128)(2,1)S(1)} collective-permute-done((bf16[16,1024]{1,0:T(8,128)(2,1)S(1)}, bf16[16,1024]{1,0:T(8,128)(2,1)S(1)}, u32[]{:S(2)}, u32[]{:S(2)}) %collective-permute-start.3) | collective-permute-done | bytes 32800 | tf_op jit(solution)/shard_map/ppermute | solution.py:16
  29.3 0.9 gather_fusion.2
  30.2 0.1 copy-done
  30.3 0.2 fusion.8
  30.4 0.0 all-gather.2.cloned.1.call-done
  30.4 1.8 %select_reduce_fusion = (f32[128]{0:T(128)S(1)}, f32[128,512]{1,0:T(8,128)S(1)}) fusion(pred[512]{0:T(512)(128)(4,1)S(1)} %fusion.15, bf16[128,1024]{1,0:T(8,128)(2,1)S(1)} %copy-done, bf16[512,1024]{1,0:T(8,128)(2,1)} %all-gather.2.cloned.1.call-done), kind=kOutput, calls=%fused_computation.24 | convolution fusion | flops 134414208 | bytes 1573888 | tf_op jit(solution)/shard_map/pd,kd->pk/dot_general | solution.py:41
  32.3 0.2 exponential_reduce_fusion
  32.5 1.2 %gather_fusion = f32[128]{0:T(128)S(1)} fusion(f32[128,128]{1,0:T(8,128)S(1)} %constant_dynamic-slice_fusion, s32[128]{0:T(128)S(1)} %or_bitcast_fusion), kind=kCustom, calls=%fused_computation | custom fusion | bytes 2048 | tf_op jit(solution)/shard_map/jit(diagonal)/cond/branch_0_fun/gather | solution.py:46
  33.7 0.7 broadcast_multiply_fusion
  34.4 0.4 convolution_multiply_fusion.1
  34.8 0.6 collective-permute-start.4
  35.4 0.1 select_convert_fusion
  35.5 3.6 %collective-permute-done.4 = f32[16,1024]{1,0:T(8,128)S(1)} collective-permute-done((f32[16,1024]{1,0:T(8,128)S(1)}, f32[16,1024]{1,0:T(8,128)S(1)}, u32[]{:S(2)}, u32[]{:S(2)}) %collective-permute-start.4) | collective-permute-done | bytes 65568 | tf_op jit(solution)/shard_map/ppermute | solution.py:16
  39.1 1.6 %collective-permute-start.5 = (f32[16,1024]{1,0:T(8,128)S(1)}, f32[16,1024]{1,0:T(8,128)S(1)}, u32[]{:S(2)}, u32[]{:S(2)}) collective-permute-start(f32[16,1024]{1,0:T(8,128)S(1)} %broadcast_select_fusion), channel_id=1, source_target_pairs={{0,2},{2,0},{1,3},{3,1},{4,6},{6,4},{5,7},{7,5},{8,10},{10,8},{9,1... | collective-permute-start | bytes 196616 | tf_op jit(solution)/shard_map/ppermute | solution.py:16
  40.8 1.0 fusion.7
  41.8 39.9 %psum.7 = f32[]{:T(128)} all-reduce(f32[]{:T(128)} %get-tuple-element.170), channel_id=1, replica_groups=mesh['loop'=4,'groups'=8] {'loop','groups'}, use_global_device_ids=true, to_apply=%region_4.5 | all-reduce | flops 1 | bytes 8 | tf_op jit(solution)/shard_map/psum | solution.py:59
  82.4 0.0 collective-permute-done.5
  82.4 1.1 collective-permute-start.6
  83.5 24.8 %while.16 = (s32[]{:T(128)}, f32[128,1024]{1,0:T(8,128)S(1)}, s32[]{:T(128)}, bf16[128,512]{1,0:T(8,128)(2,1)S(1)}, bf16[128,1024]{1,0:T(8,128)(2,1)S(1)}, /*ind...) while((s32[]{:T(128)}, f32[128,1024]{1,0:T(8,128)S(1)}, ...), condition=%wide.region_6.7_spmd.clone, body=%wide.region_5.6_spmd.clone.sunk | while | flops 34078736 | bytes 2916682 | solution.py:72
  83.5 0.3 fusion.33
  83.8 0.1 collective-permute-start
  83.9 5.8 %collective-permute-done = bf16[128,1024]{1,0:T(8,128)(2,1)S(1)} collective-permute-done((bf16[128,1024]{1,0:T(8,128)(2,1)S(1)}, bf16[128,1024]{1,0:T(8,128)(2,1)S(1)}, u32[]{:S(2)}, u32[]{:S(2)}) %collective-permute-start) | collective-permute-done | bytes 262176 | tf_op jit(solution)/shard_map/while/body/eval_jaxpr/ppermute | solution.py:22
  89.7 0.3 fusion.33
  90.0 0.1 collective-permute-start
  90.1 5.8 %collective-permute-done = bf16[128,1024]{1,0:T(8,128)(2,1)S(1)} collective-permute-done((bf16[128,1024]{1,0:T(8,128)(2,1)S(1)}, bf16[128,1024]{1,0:T(8,128)(2,1)S(1)}, u32[]{:S(2)}, u32[]{:S(2)}) %collective-permute-start) | collective-permute-done | bytes 262176 | tf_op jit(solution)/shard_map/while/body/eval_jaxpr/ppermute | solution.py:22
  95.9 0.3 fusion.33
  96.2 0.1 collective-permute-start
  96.3 5.8 %collective-permute-done = bf16[128,1024]{1,0:T(8,128)(2,1)S(1)} collective-permute-done((bf16[128,1024]{1,0:T(8,128)(2,1)S(1)}, bf16[128,1024]{1,0:T(8,128)(2,1)S(1)}, u32[]{:S(2)}, u32[]{:S(2)}) %collective-permute-start) | collective-permute-done | bytes 262176 | tf_op jit(solution)/shard_map/while/body/eval_jaxpr/ppermute | solution.py:22
  102.1 0.3 fusion.33
  102.4 0.1 collective-permute-start
  102.5 5.8 %collective-permute-done = bf16[128,1024]{1,0:T(8,128)(2,1)S(1)} collective-permute-done((bf16[128,1024]{1,0:T(8,128)(2,1)S(1)}, bf16[128,1024]{1,0:T(8,128)(2,1)S(1)}, u32[]{:S(2)}, u32[]{:S(2)}) %collective-permute-start) | collective-permute-done | bytes 262176 | tf_op jit(solution)/shard_map/while/body/eval_jaxpr/ppermute | solution.py:22
  108.3 0.0 collective-permute-done.6
  108.3 1.2 %fusion.3 = bf16[128,1024]{1,0:T(8,128)(2,1)} fusion(f32[128,1024]{1,0:T(8,128)S(1)} %get-tuple-element.136, bf16[128,1024]{1,0:T(8,128)(2,1)S(1)} %get-tuple-element.239, f32[128]{0:T(128)S(1)} %get-tuple-element.165, f32[16,1024]{1,0:T(8,128)S(1)} %collective-permute-done.6, f32[16,1024]{1,0:T(8,128)S(1)} %broadcast_select_fusion.2, pred[]{:T(512)} %bitcast.5, ...), kind=kOutput, calls=%fused_computation.8 | convolution fusion | flops 25839616 | bytes 1180225 | tf_op jit(solution)/shard_map/dot_general | solution.py:80
  (26 shorter events, 0.3 us)
Async XLA Ops:
  7.2 1.5 %copy-start.2 = (bf16[128,1024]{1,0:T(8,128)(2,1)S(1)}, bf16[128,1024]{1,0:T(8,128)(2,1)}, u32[]{:S(2)}) copy-start(bf16[128,1024]{1,0:T(8,128)(2,1)} %param.9) | copy-start | bytes 786436
  7.2 23.2 %all-gather.2.cloned.1.call-start = ((), (), s32[]{:S(2)}) async-start(), calls=%async_computation | async-start | bytes 1310720 | tf_op jit(solution)/shard_map/all_gather | solution.py:35
  7.9 0.7 copy-start.3
  9.2 0.7 copy-start.5
  11.2 9.3 %collective-permute-start.1 = (bf16[16,1024]{1,0:T(8,128)(2,1)S(1)}, bf16[16,1024]{1,0:T(8,128)(2,1)S(1)}, u32[]{:S(2)}, u32[]{:S(2)}) collective-permute-start(bf16[16,1024]{1,0:T(8,128)(2,1)S(1)} %gather_fusion.1), channel_id=1, source_target_pairs={{0,1},{1,0},{2,3},{3,2},{4,5},{5,4},{6,7},{7,6},{8,9},{9,8},{10,11... | collective-permute-start | bytes 98312 | tf_op jit(solution)/shard_map/ppermute | solution.py:16
  19.1 0.7 copy-start.4
  20.4 4.0 %collective-permute-start.2 = (bf16[16,1024]{1,0:T(8,128)(2,1)S(1)}, bf16[16,1024]{1,0:T(8,128)(2,1)S(1)}, u32[]{:S(2)}, u32[]{:S(2)}) collective-permute-start(bf16[16,1024]{1,0:T(8,128)(2,1)S(1)} %broadcast_select_fusion.1), channel_id=1, source_target_pairs={{0,2},{2,0},{1,3},{3,1},{4,6},{6,4},{5,7},{7,5},{8,10},{10,8},{9,1... | collective-permute-start | bytes 98312 | tf_op jit(solution)/shard_map/ppermute | solution.py:16
  24.4 4.9 %collective-permute-start.3 = (bf16[16,1024]{1,0:T(8,128)(2,1)S(1)}, bf16[16,1024]{1,0:T(8,128)(2,1)S(1)}, u32[]{:S(2)}, u32[]{:S(2)}) collective-permute-start(bf16[16,1024]{1,0:T(8,128)(2,1)S(1)} %broadcast_select_fusion.3), channel_id=1, source_target_pairs={{0,4},{4,0},{1,5},{5,1},{2,6},{6,2},{3,7},{7,3},{8,12},{12,8},{9,1... | collective-permute-start | bytes 98312 | tf_op jit(solution)/shard_map/ppermute | solution.py:16
  29.3 1.0 copy-start
  32.2 8.6 %copy-start.1 = (bf16[512,1024]{1,0:T(8,128)(2,1)S(1)}, bf16[512,1024]{1,0:T(8,128)(2,1)}, u32[]{:S(2)}) copy-start(bf16[512,1024]{1,0:T(8,128)(2,1)} %all-gather.2.cloned.1.call-done) | copy-start | bytes 3145732
  34.8 4.3 %collective-permute-start.4 = (f32[16,1024]{1,0:T(8,128)S(1)}, f32[16,1024]{1,0:T(8,128)S(1)}, u32[]{:S(2)}, u32[]{:S(2)}) collective-permute-start(f32[16,1024]{1,0:T(8,128)S(1)} %convolution_multiply_fusion.1), channel_id=1, source_target_pairs={{0,1},{1,0},{2,3},{3,2},{4,5},{5,4},{6,7},{7,6},{8,9},{9,8},{10,11... | collective-permute-start | bytes 196616 | tf_op jit(solution)/shard_map/ppermute | solution.py:16
  39.1 43.3 %collective-permute-start.5 = (f32[16,1024]{1,0:T(8,128)S(1)}, f32[16,1024]{1,0:T(8,128)S(1)}, u32[]{:S(2)}, u32[]{:S(2)}) collective-permute-start(f32[16,1024]{1,0:T(8,128)S(1)} %broadcast_select_fusion), channel_id=1, source_target_pairs={{0,2},{2,0},{1,3},{3,1},{4,6},{6,4},{5,7},{7,5},{8,10},{10,8},{9,1... | collective-permute-start | bytes 196616 | tf_op jit(solution)/shard_map/ppermute | solution.py:16
  82.4 25.9 %collective-permute-start.6 = (f32[16,1024]{1,0:T(8,128)S(1)}, f32[16,1024]{1,0:T(8,128)S(1)}, u32[]{:S(2)}, u32[]{:S(2)}) collective-permute-start(f32[16,1024]{1,0:T(8,128)S(1)} %broadcast_select_fusion.2), channel_id=1, source_target_pairs={{0,4},{4,0},{1,5},{5,1},{2,6},{6,2},{3,7},{7,3},{8,12},{12,8},{9,1... | collective-permute-start | bytes 196616 | tf_op jit(solution)/shard_map/ppermute | solution.py:16
  83.8 5.8 %collective-permute-start = (bf16[128,1024]{1,0:T(8,128)(2,1)S(1)}, bf16[128,1024]{1,0:T(8,128)(2,1)S(1)}, u32[]{:S(2)}, u32[]{:S(2)}) collective-permute-start(bf16[128,1024]{1,0:T(8,128)(2,1)S(1)} %fusion.33), channel_id=1, source_target_pairs={{0,8},{8,16},{16,24},{24,0},{1,9},{9,17},{17,25},{25,1},{2,10},{10... | collective-permute-start | bytes 786440 | tf_op jit(solution)/shard_map/while/body/eval_jaxpr/ppermute | solution.py:22
  90.0 5.8 %collective-permute-start = (bf16[128,1024]{1,0:T(8,128)(2,1)S(1)}, bf16[128,1024]{1,0:T(8,128)(2,1)S(1)}, u32[]{:S(2)}, u32[]{:S(2)}) collective-permute-start(bf16[128,1024]{1,0:T(8,128)(2,1)S(1)} %fusion.33), channel_id=1, source_target_pairs={{0,8},{8,16},{16,24},{24,0},{1,9},{9,17},{17,25},{25,1},{2,10},{10... | collective-permute-start | bytes 786440 | tf_op jit(solution)/shard_map/while/body/eval_jaxpr/ppermute | solution.py:22
  96.2 5.8 %collective-permute-start = (bf16[128,1024]{1,0:T(8,128)(2,1)S(1)}, bf16[128,1024]{1,0:T(8,128)(2,1)S(1)}, u32[]{:S(2)}, u32[]{:S(2)}) collective-permute-start(bf16[128,1024]{1,0:T(8,128)(2,1)S(1)} %fusion.33), channel_id=1, source_target_pairs={{0,8},{8,16},{16,24},{24,0},{1,9},{9,17},{17,25},{25,1},{2,10},{10... | collective-permute-start | bytes 786440 | tf_op jit(solution)/shard_map/while/body/eval_jaxpr/ppermute | solution.py:22
  102.4 5.8 %collective-permute-start = (bf16[128,1024]{1,0:T(8,128)(2,1)S(1)}, bf16[128,1024]{1,0:T(8,128)(2,1)S(1)}, u32[]{:S(2)}, u32[]{:S(2)}) collective-permute-start(bf16[128,1024]{1,0:T(8,128)(2,1)S(1)} %fusion.33), channel_id=1, source_target_pairs={{0,8},{8,16},{16,24},{24,0},{1,9},{9,17},{17,25},{25,1},{2,10},{10... | collective-permute-start | bytes 786440 | tf_op jit(solution)/shard_map/while/body/eval_jaxpr/ppermute | solution.py:22
Sparse Core Ops, SparseCore 0:
  9.6 19.4 all-gather.1
where the time goes:
time: 118 us
  blocking collectives  44.8 us (38%)
  waiting for transfers between devices  32 us (27%)
  between operations  17.3 us (15%)
  starting transfers between devices  10.9 us (9%)
  matrix products  5.48 us (5%)
  local copies, waits for them, and re-layouts  5.3 us (4%)
  other arithmetic  1.46 us (1%)
    psum x1, blocking collectives, body(): lax.psum(jnp.sum(terms), ('loop', 'groups'))  39.9 us
    ppermute x4, waiting for transfers between devices, from_behind(): return lax.ppermute(value, axis, pairs)  23.1 us
    ppermute x6, starting transfers between devices, from_partner(): return lax.ppermute(block, axis, route)  10.7 us
    ppermute x6, waiting for transfers between devices, from_partner(): return lax.ppermute(block, axis, route)  8.19 us
    unnamed x1, blocking collectives  4.9 us
    unnamed x15, local copies, waits for them, and re-layouts  2.58 us
  transfers between devices with their start and end apart: 11, of which 7 were waited for; matrix products, arithmetic and copies ran while one was open for 5% of the time, Pallas kernels for 0%

commit v1 on v0

v1 whole, which is shorter than its diff:
```python
import functools

import jax
import jax.numpy as jnp
from jax import lax
from jax.experimental import pallas as pl
from jax.experimental.pallas import tpu as pltpu
from jax.sharding import PartitionSpec as P

SCALE = 3.0
LANES = 128
F32 = jnp.float32
BF16 = jnp.bfloat16
VMEM = pl.BlockSpec(memory_space=pltpu.VMEM)
SMEM = pl.BlockSpec(memory_space=pltpu.SMEM)
PARAMS = pltpu.CompilerParams(vmem_limit_bytes=40 << 20)


def swap(block, axis, mask):
    count = lax.axis_size(axis)
    return lax.ppermute(block, axis, [(i, i ^ mask) for i in range(count)])


def dot(a, b, dims):
    return lax.dot_general(a, b, (dims, ((), ())), preferred_element_type=F32)


def total(x):
    return jnp.sum(jnp.sum(x, axis=0, keepdims=True), axis=1, keepdims=True)


def parts(x):
    hi = x.astype(BF16)
    rest = x - hi.astype(F32)
    mid = rest.astype(BF16)
    low = (rest - mid.astype(F32)).astype(BF16)
    return hi, mid, low


def place_of(rows, picked):
    slot = lax.broadcasted_iota(jnp.int32, (rows, picked.shape[1]), 0)
    return jnp.where(slot == picked, 1.0, 0.0).astype(BF16)


def pack(message, block, scalar):
    width = block.shape[1]
    message[:, :width] = block.astype(BF16)
    for i, piece in enumerate(parts(jnp.broadcast_to(scalar, (block.shape[0], LANES)))):
        message[:, width + i * LANES : width + (i + 1) * LANES] = piece


def unpack(message):
    width = message.shape[1] - 3 * LANES
    pieces = [
        message[:, width + i * LANES : width + (i + 1) * LANES].astype(F32)
        for i in range(3)
    ]
    return message[:, :width], (pieces[0] + pieces[1] + pieces[2])[0:1, 0:1]


def merge_kernel(level, mine, other, mask, out, summed):
    block, scalar = unpack(mine)
    other_block, other_scalar = unpack(other)
    take = mask[0] >> level & 1
    block = jnp.where(jnp.full(block.shape, take, jnp.int32) == 1, other_block, block)
    scalar = scalar + other_scalar
    pack(out, block, scalar)
    summed[...] = jnp.broadcast_to(scalar, summed.shape)


def offer_kernel(premises, send_rows, counts, offered, limit):
    place = place_of(premises.shape[0], send_rows[...])
    offered[...] = dot(place, premises[...], ((0,), (0,))).astype(BF16)
    limit[...] = jnp.full(limit.shape, counts[0, 0], jnp.int32)


def hard_kernel(states, premises, pool, hard_idx, counts, qval, back, soft):
    rows, offer = states.shape[0], pool.shape[0]
    which = lax.broadcasted_iota(jnp.int32, (offer, rows), 0)
    pick = jnp.where(which == hard_idx[...], 1.0, 0.0)
    hard = dot(pick.astype(BF16), pool[...], ((0,), (0,)))
    states_f = states[...].astype(F32)
    tval = SCALE * jnp.sum(states_f * hard, axis=1, keepdims=True)
    pos = SCALE * jnp.sum(states_f * premises[...].astype(F32), axis=1, keepdims=True)
    valid = lax.broadcasted_iota(jnp.int32, (rows, 1), 0) < counts[0, 0]
    gap = tval - pos
    q = jnp.where(valid, 1.0 / (1.0 + jnp.exp(-gap)), 0.0)
    plus = jnp.maximum(gap, 0.0) + jnp.log(1.0 + jnp.exp(-jnp.abs(gap)))
    qval[...] = jnp.broadcast_to(q, qval.shape)
    soft[...] = jnp.broadcast_to(total(jnp.where(valid, plus - pos, 0.0)), soft.shape)
    weight = jnp.broadcast_to(q, (rows, rows)).T[:offer] * pick
    split = jnp.concatenate(parts(weight), axis=0)
    summed = dot(split, states[...], ((1,), (0,)))
    back[...] = SCALE * (
        summed[:offer] + summed[offer : 2 * offer] + summed[2 * offer :]
    )


def softmax(rows_block, keys, limits):
    rows = keys[0].shape[0]
    column = lax.broadcasted_iota(jnp.int32, (1, rows), 1)
    scores = []
    top = None
    for key, limit in zip(keys, limits):
        block = SCALE * dot(rows_block, key[...], ((1,), (1,)))
        block = jnp.where(column < limit[0:1, :], block, -jnp.inf)
        scores.append(block)
        best = jnp.max(block, axis=1, keepdims=True)
        top = best if top is None else jnp.maximum(top, best)
    weights = [jnp.exp(block - top) for block in scores]
    mass = sum(jnp.sum(w, axis=1, keepdims=True) for w in weights)
    return weights, top + jnp.log(mass), 1.0 / mass


def near_kernel(size, *refs):
    keys, limits = refs[:size], refs[size : 2 * size]
    own, sib, soft, soft_sib, back, prob, prob_sib, message = refs[2 * size :]
    rows = own.shape[0]
    slot = lax.broadcasted_iota(jnp.int32, (rows, 1), 0)
    summed = soft[0:1, 0:1] + soft_sib[0:1, 0:1]
    for block, limit, which in ((own, limits[0], 0), (sib, limits[1], 1)):
        weights, lse, inverse = softmax(block[...], keys, limits)
        valid = slot < limit[0:1, 0:1]
        summed = summed + total(jnp.where(valid, lse, 0.0))
        scale = jnp.where(valid, inverse, 0.0)
        if which == 0:
            for b in range(size):
                prob[:, b * rows : (b + 1) * rows] = (weights[b] * scale).astype(BF16)
        else:
            prob_sib[...] = (weights[0] * scale).astype(BF16)
    pack(message, back[...], summed)


def states_kernel(size, *refs):
    keys = refs[:size]
    prob, pool, hard_idx, qval, counts, out = refs[size:]
    rows, offer = keys[0].shape[0], pool.shape[0]
    grad = None
    for b in range(size):
        piece = dot(prob[:, b * rows : (b + 1) * rows], keys[b][...], ((1,), (0,)))
        grad = piece if grad is None else grad + piece
    which = lax.broadcasted_iota(jnp.int32, (offer, rows), 0)
    pick = jnp.where(which == hard_idx[...], 1.0, 0.0).astype(BF16)
    hard = dot(pick, pool[...], ((0,), (0,)))
    valid = lax.broadcasted_iota(jnp.int32, (rows, 1), 0) < counts[0, 0]
    q = qval[:, 0:1]
    vq = jnp.where(valid, 1.0, 0.0) + q
    grad = grad + q * hard - vq * keys[0][...].astype(F32)
    out[...] = (SCALE * grad).astype(BF16)


def premises_kernel(size, *refs):
    keys, limits, states = refs[:size], refs[size : 2 * size], refs[2 * size : 3 * size]
    prob, prob_sib, qval, counts, out = refs[3 * size :]
    rows = keys[0].shape[0]
    slot = lax.broadcasted_iota(jnp.int32, (rows, 1), 0)
    grad = dot(prob[:, :rows], states[0][...], ((0,), (0,)))
    grad = grad + dot(prob_sib[...], states[1][...], ((0,), (0,)))
    for b in range(2, size):
        weights, _, inverse = softmax(states[b][...], keys, limits)
        scale = jnp.where(slot < limits[b][0:1, 0:1], inverse, 0.0)
        mine = (weights[0] * scale).astype(BF16)
        grad = grad + dot(mine, states[b][...], ((0,), (0,)))
    vq = jnp.where(slot < counts[0, 0], 1.0, 0.0) + qval[:, 0:1]
    out[...] = grad - SCALE * vq * states[0][...].astype(F32)


def finish_kernel(grad, home, send_rows, out):
    place = place_of(grad.shape[0], send_rows[...])
    out[...] = (grad[...] + dot(place, home[...], ((1,), (0,)))).astype(BF16)


def shape(dims, dtype):
    return jax.ShapeDtypeStruct(dims, dtype)


def spread(held, bits):
    for bit in reversed(range(bits - 1)):
        for m in list(held):
            if m | 1 << bit not in held:
                held[m | 1 << bit] = swap(held[m], "loop", 1 << bit)


def body(states, premises, counts, partner_mask, send_rows, hard_idx):
    rows, width = states.shape
    offer = send_rows.shape[2]
    loop_size = lax.axis_size("loop")
    group_size = lax.axis_size("groups")
    loop_bits = loop_size.bit_length() - 1
    group_bits = group_size.bit_length() - 1
    mask = partner_mask[0]
    sent = send_rows[0]
    index = hard_idx[None, :]

    def after(value, *earlier):
        return lax.optimization_barrier((value, *earlier))[0]

    keys = {0: premises}
    all_states = {0: states}
    top_bit = 1 << (loop_bits - 1)
    keys[top_bit] = swap(premises, "loop", top_bit)
    all_states[top_bit] = swap(states, "loop", top_bit)
    offered, limit = pl.pallas_call(
        offer_kernel,
        out_shape=(shape((offer, width), BF16), shape((8, rows), jnp.int32)),
        in_specs=[VMEM, VMEM, SMEM],
        out_specs=(VMEM, VMEM),
        compiler_params=PARAMS,
        name="offer",
    )(premises, sent, counts)
    limits = {0: limit, top_bit: swap(limit, "loop", top_bit)}

    def route(m):
        return lambda block: block if m == 0 else swap(block, "groups", m)

    pool = lax.switch(mask, [route(m) for m in range(group_size)], offered)

    qval, back, soft = pl.pallas_call(
        hard_kernel,
        out_shape=(
            shape((rows, LANES), F32),
            shape((offer, width), F32),
            shape((8, LANES), F32),
        ),
        in_specs=[VMEM] * 4 + [SMEM],
        out_specs=(VMEM,) * 3,
        compiler_params=PARAMS,
        name="hard",
    )(states, premises, pool, index, counts)
    soft_sib = swap(soft, "loop", 1)
    keys[top_bit] = after(keys[top_bit], soft)
    spread(limits, loop_bits)
    spread(keys, loop_bits)
    keys = [keys[m] for m in range(loop_size)]
    limits = [limits[m] for m in range(loop_size)]
    states_sib = swap(states, "loop", 1)

    prob, prob_sib, message = pl.pallas_call(
        functools.partial(near_kernel, loop_size),
        out_shape=(
            shape((rows, loop_size * rows), BF16),
            shape((rows, rows), BF16),
            shape((offer, width + 3 * LANES), BF16),
        ),
        in_specs=[VMEM] * (2 * loop_size + 5),
        out_specs=(VMEM,) * 3,
        compiler_params=PARAMS,
        name="near",
    )(*keys, *limits, states, states_sib, soft, soft_sib, back)

    for level in range(group_bits):
        message, part = pl.pallas_call(
            functools.partial(merge_kernel, level),
            out_shape=(shape(message.shape, BF16), shape((8, LANES), F32)),
            in_specs=[VMEM, VMEM, SMEM],
            out_specs=(VMEM, VMEM),
            compiler_params=PARAMS,
            name="merge",
        )(message, swap(message, "groups", 1 << level), partner_mask)
    odd = lax.axis_index("loop") & 1

    def across(block):
        for bit in range(1, loop_bits):
            block = block + swap(block, "loop", 1 << bit)
        return block

    part = lax.cond(odd == 1, across, lambda block: block, part)
    part = jnp.where(odd == 1, part, swap(part, "loop", 1))
    loss = part[0, 0] / (loop_size * group_size * rows)
    home = message[:, :width]

    all_states[top_bit] = after(all_states[top_bit], prob)
    spread(all_states, loop_bits)
    all_states[1] = states_sib
    all_states = [all_states[m] for m in range(loop_size)]
    grad_states = pl.pallas_call(
        functools.partial(states_kernel, loop_size),
        out_shape=shape((rows, width), BF16),
        in_specs=[VMEM] * (loop_size + 4) + [SMEM],
        out_specs=VMEM,
        compiler_params=PARAMS,
        name="states",
    )(*keys, prob, pool, index, qval, counts)
    partial_grad = pl.pallas_call(
        functools.partial(premises_kernel, loop_size),
        out_shape=shape((rows, width), F32),
        in_specs=[VMEM] * (3 * loop_size + 3) + [SMEM],
        out_specs=VMEM,
        compiler_params=PARAMS,
        name="premises",
    )(*keys, *limits, *all_states, prob, prob_sib, qval, counts)
    grad_premises = pl.pallas_call(
        finish_kernel,
        out_shape=shape((rows, width), BF16),
        in_specs=[VMEM] * 3,
        out_specs=VMEM,
        compiler_params=PARAMS,
        name="finish",
    )(partial_grad, home, sent)
    return loss, grad_states, grad_premises


def solution(mesh):
    return jax.shard_map(
        body,
        mesh=mesh,
        in_specs=(
            P(("loop", "groups"), None),
            P(("loop", "groups"), None),
            P("loop", "groups"),
            P("loop"),
            P("loop", "groups", None),
            P(("loop", "groups")),
        ),
        out_specs=(P(), P(("loop", "groups"), None), P(("loop", "groups"), None)),
        check_vma=False,
    )
```

time: 118 us -> 47.5 us (0.40)
  blocking collectives: 44.8 us -> 0 us
  between operations: 17.3 us -> 3.79 us
  waiting for transfers between devices: 32 us -> 18.7 us
  Pallas kernels: 0 us -> 7.04 us
  matrix products: 5.48 us -> 0 us
  starting transfers between devices: 10.9 us -> 14.9 us
  local copies, waits for them, and re-layouts: 5.3 us -> 2.76 us
  other arithmetic: 1.46 us -> 0.01 us
    psum x1 -> x0, blocking collectives: 39.9 us -> none  [body(): lax.psum(jnp.sum(terms), ('loop', 'groups'))]
    ppermute x10 -> x15, waiting for transfers between devices: 31.3 us -> 18.7 us  [swap(): return lax.ppermute(block, axis, [(i, i ^ mask) for i in range(count)])]
    pallas_call x0 -> x9, Pallas kernels: none -> 7.04 us  [the longest x1 1.89 us: body(): pl.pallas_call(functools.partial(premises_kernel, loop_size), out_shape=s...]
    dot_general x8 -> x0, matrix products: 5.48 us -> none  [the longest x1 1.79 us: body(): jnp.einsum('pd,kd->pk', states, keys, preferred_element_type=jnp.float32)]
    unnamed x1 -> x0, blocking collectives: 4.9 us -> none
    ppermute x10 -> x15, starting transfers between devices: 10.9 us -> 14.9 us  [swap(): return lax.ppermute(block, axis, [(i, i ^ mask) for i in range(count)])]
    gather x3 -> x0, local copies, waits for them, and re-layouts: 2.7 us -> none  [the longest x1 1.25 us: body(): pos = jnp.diagonal(own_block)]
    unnamed x15 -> x10, local copies, waits for them, and re-layouts: 2.58 us -> 2.24 us
  transfers between devices with their start and end apart: 11 -> 15, of which waited for: 7 -> 8; matrix products, arithmetic and copies ran while one was open for 5% -> 1% of each run, Pallas kernels for 0% -> 9%
where the time goes in v1:
time: 47.5 us; the launch traced here: 47.2 us
  waiting for transfers between devices  18.7 us (39%)
  starting transfers between devices  14.9 us (31%)
  Pallas kernels  7.04 us (15%)
  between operations  3.79 us (8%)
  local copies, waits for them, and re-layouts  2.76 us (6%)
    ppermute x15, waiting for transfers between devices, swap(): return lax.ppermute(block, axis, [(i, i ^ mask) for i in range(count)])  18.7 us
    ppermute x15, starting transfers between devices, swap(): return lax.ppermute(block, axis, [(i, i ^ mask) for i in range(count)])  14.9 us
    unnamed x10, local copies, waits for them, and re-layouts  2.24 us
    pallas_call x1, Pallas kernels, body(): pl.pallas_call(functools.partial(premises_kernel, loop_size), out_shape=s...  1.89 us
    pallas_call x3, Pallas kernels, body(): pl.pallas_call(functools.partial(merge_kernel, level), out_shape=(shape(m...  1.32 us
    pallas_call x1, Pallas kernels, body(): pl.pallas_call(functools.partial(states_kernel, loop_size), out_shape=sha...  1.23 us
    pallas_call x1, Pallas kernels, body(): pl.pallas_call(functools.partial(near_kernel, loop_size), out_shape=(shap...  0.99 us
  transfers between devices with their start and end apart: 15, of which 8 were waited for; matrix products, arithmetic and copies ran while one was open for 1% of the time, Pallas kernels for 9%

profile of v1, /device:TPU:0, one launch (start us, length us, event | category | flops | bytes accessed | tf_op | source)
XLA Modules:
  0.0 47.2 jit_solution(4645741717443076765)
XLA Ops:
  0.6 3.0 %collective-permute-start.9 = (bf16[128,1024]{1,0:T(8,128)(2,1)}, bf16[128,1024]{1,0:T(8,128)(2,1)S(1)}, u32[]{:S(2)}, u32[]{:S(2)}) collective-permute-start(bf16[128,1024]{1,0:T(8,128)(2,1)} %refs_0_.5), channel_id=1, source_target_pairs={{0,16},{8,24},{16,0},{24,8},{1,17},{9,25},{17,1},{25,9},{2,18},{10... | collective-permute-start | bytes 786440 | tf_op jit(solution)/shard_map/ppermute | solution.py:21
  3.6 0.0 collective-permute-start.8
  3.6 0.5 %collective-permute-start.14 = (bf16[128,1024]{1,0:T(8,128)(2,1)}, bf16[128,1024]{1,0:T(8,128)(2,1)S(1)}, u32[]{:S(2)}, u32[]{:S(2)}) collective-permute-start(bf16[128,1024]{1,0:T(8,128)(2,1)} %refs_8_.4), channel_id=1, source_target_pairs={{0,8},{8,0},{16,24},{24,16},{1,9},{9,1},{17,25},{25,17},{2,10},{10... | collective-permute-start | bytes 786440 | tf_op jit(solution)/shard_map/ppermute | solution.py:21
  5.4 0.0 copy-start.4
  5.5 0.6 %copy-done.4 = s32[1,1,16]{2,1,0:T(1,128)S(1)} copy-done((s32[1,1,16]{2,1,0:T(1,128)S(1)}, s32[1,1,16]{2,1,0:T(1,128)}, u32[]{:S(2)}) %copy-start.4) | copy-done | bytes 88
  6.1 0.0 copy-start
  6.1 0.9 %copy-done = bf16[128,1024]{1,0:T(8,128)(2,1)S(1)} copy-done((bf16[128,1024]{1,0:T(8,128)(2,1)S(1)}, bf16[128,1024]{1,0:T(8,128)(2,1)}, u32[]{:S(2)}) %copy-start) | copy-done | bytes 262168
  7.0 0.0 copy-start.2
  7.1 0.2 offer.1
  7.2 5.1 %conditional.2 = (bf16[16,1024]{1,0:T(8,128)(2,1)S(1)}) conditional(s32[]{:T(128)} %bitcast, bf16[16,1024]{1,0:T(8,128)(2,1)S(1)} %get-tuple-element.39, bf16[16,1024]{1,0:T(8,128)(2,1)S(1)} %get-tuple-element.39, bf16[16,1024]{1,0:T(8,128)(2,1)S(1)} %get-tuple-element.39, ...), branch_computations={%region_0.0_spmd, %region_1.0_spmd, %region_2.0_spmd, %region_3.0_... | conditional | bytes 196656 | solution.py:216
  7.2 2.6 %collective-permute-start.3 = (bf16[16,1024]{1,0:T(8,128)(2,1)S(1)}, bf16[16,1024]{1,0:T(8,128)(2,1)S(1)}, u32[]{:S(2)}, u32[]{:S(2)}) collective-permute-start(bf16[16,1024]{1,0:T(8,128)(2,1)S(1)} %param.4), channel_id=1, source_target_pairs={{0,4},{1,5},{2,6},{3,7},{4,0},{5,1},{6,2},{7,3},{8,12},{9,13},{10,... | collective-permute-start | bytes 98312 | tf_op jit(solution)/shard_map/cond/branch_4_fun/ppermute | solution.py:21
  9.9 2.5 %collective-permute-done.3 = bf16[16,1024]{1,0:T(8,128)(2,1)S(1)} collective-permute-done((bf16[16,1024]{1,0:T(8,128)(2,1)S(1)}, bf16[16,1024]{1,0:T(8,128)(2,1)S(1)}, u32[]{:S(2)}, u32[]{:S(2)}) %collective-permute-start.3) | collective-permute-done | bytes 32800 | tf_op jit(solution)/shard_map/cond/branch_4_fun/ppermute | solution.py:21
  12.3 0.0 copy-done.2
  12.4 0.0 copy-done.1
  12.4 0.6 %copy-done.3 = s32[128]{0:T(128)S(1)} copy-done((s32[128]{0:T(128)S(1)}, s32[128]{0:T(128)}, u32[]{:S(2)}) %copy-start.3) | copy-done | bytes 536
  13.0 0.5 %hard.1 = (f32[128,128]{1,0:T(8,128)S(1)}, f32[16,1024]{1,0:T(8,128)S(1)}, f32[8,128]{1,0:T(8,128)S(1)}) custom-call(bf16[128,1024]{1,0:T(8,128)(2,1)S(1)} %copy-done.2, bf16[128,1024]{1,0:T(8,128)(2,1)S(1)} %copy-done.1, bf16[16,1024]{1,0:T(8,128)(2,1)S(1)} %get-tuple-element.53.pool.refs_5_, s32[1,128]{1,0:T(1,128)S(1)} %bitcast.4, ...), custom_call_target="tpu_custom_call" | custom-call | tf_op jit(solution)/shard_map/hard/pallas_call | solution.py:218
  13.5 0.0 collective-permute-done.9.refs_2_
  13.5 0.7 %collective-permute-start.10 = (bf16[128,1024]{1,0:T(8,128)(2,1)S(1)}, bf16[128,1024]{1,0:T(8,128)(2,1)S(1)}, u32[]{:S(2)}, u32[]{:S(2)}) collective-permute-start(bf16[128,1024]{1,0:T(8,128)(2,1)S(1)} %collective-permute-done.9.refs_2_), channel_id=1, source_target_pairs={{0,8},{8,0},{16,24},{24,16},{1,9},{9,1},{17,25},{25,17},{2,10},{10... | collective-permute-start | bytes 786440 | tf_op jit(solution)/shard_map/ppermute | solution.py:21
  14.3 0.0 collective-permute-start.20
  14.3 0.2 collective-permute-start.15
  14.4 1.0 %collective-permute-done.15.refs_11_ = f32[8,128]{1,0:T(8,128)S(1)} collective-permute-done((f32[8,128]{1,0:T(8,128)S(1)}, f32[8,128]{1,0:T(8,128)S(1)}, u32[]{:S(2)}, u32[]{:S(2)}) %collective-permute-start.15) | collective-permute-done | bytes 4128 | tf_op jit(solution)/shard_map/ppermute | solution.py:21
  15.4 2.0 %collective-permute-start.12 = (s32[8,128]{1,0:T(8,128)S(1)}, s32[8,128]{1,0:T(8,128)S(1)}, u32[]{:S(2)}, u32[]{:S(2)}) collective-permute-start(s32[8,128]{1,0:T(8,128)S(1)} %get-tuple-element.42.refs_4_), channel_id=1, source_target_pairs={{0,16},{8,24},{16,0},{24,8},{1,17},{9,25},{17,1},{25,9},{2,18},{10... | collective-permute-start | bytes 12296 | tf_op jit(solution)/shard_map/ppermute | solution.py:21
  17.5 5.2 %collective-permute-done.12.refs_6_ = s32[8,128]{1,0:T(8,128)S(1)} collective-permute-done((s32[8,128]{1,0:T(8,128)S(1)}, s32[8,128]{1,0:T(8,128)S(1)}, u32[]{:S(2)}, u32[]{:S(2)}) %collective-permute-start.12) | collective-permute-done | bytes 4128 | tf_op jit(solution)/shard_map/ppermute | solution.py:21
  22.6 0.0 collective-permute-start.11
  22.6 1.2 %collective-permute-done.11.refs_5_ = s32[8,128]{1,0:T(8,128)S(1)} collective-permute-done((s32[8,128]{1,0:T(8,128)S(1)}, s32[8,128]{1,0:T(8,128)S(1)}, u32[]{:S(2)}, u32[]{:S(2)}) %collective-permute-start.11) | collective-permute-done | bytes 4128 | tf_op jit(solution)/shard_map/ppermute | solution.py:21
  23.8 0.2 collective-permute-start.13
  24.0 1.0 %collective-permute-done.13.refs_7_ = s32[8,128]{1,0:T(8,128)S(1)} collective-permute-done((s32[8,128]{1,0:T(8,128)S(1)}, s32[8,128]{1,0:T(8,128)S(1)}, u32[]{:S(2)}, u32[]{:S(2)}) %collective-permute-start.13) | collective-permute-done | bytes 4128 | tf_op jit(solution)/shard_map/ppermute | solution.py:21
  25.0 0.0 collective-permute-done.8.refs_1_
  25.0 0.0 collective-permute-done.14.refs_9_
  25.0 0.0 collective-permute-done.10.refs_3_
  25.0 1.0 %near.1 = (bf16[128,512]{1,0:T(8,128)(2,1)S(1)}, bf16[128,128]{1,0:T(8,128)(2,1)S(1)}, bf16[16,1408]{1,0:T(8,128)(2,1)S(1)}) custom-call(bf16[128,1024]{1,0:T(8,128)(2,1)S(1)} %copy-done.1, bf16[128,1024]{1,0:T(8,128)(2,1)S(1)} %collective-permute-done.8.refs_1_, bf16[128,1024]{1,0:T(8,128)(2,1)S(1)} %collective-permute-done.9.refs_2_, ...), custom_call_target="tpu_custom_call" | custom-call | tf_op jit(solution)/shard_map/near/pallas_call | solution.py:238
  26.0 1.6 %collective-permute-start.16 = (bf16[16,1408]{1,0:T(8,128)(2,1)S(1)}, bf16[16,1408]{1,0:T(8,128)(2,1)S(1)}, u32[]{:S(2)}, u32[]{:S(2)}) collective-permute-start(bf16[16,1408]{1,0:T(8,128)(2,1)S(1)} %get-tuple-element.44.mine), channel_id=1, source_target_pairs={{0,1},{1,0},{2,3},{3,2},{4,5},{5,4},{6,7},{7,6},{8,9},{9,8},{10,11... | collective-permute-start | bytes 135176 | tf_op jit(solution)/shard_map/ppermute | solution.py:21
  27.6 2.5 %collective-permute-done.16.other = bf16[16,1408]{1,0:T(8,128)(2,1)S(1)} collective-permute-done((bf16[16,1408]{1,0:T(8,128)(2,1)S(1)}, bf16[16,1408]{1,0:T(8,128)(2,1)S(1)}, u32[]{:S(2)}, u32[]{:S(2)}) %collective-permute-start.16) | collective-permute-done | bytes 45088 | tf_op jit(solution)/shard_map/ppermute | solution.py:21
  30.1 0.6 %merge.3 = (bf16[16,1408]{1,0:T(8,128)(2,1)S(1)}, f32[8,128]{1,0:T(8,128)}) custom-call(bf16[16,1408]{1,0:T(8,128)(2,1)S(1)} %get-tuple-element.44.mine, bf16[16,1408]{1,0:T(8,128)(2,1)S(1)} %collective-permute-done.16.other, s32[1]{0:T(128)S(6)} %copy.20.mask), custom_call_target="tpu_custom_call" | custom-call | tf_op jit(solution)/shard_map/merge/pallas_call | solution.py:252
  30.7 1.4 %collective-permute-start.17 = (bf16[16,1408]{1,0:T(8,128)(2,1)S(1)}, bf16[16,1408]{1,0:T(8,128)(2,1)S(1)}, u32[]{:S(2)}, u32[]{:S(2)}) collective-permute-start(bf16[16,1408]{1,0:T(8,128)(2,1)S(1)} %get-tuple-element.45.mine), channel_id=1, source_target_pairs={{0,2},{1,3},{2,0},{3,1},{4,6},{5,7},{6,4},{7,5},{8,10},{9,11},{10,... | collective-permute-start | bytes 135176 | tf_op jit(solution)/shard_map/ppermute | solution.py:21
  32.1 2.7 %collective-permute-done.17.other = bf16[16,1408]{1,0:T(8,128)(2,1)S(1)} collective-permute-done((bf16[16,1408]{1,0:T(8,128)(2,1)S(1)}, bf16[16,1408]{1,0:T(8,128)(2,1)S(1)}, u32[]{:S(2)}, u32[]{:S(2)}) %collective-permute-start.17) | collective-permute-done | bytes 45088 | tf_op jit(solution)/shard_map/ppermute | solution.py:21
  34.8 0.6 %merge.4 = (bf16[16,1408]{1,0:T(8,128)(2,1)S(1)}, f32[8,128]{1,0:T(8,128)}) custom-call(bf16[16,1408]{1,0:T(8,128)(2,1)S(1)} %get-tuple-element.45.mine, bf16[16,1408]{1,0:T(8,128)(2,1)S(1)} %collective-permute-done.17.other, s32[1]{0:T(128)S(6)} %copy.20.mask), custom_call_target="tpu_custom_call" | custom-call | tf_op jit(solution)/shard_map/merge/pallas_call | solution.py:252
  35.4 2.3 %collective-permute-start.18 = (bf16[16,1408]{1,0:T(8,128)(2,1)S(1)}, bf16[16,1408]{1,0:T(8,128)(2,1)S(1)}, u32[]{:S(2)}, u32[]{:S(2)}) collective-permute-start(bf16[16,1408]{1,0:T(8,128)(2,1)S(1)} %get-tuple-element.46.mine), channel_id=1, source_target_pairs={{0,4},{1,5},{2,6},{3,7},{4,0},{5,1},{6,2},{7,3},{8,12},{9,13},{10,... | collective-permute-start | bytes 135176 | tf_op jit(solution)/shard_map/ppermute | solution.py:21
  37.7 0.0 collective-permute-done.20.refs_10_
  37.7 0.0 collective-permute-start.21
  37.7 2.6 %collective-permute-done.18.other = bf16[16,1408]{1,0:T(8,128)(2,1)S(1)} collective-permute-done((bf16[16,1408]{1,0:T(8,128)(2,1)S(1)}, bf16[16,1408]{1,0:T(8,128)(2,1)S(1)}, u32[]{:S(2)}, u32[]{:S(2)}) %collective-permute-start.18) | collective-permute-done | bytes 45088 | tf_op jit(solution)/shard_map/ppermute | solution.py:21
  40.4 0.4 collective-permute-start.19
  40.8 1.2 %states.3 = bf16[128,1024]{1,0:T(8,128)(2,1)} custom-call(bf16[128,1024]{1,0:T(8,128)(2,1)S(1)} %copy-done.1, bf16[128,1024]{1,0:T(8,128)(2,1)S(1)} %collective-permute-done.8.refs_1_, bf16[128,1024]{1,0:T(8,128)(2,1)S(1)} %collective-permute-done.9.refs_2_, bf16[128,1024]{1,0:T(8,128)(2,1)S(1)} %collective-permute-done.10.refs_3_, ...), custom_call_target="tpu_custom_call" | custom-call | tf_op jit(solution)/shard_map/states/pallas_call | solution.py:276
  42.1 0.0 collective-permute-done.19
  42.1 0.5 %slice.6 = f32[1,1]{1,0:T(1,128)} slice(f32[8,128]{1,0:T(8,128)S(1)} %broadcast_select_fusion), slice={[0:1], [0:1]} | slice | bytes 8 | tf_op jit(solution)/shard_map/slice | solution.py:269
  43.2 0.0 collective-permute-done.21.refs_11_
  43.3 1.9 %premises.5.grad = f32[128,1024]{1,0:T(8,128)S(1)} custom-call(bf16[128,1024]{1,0:T(8,128)(2,1)S(1)} %copy-done.1, bf16[128,1024]{1,0:T(8,128)(2,1)S(1)} %collective-permute-done.8.refs_1_, bf16[128,1024]{1,0:T(8,128)(2,1)S(1)} %collective-permute-done.9.refs_2_, bf16[128,1024]{1,0:T(8,128)(2,1)S(1)} %collective-permute-done.10.refs_3_, ...), custom_call_target="tpu_custom_call" | custom-call | tf_op jit(solution)/shard_map/premises/pallas_call | solution.py:284
  45.2 0.9 %finish.1 = bf16[128,1024]{1,0:T(8,128)(2,1)} custom-call(f32[128,1024]{1,0:T(8,128)S(1)} %premises.5.grad, bf16[16,1024]{1,0:T(8,128)(2,1)S(1)} %slice.7.home, s32[1,16]{1,0:T(1,128)S(1)} %bitcast.7), custom_call_target="tpu_custom_call" | custom-call | tf_op jit(solution)/shard_map/finish/pallas_call | solution.py:292
  (7 shorter events, 0.1 us)
Async XLA Ops:
  0.6 12.9 %collective-permute-start.9 = (bf16[128,1024]{1,0:T(8,128)(2,1)}, bf16[128,1024]{1,0:T(8,128)(2,1)S(1)}, u32[]{:S(2)}, u32[]{:S(2)}) collective-permute-start(bf16[128,1024]{1,0:T(8,128)(2,1)} %refs_0_.5), channel_id=1, source_target_pairs={{0,16},{8,24},{16,0},{24,8},{1,17},{9,25},{17,1},{25,9},{2,18},{10... | collective-permute-start | bytes 786440 | tf_op jit(solution)/shard_map/ppermute | solution.py:21
  3.6 21.3 %collective-permute-start.8 = (bf16[128,1024]{1,0:T(8,128)(2,1)}, bf16[128,1024]{1,0:T(8,128)(2,1)S(1)}, u32[]{:S(2)}, u32[]{:S(2)}) collective-permute-start(bf16[128,1024]{1,0:T(8,128)(2,1)} %refs_0_.5), channel_id=1, source_target_pairs={{0,8},{8,0},{16,24},{24,16},{1,9},{9,1},{17,25},{25,17},{2,10},{10... | collective-permute-start | bytes 786440 | tf_op jit(solution)/shard_map/ppermute | solution.py:21
  3.6 21.3 %collective-permute-start.14 = (bf16[128,1024]{1,0:T(8,128)(2,1)}, bf16[128,1024]{1,0:T(8,128)(2,1)S(1)}, u32[]{:S(2)}, u32[]{:S(2)}) collective-permute-start(bf16[128,1024]{1,0:T(8,128)(2,1)} %refs_8_.4), channel_id=1, source_target_pairs={{0,8},{8,0},{16,24},{24,16},{1,9},{9,1},{17,25},{25,17},{2,10},{10... | collective-permute-start | bytes 786440 | tf_op jit(solution)/shard_map/ppermute | solution.py:21
  5.4 0.7 %copy-start.4 = (s32[1,1,16]{2,1,0:T(1,128)S(1)}, s32[1,1,16]{2,1,0:T(1,128)}, u32[]{:S(2)}) copy-start(s32[1,1,16]{2,1,0:T(1,128)} %param.20) | copy-start | bytes 196
  6.1 0.9 %copy-start = (bf16[128,1024]{1,0:T(8,128)(2,1)S(1)}, bf16[128,1024]{1,0:T(8,128)(2,1)}, u32[]{:S(2)}) copy-start(bf16[128,1024]{1,0:T(8,128)(2,1)} %refs_0_.5) | copy-start | bytes 786436
  7.0 5.3 %copy-start.2 = (bf16[128,1024]{1,0:T(8,128)(2,1)S(1)}, bf16[128,1024]{1,0:T(8,128)(2,1)}, u32[]{:S(2)}) copy-start(bf16[128,1024]{1,0:T(8,128)(2,1)} %refs_8_.4) | copy-start | bytes 786436
  7.2 5.1 %copy-start.1 = (bf16[128,1024]{1,0:T(8,128)(2,1)S(1)}, bf16[128,1024]{1,0:T(8,128)(2,1)}, u32[]{:S(2)}) copy-start(bf16[128,1024]{1,0:T(8,128)(2,1)} %refs_0_.5) | copy-start | bytes 786436
  7.2 5.1 %collective-permute-start.3 = (bf16[16,1024]{1,0:T(8,128)(2,1)S(1)}, bf16[16,1024]{1,0:T(8,128)(2,1)S(1)}, u32[]{:S(2)}, u32[]{:S(2)}) collective-permute-start(bf16[16,1024]{1,0:T(8,128)(2,1)S(1)} %param.4), channel_id=1, source_target_pairs={{0,4},{1,5},{2,6},{3,7},{4,0},{5,1},{6,2},{7,3},{8,12},{9,13},{10,... | collective-permute-start | bytes 98312 | tf_op jit(solution)/shard_map/cond/branch_4_fun/ppermute | solution.py:21
  12.3 0.7 %copy-start.3 = (s32[128]{0:T(128)S(1)}, s32[128]{0:T(128)}, u32[]{:S(2)}) copy-start(s32[128]{0:T(128)} %param.21) | copy-start | bytes 1540
  13.5 11.4 %collective-permute-start.10 = (bf16[128,1024]{1,0:T(8,128)(2,1)S(1)}, bf16[128,1024]{1,0:T(8,128)(2,1)S(1)}, u32[]{:S(2)}, u32[]{:S(2)}) collective-permute-start(bf16[128,1024]{1,0:T(8,128)(2,1)S(1)} %collective-permute-done.9.refs_2_), channel_id=1, source_target_pairs={{0,8},{8,0},{16,24},{24,16},{1,9},{9,1},{17,25},{25,17},{2,10},{10... | collective-permute-start | bytes 786440 | tf_op jit(solution)/shard_map/ppermute | solution.py:21
  14.3 23.5 %collective-permute-start.20 = (bf16[128,1024]{1,0:T(8,128)(2,1)S(1)}, bf16[128,1024]{1,0:T(8,128)(2,1)S(1)}, u32[]{:S(2)}, u32[]{:S(2)}) collective-permute-start(bf16[128,1024]{1,0:T(8,128)(2,1)S(1)} %copy-done.2), channel_id=1, source_target_pairs={{0,16},{8,24},{16,0},{24,8},{1,17},{9,25},{17,1},{25,9},{2,18},{10... | collective-permute-start | bytes 786440 | tf_op jit(solution)/shard_map/ppermute | solution.py:21
  14.3 1.2 %collective-permute-start.15 = (f32[8,128]{1,0:T(8,128)S(1)}, f32[8,128]{1,0:T(8,128)S(1)}, u32[]{:S(2)}, u32[]{:S(2)}) collective-permute-start(f32[8,128]{1,0:T(8,128)S(1)} %get-tuple-element.40.refs_10_), channel_id=1, source_target_pairs={{0,8},{8,0},{16,24},{24,16},{1,9},{9,1},{17,25},{25,17},{2,10},{10... | collective-permute-start | bytes 12296 | tf_op jit(solution)/shard_map/ppermute | solution.py:21
  15.4 7.2 %collective-permute-start.12 = (s32[8,128]{1,0:T(8,128)S(1)}, s32[8,128]{1,0:T(8,128)S(1)}, u32[]{:S(2)}, u32[]{:S(2)}) collective-permute-start(s32[8,128]{1,0:T(8,128)S(1)} %get-tuple-element.42.refs_4_), channel_id=1, source_target_pairs={{0,16},{8,24},{16,0},{24,8},{1,17},{9,25},{17,1},{25,9},{2,18},{10... | collective-permute-start | bytes 12296 | tf_op jit(solution)/shard_map/ppermute | solution.py:21
  22.6 1.2 %collective-permute-start.11 = (s32[8,128]{1,0:T(8,128)S(1)}, s32[8,128]{1,0:T(8,128)S(1)}, u32[]{:S(2)}, u32[]{:S(2)}) collective-permute-start(s32[8,128]{1,0:T(8,128)S(1)} %get-tuple-element.42.refs_4_), channel_id=1, source_target_pairs={{0,8},{8,0},{16,24},{24,16},{1,9},{9,1},{17,25},{25,17},{2,10},{10... | collective-permute-start | bytes 12296 | tf_op jit(solution)/shard_map/ppermute | solution.py:21
  23.8 1.2 %collective-permute-start.13 = (s32[8,128]{1,0:T(8,128)S(1)}, s32[8,128]{1,0:T(8,128)S(1)}, u32[]{:S(2)}, u32[]{:S(2)}) collective-permute-start(s32[8,128]{1,0:T(8,128)S(1)} %collective-permute-done.12.refs_6_), channel_id=1, source_target_pairs={{0,8},{8,0},{16,24},{24,16},{1,9},{9,1},{17,25},{25,17},{2,10},{10... | collective-permute-start | bytes 12296 | tf_op jit(solution)/shard_map/ppermute | solution.py:21
  26.0 4.1 %collective-permute-start.16 = (bf16[16,1408]{1,0:T(8,128)(2,1)S(1)}, bf16[16,1408]{1,0:T(8,128)(2,1)S(1)}, u32[]{:S(2)}, u32[]{:S(2)}) collective-permute-start(bf16[16,1408]{1,0:T(8,128)(2,1)S(1)} %get-tuple-element.44.mine), channel_id=1, source_target_pairs={{0,1},{1,0},{2,3},{3,2},{4,5},{5,4},{6,7},{7,6},{8,9},{9,8},{10,11... | collective-permute-start | bytes 135176 | tf_op jit(solution)/shard_map/ppermute | solution.py:21
  30.7 4.0 %collective-permute-start.17 = (bf16[16,1408]{1,0:T(8,128)(2,1)S(1)}, bf16[16,1408]{1,0:T(8,128)(2,1)S(1)}, u32[]{:S(2)}, u32[]{:S(2)}) collective-permute-start(bf16[16,1408]{1,0:T(8,128)(2,1)S(1)} %get-tuple-element.45.mine), channel_id=1, source_target_pairs={{0,2},{1,3},{2,0},{3,1},{4,6},{5,7},{6,4},{7,5},{8,10},{9,11},{10,... | collective-permute-start | bytes 135176 | tf_op jit(solution)/shard_map/ppermute | solution.py:21
  35.4 4.9 %collective-permute-start.18 = (bf16[16,1408]{1,0:T(8,128)(2,1)S(1)}, bf16[16,1408]{1,0:T(8,128)(2,1)S(1)}, u32[]{:S(2)}, u32[]{:S(2)}) collective-permute-start(bf16[16,1408]{1,0:T(8,128)(2,1)S(1)} %get-tuple-element.46.mine), channel_id=1, source_target_pairs={{0,4},{1,5},{2,6},{3,7},{4,0},{5,1},{6,2},{7,3},{8,12},{9,13},{10,... | collective-permute-start | bytes 135176 | tf_op jit(solution)/shard_map/ppermute | solution.py:21
  37.7 5.5 %collective-permute-start.21 = (bf16[128,1024]{1,0:T(8,128)(2,1)S(1)}, bf16[128,1024]{1,0:T(8,128)(2,1)S(1)}, u32[]{:S(2)}, u32[]{:S(2)}) collective-permute-start(bf16[128,1024]{1,0:T(8,128)(2,1)S(1)} %collective-permute-done.20.refs_10_), channel_id=1, source_target_pairs={{0,8},{8,0},{16,24},{24,16},{1,9},{9,1},{17,25},{25,17},{2,10},{10... | collective-permute-start | bytes 786440 | tf_op jit(solution)/shard_map/ppermute | solution.py:21
  40.4 1.6 %collective-permute-start.19 = (f32[8,128]{1,0:T(8,128)S(1)}, f32[8,128]{1,0:T(8,128)S(1)}, u32[]{:S(2)}, u32[]{:S(2)}) collective-permute-start(f32[8,128]{1,0:T(8,128)S(1)} %get-tuple-element.54), channel_id=1, source_target_pairs={{0,8},{8,0},{16,24},{24,16},{1,9},{9,1},{17,25},{25,17},{2,10},{10... | collective-permute-start | bytes 12296 | tf_op jit(solution)/shard_map/ppermute | solution.py:21

commit v2 on v0

v2 whole, which is shorter than its diff:
```python
import functools

import jax
import jax.numpy as jnp
from jax import lax
from jax.experimental import pallas as pl
from jax.experimental.pallas import tpu as pltpu
from jax.sharding import PartitionSpec as P

SCALE = 3.0
LANES = 128
F32 = jnp.float32
BF16 = jnp.bfloat16
VMEM = pl.BlockSpec(memory_space=pltpu.VMEM)
SMEM = pl.BlockSpec(memory_space=pltpu.SMEM)
HBM = pl.BlockSpec(memory_space=pltpu.HBM)


def swap(block, axis, mask):
    count = lax.axis_size(axis)
    return lax.ppermute(block, axis, [(i, i ^ mask) for i in range(count)])


def shape(dims, dtype=BF16):
    return jax.ShapeDtypeStruct(dims, dtype)


def call(kernel, name, outs, *args, ins=None, out_specs=None, scratch=(), cost=0, vmem=40 << 20):
    ins = ins or {}
    return pl.pallas_call(
        kernel,
        out_shape=outs,
        in_specs=[ins.get(i, VMEM) for i in range(len(args))],
        out_specs=out_specs or jax.tree.map(lambda _: VMEM, outs),
        scratch_shapes=scratch,
        compiler_params=pltpu.CompilerParams(vmem_limit_bytes=vmem),
        cost_estimate=pl.CostEstimate(flops=0, bytes_accessed=cost, transcendentals=0),
        name=name,
    )(*args)


def dot(a, b, dims):
    return lax.dot_general(a, b, (dims, ((), ())), preferred_element_type=F32)


def total(x):
    return jnp.sum(jnp.sum(x, axis=0, keepdims=True), axis=1, keepdims=True)


def parts(x):
    hi = x.astype(BF16)
    rest = x - hi.astype(F32)
    mid = rest.astype(BF16)
    low = (rest - mid.astype(F32)).astype(BF16)
    return hi, mid, low


def place_of(rows, picked):
    slot = lax.broadcasted_iota(jnp.int32, (rows, picked.shape[1]), 0)
    return jnp.where(slot == picked, 1.0, 0.0).astype(BF16)


def pick_of(offer, hard_idx):
    which = lax.broadcasted_iota(jnp.int32, (offer, hard_idx.shape[1]), 0)
    return jnp.where(which == hard_idx, 1.0, 0.0)


def column(rows):
    return lax.broadcasted_iota(jnp.int32, (rows, 1), 0).astype(F32)


def pack(message, block, scalar):
    offer, width = block.shape
    message[:, :width] = block.astype(BF16)
    row = lax.broadcasted_iota(jnp.int32, (offer, LANES), 0)
    hi, mid, low = (p.astype(F32) for p in parts(jnp.broadcast_to(scalar, row.shape)))
    spread = jnp.where(row == 0, hi, jnp.where(row == 1, mid, jnp.where(row == 2, low, 0.0)))
    message[:, width:] = spread.astype(BF16)


def unpack(message):
    width = message.shape[1] - LANES
    spread = message[:, width:].astype(F32)
    return message[:, :width], jnp.sum(spread, axis=0, keepdims=True)[:, 0:1]


def mark_kernel(premises, count, marked, held, sem):
    copy = pltpu.make_async_copy(premises, held, sem)
    copy.start()
    copy.wait()
    rows = premises.shape[0]
    row = lax.broadcasted_iota(jnp.int32, (rows, LANES), 0)
    lane = lax.broadcasted_iota(jnp.int32, (rows, LANES), 1)
    invalid = jnp.logical_and(row >= count[0, 0], lane == 0)
    marked[:, LANES:] = held[:, LANES:]
    marked[:, :LANES] = jnp.where(invalid, jnp.inf, held[:, :LANES].astype(F32)).astype(BF16)


def is_valid(key):
    return key[:, 0:1].astype(F32) < jnp.inf


def count_of(meta):
    return meta[3:4, 0:1].astype(F32)


def front_kernel(size, *refs):
    sources, (offered, meta), held = refs[:size], refs[size : size + 2], refs[size + 2 : -1]
    sems = refs[-1]
    copies = [
        pltpu.make_async_copy(source, target, sems.at[i])
        for i, (source, target) in enumerate(zip(sources, held))
    ]
    for copy in copies:
        copy.start()
    for copy in copies:
        copy.wait()
    premises, send_rows, hard_idx, mask, counts = held
    row = lax.broadcasted_iota(jnp.int32, meta.shape, 0)
    meta[...] = jnp.where(
        row == 0, hard_idx[...], jnp.where(row == 2, mask[...], counts[...])
    )
    meta[1:2, 0 : send_rows.shape[1]] = send_rows[...]
    place = place_of(premises.shape[0], send_rows[...])
    offered[...] = dot(place, premises[...], ((0,), (0,))).astype(BF16)


def hard_kernel(states, premises, pool, meta, qval, back, soft):
    rows, offer = states.shape[0], pool.shape[0]
    pick = pick_of(offer, meta[0:1, :])
    hard = dot(pick.astype(BF16), pool[...], ((0,), (0,)))
    states_f = states[...].astype(F32)
    tval = SCALE * jnp.sum(states_f * hard, axis=1, keepdims=True)
    pos = SCALE * jnp.sum(states_f * premises[...].astype(F32), axis=1, keepdims=True)
    valid = column(rows) < count_of(meta)
    gap = tval - pos
    q = jnp.where(valid, 1.0 / (1.0 + jnp.exp(-gap)), 0.0)
    plus = jnp.maximum(gap, 0.0) + jnp.log(1.0 + jnp.exp(-jnp.abs(gap)))
    qval[...] = jnp.broadcast_to(q, qval.shape)
    soft[...] = jnp.broadcast_to(total(jnp.where(valid, plus - pos, 0.0)), soft.shape)
    weight = jnp.broadcast_to(q, (rows, rows)).T[:offer] * pick
    split = jnp.concatenate(parts(weight), axis=0)
    summed = dot(split, states[...], ((1,), (0,)))
    summed = summed[:offer] + summed[offer : 2 * offer] + summed[2 * offer :]
    back[...] = (SCALE * summed).astype(BF16)


def line(width):
    return lax.broadcasted_iota(jnp.int32, (1, width), 1).astype(F32)


def mask_keys(scores, ok):
    return jnp.where(ok, scores, -jnp.inf)


def score(key, block, limit):
    return mask_keys(SCALE * dot(key, block, ((1,), (1,))), column(key.shape[0]) < limit)


def tops(blocks):
    return jnp.max(functools.reduce(jnp.maximum, blocks), axis=0, keepdims=True)


def masses(blocks, top):
    weights = functools.reduce(jnp.add, [jnp.exp(block - top) for block in blocks])
    return jnp.sum(weights, axis=0, keepdims=True)


def early_kernel(size, own, sib, soft, *refs):
    keys, stats = refs[:size], refs[size]
    rows = own.shape[0]
    both = jnp.concatenate([own[...], sib[...]], axis=0)
    oks = [is_valid(key) for key in keys]
    blocks = [mask_keys(SCALE * dot(key[...], both, ((1,), (1,))), ok) for key, ok in zip(keys, oks)]
    top = tops(blocks)
    stats[0:1, :] = top
    stats[1:2, :] = masses(blocks, top)
    info = jnp.broadcast_to(soft[0:1, 0:1], (1, stats.shape[1]))
    for i, ok in enumerate(oks):
        info = jnp.where(line(stats.shape[1]) == 1 + i, total(jnp.where(ok, 1.0, 0.0)), info)
    stats[2:3, :] = info


def limit_of(stats, stats_sib, m):
    return (stats_sib if m & 1 else stats)[2:3, 1 + (m >> 1) : 2 + (m >> 1)]


def valid_lanes(stats, stats_sib, m, rows):
    slots = line(rows)
    pair = [slots < limit_of(stats, stats_sib, m + i) for i in range(2)]
    return jnp.concatenate(pair, axis=1)


def near_kernel(stats, stats_sib, back, lse, message):
    rows = stats.shape[1] // 2
    top, mass = stats[0:1, :], stats[1:2, :]
    flip = [
        jnp.concatenate([stats_sib[i : i + 1, rows:], stats_sib[i : i + 1, :rows]], axis=1)
        for i in range(2)
    ]
    best = jnp.maximum(top, flip[0])
    mass = mass * jnp.exp(top - best) + flip[1] * jnp.exp(flip[0] - best)
    out = best + jnp.log(mass)
    lse[...] = jnp.broadcast_to(out, lse.shape)
    out = jnp.where(valid_lanes(stats, stats_sib, 0, rows), out, 0.0)
    pack(message, back[...], total(out) + stats[2:3, 0:1] + stats_sib[2:3, 0:1])


def merge_kernel(level, last, mine, other, meta, *outs):
    block, scalar = unpack(mine)
    other_block, other_scalar = unpack(other)
    take = meta[2:3, 0:1] >> level & 1
    block = jnp.where(take == 1, other_block.astype(F32), block.astype(F32)).astype(BF16)
    scalar = scalar + other_scalar
    if last:
        outs[0][...] = block
        outs[1][...] = jnp.broadcast_to(scalar, outs[1].shape)
    else:
        pack(outs[0], block, scalar)


def states_kernel(size, *refs):
    keys = refs[:size]
    states, lse, pool, meta, qval, stats, stats_sib, out = refs[size:]
    rows, offer = states.shape[0], pool.shape[0]
    slot = column(rows)
    valid = slot < count_of(meta)
    limits = [limit_of(stats, stats_sib, m) for m in range(size)]
    cleared = [keys[0][...]] + [
        jnp.where(slot < limit, key[...].astype(F32), 0.0).astype(BF16)
        for key, limit in zip(keys[1:], limits[1:])
    ]
    cleared = jnp.concatenate(cleared, axis=0)
    scores = SCALE * dot(states[...], cleared, ((1,), (1,)))
    lse_column = jnp.broadcast_to(lse[0:1, :rows], (rows, rows)).T[:, 0:1]
    ok = jnp.concatenate([line(rows) < limit for limit in limits], axis=1)
    prob = jnp.where(jnp.logical_and(valid, ok), jnp.exp(scores - lse_column), 0.0)
    grad = dot(prob.astype(BF16), cleared, ((1,), (0,)))
    hard = dot(pick_of(offer, meta[0:1, :]).astype(BF16), pool[...], ((0,), (0,)))
    q = qval[:, 0:1]
    vq = jnp.where(valid, 1.0, 0.0) + q
    grad = grad + q * hard - vq * keys[0][...].astype(F32)
    out[...] = (SCALE * grad).astype(BF16)


def premises_kernel(size, *refs):
    keys, states = refs[:size], refs[size : 2 * size]
    lse, meta, qval, stats, stats_sib, out = refs[2 * size :]
    rows = states[0].shape[0]
    grad = None
    for b in range(0, size, 2):
        both = jnp.concatenate([states[b][...], states[b + 1][...]], axis=0)
        mine = score(keys[0][...], both, count_of(meta))
        if b == 0:
            total_lse = lse[0:1, :]
        else:
            blocks = [mine] + [
                score(keys[m][...], both, limit_of(stats, stats_sib, m))
                for m in range(1, size)
            ]
            top = tops(blocks)
            total_lse = top + jnp.log(masses(blocks, top))
        row_ok = valid_lanes(stats, stats_sib, b, rows)
        prob = jnp.where(row_ok, jnp.exp(mine - total_lse), 0.0).astype(BF16)
        piece = dot(prob, both, ((1,), (0,)))
        grad = piece if grad is None else grad + piece
    vq = jnp.where(column(rows) < count_of(meta), 1.0, 0.0) + qval[:, 0:1]
    out[...] = grad - SCALE * vq * states[0][...].astype(F32)


def finish_kernel(count, grad_states, grad, home, meta, part, other, out_states, out, loss):
    place = place_of(grad.shape[0], meta[1:2, 0 : home.shape[0]])
    out[...] = (grad[...] + dot(place, home[...], ((1,), (0,)))).astype(BF16)
    out_states[...] = grad_states[...]
    odd = jnp.full((1, 1), lax.axis_index("loop") & 1, jnp.int32) == 1
    loss[...] = jnp.where(odd, part[0:1, 0:1], other[0:1, 0:1]) / count


def across_chips(held, bits):
    for bit in reversed(range(1, bits)):
        held.update({m | 1 << bit: swap(b, "loop", 1 << bit) for m, b in held.items()})
    return held


def from_sibling(held):
    for m in [m for m in held if not m & 1 and m | 1 not in held]:
        held[m | 1] = swap(held[m], "loop", 1)
    return [held[m] for m in range(len(held))]


def body(states, premises, counts, partner_mask, send_rows, hard_idx):
    rows, width = states.shape
    offer = send_rows.shape[2]
    loop_size = lax.axis_size("loop")
    group_size = lax.axis_size("groups")
    loop_bits = loop_size.bit_length() - 1
    group_bits = group_size.bit_length() - 1

    def after(value, *earlier):
        return lax.optimization_barrier((value, *earlier))[0] if earlier else value

    sources = (premises, send_rows[0], hard_idx[None, :], partner_mask[None, :], counts)
    marked = call(
        mark_kernel,
        "mark",
        shape((rows, width)),
        premises,
        counts,
        ins={0: HBM, 1: SMEM},
        scratch=[pltpu.VMEM((rows, width), BF16), pltpu.SemaphoreType.DMA(())],
        vmem=40 << 20,
    )
    offered, meta = call(
        functools.partial(front_kernel, len(sources)),
        "front",
        (shape((offer, width)), shape((8, rows), jnp.int32)),
        *sources,
        ins={i: HBM for i in range(len(sources))},
        scratch=[pltpu.VMEM(source.shape, source.dtype) for source in sources]
        + [pltpu.SemaphoreType.DMA((len(sources),))],
        vmem=40 << 20,
    )
    keys = across_chips({0: marked}, loop_bits)
    states_sib = swap(after(states, marked), "loop", 1)

    def route(m):
        return lambda block: block if m == 0 else swap(block, "groups", m)

    pool = lax.switch(partner_mask[0], [route(m) for m in range(group_size)], offered)

    qval, back, soft = call(
        hard_kernel,
        "hard",
        (shape((rows, LANES), F32), shape((offer, width)), shape((8, LANES), F32)),
        states,
        premises,
        pool,
        meta,
    )
    even = range(0, loop_size, 2)
    for m in even:
        if m:
            keys[m] = after(keys[m], back)
    states_sib, keys_sib = lax.optimization_barrier(
        (states_sib, swap(marked, "loop", 1))
    )
    stats = call(
        functools.partial(early_kernel, len(even)),
        "early",
        shape((8, 2 * rows), F32),
        states,
        states_sib,
        soft,
        *(keys[m] for m in even),
    )
    stats_sib = swap(stats, "loop", 1)
    lse, message = call(
        near_kernel,
        "near",
        (shape((8, 2 * rows), F32), shape((offer, width + LANES))),
        stats,
        stats_sib,
        back,
    )
    for m in even:
        keys[m] = after(keys[m], stats)
    keys[1] = keys_sib
    keys = from_sibling(keys)
    keys[0] = premises
    grad_states = call(
        functools.partial(states_kernel, loop_size),
        "states",
        shape((rows, width)),
        *keys,
        states,
        lse,
        pool,
        meta,
        qval,
        stats,
        stats_sib,
        cost=1 << 22,
    )
    all_states = across_chips({0: after(states, marked)}, loop_bits)
    for level in range(group_bits):
        last = level == group_bits - 1
        outs = (shape((offer, width)), shape((8, LANES), F32))
        other = swap(message, "groups", 1 << level)
        if level == 1:
            other = after(other, grad_states)
        if level == 2:
            other = after(other, grad)
        message = call(
            functools.partial(merge_kernel, level, last),
            "merge",
            outs if last else shape(message.shape),
            message,
            other,
            meta,
        )
        if level == 0:
            for m in even:
                if m:
                    all_states[m] = after(all_states[m], message)
            all_states[1] = states_sib
            all_states = from_sibling(all_states)
            grad = call(
                functools.partial(premises_kernel, loop_size),
                "premises",
                shape((rows, width), F32),
                *keys,
                *all_states,
                lse,
                meta,
                qval,
                stats,
                stats_sib,
                cost=1 << 22,
            )
    home, part = message
    odd = lax.axis_index("loop") & 1

    def across(block):
        for bit in range(1, loop_bits):
            block = block + swap(block, "loop", 1 << bit)
        return block

    part = lax.cond(odd == 1, across, lambda block: block, part)
    grad_states, grad_premises, loss = call(
        functools.partial(finish_kernel, loop_size * group_size * rows),
        "finish",
        (shape((rows, width)), shape((rows, width)), shape((1, 1), F32)),
        grad_states,
        grad,
        home,
        meta,
        part,
        swap(part, "loop", 1),
    )
    return loss[0, 0], grad_states, grad_premises


def solution(mesh):
    return jax.shard_map(
        body,
        mesh=mesh,
        in_specs=(
            P(("loop", "groups"), None),
            P(("loop", "groups"), None),
            P("loop", "groups"),
            P("loop"),
            P("loop", "groups", None),
            P(("loop", "groups")),
        ),
        out_specs=(P(), P(("loop", "groups"), None), P(("loop", "groups"), None)),
        check_vma=False,
    )
```

time: 118 us -> 32.9 us (0.28)
  blocking collectives: 44.8 us -> 0 us
  waiting for transfers between devices: 32 us -> 8.44 us
  between operations: 17.3 us -> 2.05 us
  matrix products: 5.48 us -> 0 us
  Pallas kernels: 0 us -> 5.2 us
  starting transfers between devices: 10.9 us -> 14.9 us
  local copies, waits for them, and re-layouts: 5.3 us -> 1.62 us
  other arithmetic: 1.46 us -> 0 us
    psum x1 -> x0, blocking collectives: 39.9 us -> none  [body(): lax.psum(jnp.sum(terms), ('loop', 'groups'))]
    ppermute x10 -> x12, waiting for transfers between devices: 31.3 us -> 8.44 us  [swap(): return lax.ppermute(block, axis, [(i, i ^ mask) for i in range(count)])]
    dot_general x8 -> x0, matrix products: 5.48 us -> none  [the longest x1 1.79 us: body(): jnp.einsum('pd,kd->pk', states, keys, preferred_element_type=jnp.float32)]
    pallas_call x0 -> x11, Pallas kernels: none -> 5.2 us  [call(): pl.pallas_call(kernel, out_shape=outs, in_specs=[ins.get(i, VMEM) for i i...]
    unnamed x1 -> x0, blocking collectives: 4.9 us -> none
    ppermute x10 -> x12, starting transfers between devices: 10.9 us -> 14.9 us  [swap(): return lax.ppermute(block, axis, [(i, i ^ mask) for i in range(count)])]
    gather x3 -> x0, local copies, waits for them, and re-layouts: 2.7 us -> none  [the longest x1 1.25 us: body(): pos = jnp.diagonal(own_block)]
    unnamed x15 -> x10, local copies, waits for them, and re-layouts: 2.58 us -> 1.61 us
  transfers between devices with their start and end apart: 11 -> 12, of which waited for: 7 -> 6; matrix products, arithmetic and copies ran while one was open for 5% -> 0% of each run, Pallas kernels for 0% -> 13%
where the time goes in v2:
time: 32.9 us; the launch traced here: 32.3 us
  starting transfers between devices  14.9 us (45%)
  waiting for transfers between devices  8.44 us (26%)
  Pallas kernels  5.2 us (16%)
  between operations  2.05 us (6%)
  local copies, waits for them, and re-layouts  1.62 us (5%)
    ppermute x12, starting transfers between devices, swap(): return lax.ppermute(block, axis, [(i, i ^ mask) for i in range(count)])  14.9 us
    ppermute x12, waiting for transfers between devices, swap(): return lax.ppermute(block, axis, [(i, i ^ mask) for i in range(count)])  8.44 us
    pallas_call x11, Pallas kernels, call(): pl.pallas_call(kernel, out_shape=outs, in_specs=[ins.get(i, VMEM) for i i...  5.2 us
    unnamed x10, local copies, waits for them, and re-layouts  1.61 us
  transfers between devices with their start and end apart: 12, of which 6 were waited for; matrix products, arithmetic and copies ran while one was open for 0% of the time, Pallas kernels for 13%

profile of v2, /device:TPU:0, one launch (start us, length us, event | category | flops | bytes accessed | tf_op | source)
XLA Modules:
  0.0 32.3 jit_solution(10305390384663685429)
XLA Ops:
  1.3 0.0 copy-start
  1.3 0.9 %copy-done = bf16[128,1024]{1,0:T(8,128)(2,1)S(1)} copy-done((bf16[128,1024]{1,0:T(8,128)(2,1)S(1)}, bf16[128,1024]{1,0:T(8,128)(2,1)}, u32[]{:S(2)}) %copy-start) | copy-done | bytes 262168
  2.2 0.0 copy-start.2
  2.2 0.1 mark.1.refs_0_
  2.3 3.0 %collective-permute-start.10 = (bf16[128,1024]{1,0:T(8,128)(2,1)S(1)}, bf16[128,1024]{1,0:T(8,128)(2,1)S(1)}, u32[]{:S(2)}, u32[]{:S(2)}) collective-permute-start(bf16[128,1024]{1,0:T(8,128)(2,1)S(1)} %mark.1.refs_0_), channel_id=1, source_target_pairs={{0,16},{8,24},{16,0},{24,8},{1,17},{9,25},{17,1},{25,9},{2,18},{10... | collective-permute-start | bytes 786440 | tf_op jit(solution)/shard_map/ppermute | solution.py:21
  5.3 0.0 copy-done.2
  5.3 0.0 collective-permute-start.8
  5.3 0.5 %collective-permute-start.9 = (bf16[128,1024]{1,0:T(8,128)(2,1)S(1)}, bf16[128,1024]{1,0:T(8,128)(2,1)S(1)}, u32[]{:S(2)}, u32[]{:S(2)}) collective-permute-start(bf16[128,1024]{1,0:T(8,128)(2,1)S(1)} %mark.1.refs_0_), channel_id=1, source_target_pairs={{0,8},{8,0},{16,24},{24,16},{1,9},{9,1},{17,25},{25,17},{2,10},{10... | collective-permute-start | bytes 786440 | tf_op jit(solution)/shard_map/ppermute | solution.py:21
  5.8 0.8 %collective-permute-start.13 = (bf16[128,1024]{1,0:T(8,128)(2,1)S(1)}, bf16[128,1024]{1,0:T(8,128)(2,1)S(1)}, u32[]{:S(2)}, u32[]{:S(2)}) collective-permute-start(bf16[128,1024]{1,0:T(8,128)(2,1)S(1)} %copy-done.2), channel_id=1, source_target_pairs={{0,16},{8,24},{16,0},{24,8},{1,17},{9,25},{17,1},{25,9},{2,18},{10... | collective-permute-start | bytes 786440 | tf_op jit(solution)/shard_map/ppermute | solution.py:21
  7.3 0.0 copy-start.3
  7.3 0.0 copy-start.4
  7.3 0.6 %copy-done.3 = s32[1,1,16]{2,1,0:T(1,128)S(1)} copy-done((s32[1,1,16]{2,1,0:T(1,128)S(1)}, s32[1,1,16]{2,1,0:T(1,128)}, u32[]{:S(2)}) %copy-start.3) | copy-done | bytes 88
  7.9 0.0 copy-done.4
  8.0 0.3 front.1
  8.2 0.0 copy-start.1
  8.2 4.9 %conditional.2 = (bf16[16,1024]{1,0:T(8,128)(2,1)S(1)}) conditional(s32[]{:T(128)} %bitcast, bf16[16,1024]{1,0:T(8,128)(2,1)S(1)} %get-tuple-element.47, bf16[16,1024]{1,0:T(8,128)(2,1)S(1)} %get-tuple-element.47, bf16[16,1024]{1,0:T(8,128)(2,1)S(1)} %get-tuple-element.47, ...), branch_computations={%region_0.0_spmd, %region_1.0_spmd, %region_2.0_spmd, %region_3.0_... | conditional | bytes 196656 | solution.py:329
  8.3 2.7 %collective-permute-start.3 = (bf16[16,1024]{1,0:T(8,128)(2,1)S(1)}, bf16[16,1024]{1,0:T(8,128)(2,1)S(1)}, u32[]{:S(2)}, u32[]{:S(2)}) collective-permute-start(bf16[16,1024]{1,0:T(8,128)(2,1)S(1)} %param.4), channel_id=1, source_target_pairs={{0,4},{1,5},{2,6},{3,7},{4,0},{5,1},{6,2},{7,3},{8,12},{9,13},{10,... | collective-permute-start | bytes 98312 | tf_op jit(solution)/shard_map/cond/branch_4_fun/ppermute | solution.py:21
  10.9 2.2 %collective-permute-done.3 = bf16[16,1024]{1,0:T(8,128)(2,1)S(1)} collective-permute-done((bf16[16,1024]{1,0:T(8,128)(2,1)S(1)}, bf16[16,1024]{1,0:T(8,128)(2,1)S(1)}, u32[]{:S(2)}, u32[]{:S(2)}) %collective-permute-start.3) | collective-permute-done | bytes 32800 | tf_op jit(solution)/shard_map/cond/branch_4_fun/ppermute | solution.py:21
  13.2 0.0 copy-done.1
  13.2 0.6 %hard.1 = (f32[128,128]{1,0:T(8,128)S(1)}, bf16[16,1024]{1,0:T(8,128)(2,1)S(1)}, f32[8,128]{1,0:T(8,128)S(1)}) custom-call(bf16[128,1024]{1,0:T(8,128)(2,1)S(1)} %copy-done.2, bf16[128,1024]{1,0:T(8,128)(2,1)S(1)} %copy-done.1, bf16[16,1024]{1,0:T(8,128)(2,1)S(1)} %get-tuple-element.65.pool.refs_6_, s32[8,128]{1,0:T(8,128)S(1)} %get-tuple-element.48.meta.refs_7_.refs_9_), custom_call_target="tpu_custom_call" | custom-call | tf_op jit(solution)/shard_map/hard/pallas_call | solution.py:30
  13.8 0.0 collective-permute-done.10.refs_1_.refs_2_
  13.8 0.0 collective-permute-done.8.sib.refs_5_
  13.8 0.0 collective-permute-done.9.refs_1_
  13.8 0.5 %early.1.stats.refs_9_.refs_11_ = f32[8,256]{1,0:T(8,128)S(1)} custom-call(bf16[128,1024]{1,0:T(8,128)(2,1)S(1)} %copy-done.2, bf16[128,1024]{1,0:T(8,128)(2,1)S(1)} %collective-permute-done.8.sib.refs_5_, f32[8,128]{1,0:T(8,128)S(1)} %get-tuple-element.52.soft, bf16[128,1024]{1,0:T(8,128)(2,1)S(1)} %mark.1.refs_0_, ...), custom_call_target="tpu_custom_call" | custom-call | tf_op jit(solution)/shard_map/early/pallas_call | solution.py:30
  14.4 0.1 collective-permute-start.12
  14.4 0.5 %collective-permute-start.11 = (bf16[128,1024]{1,0:T(8,128)(2,1)S(1)}, bf16[128,1024]{1,0:T(8,128)(2,1)S(1)}, u32[]{:S(2)}, u32[]{:S(2)}) collective-permute-start(bf16[128,1024]{1,0:T(8,128)(2,1)S(1)} %collective-permute-done.10.refs_1_.refs_2_), channel_id=1, source_target_pairs={{0,8},{8,0},{16,24},{24,16},{1,9},{9,1},{17,25},{25,17},{2,10},{10... | collective-permute-start | bytes 786440 | tf_op jit(solution)/shard_map/ppermute | solution.py:21
  14.9 0.7 %collective-permute-done.12.stats_sib.refs_10_.refs_12_ = f32[8,256]{1,0:T(8,128)S(1)} collective-permute-done((f32[8,256]{1,0:T(8,128)S(1)}, f32[8,256]{1,0:T(8,128)S(1)}, u32[]{:S(2)}, u32[]{:S(2)}) %collective-permute-start.12) | collective-permute-done | bytes 8224 | tf_op jit(solution)/shard_map/ppermute | solution.py:21
  15.6 0.2 near.1
  15.8 1.6 %collective-permute-start.14 = (bf16[16,1152]{1,0:T(8,128)(2,1)S(1)}, bf16[16,1152]{1,0:T(8,128)(2,1)S(1)}, u32[]{:S(2)}, u32[]{:S(2)}) collective-permute-start(bf16[16,1152]{1,0:T(8,128)(2,1)S(1)} %get-tuple-element.56.mine), channel_id=1, source_target_pairs={{0,1},{1,0},{2,3},{3,2},{4,5},{5,4},{6,7},{7,6},{8,9},{9,8},{10,11... | collective-permute-start | bytes 110600 | tf_op jit(solution)/shard_map/ppermute | solution.py:21
  17.4 2.4 %collective-permute-done.14.other = bf16[16,1152]{1,0:T(8,128)(2,1)S(1)} collective-permute-done((bf16[16,1152]{1,0:T(8,128)(2,1)S(1)}, bf16[16,1152]{1,0:T(8,128)(2,1)S(1)}, u32[]{:S(2)}, u32[]{:S(2)}) %collective-permute-start.14) | collective-permute-done | bytes 36896 | tf_op jit(solution)/shard_map/ppermute | solution.py:21
  19.8 0.1 merge.3.mine
  19.9 0.0 collective-permute-done.13.refs_6_
  19.9 0.1 collective-permute-start.15
  20.0 1.6 %collective-permute-start.16 = (bf16[16,1152]{1,0:T(8,128)(2,1)S(1)}, bf16[16,1152]{1,0:T(8,128)(2,1)S(1)}, u32[]{:S(2)}, u32[]{:S(2)}) collective-permute-start(bf16[16,1152]{1,0:T(8,128)(2,1)S(1)} %merge.3.mine), channel_id=1, source_target_pairs={{0,2},{1,3},{2,0},{3,1},{4,6},{5,7},{6,4},{7,5},{8,10},{9,11},{10,... | collective-permute-start | bytes 110600 | tf_op jit(solution)/shard_map/ppermute | solution.py:21
  21.6 0.0 collective-permute-done.11.refs_3_
  21.6 0.8 %states.3.grad_states = bf16[128,1024]{1,0:T(8,128)(2,1)S(1)} custom-call(bf16[128,1024]{1,0:T(8,128)(2,1)S(1)} %copy-done.1, bf16[128,1024]{1,0:T(8,128)(2,1)S(1)} %collective-permute-done.9.refs_1_, bf16[128,1024]{1,0:T(8,128)(2,1)S(1)} %collective-permute-done.10.refs_1_.refs_2_, bf16[128,1024]{1,0:T(8,128)(2,1)S(1)} %collective-permute-done.11.refs_3_, ...), custom_call_target="tpu_custom_call" | custom-call | bytes 4194304 | tf_op jit(solution)/shard_map/states/pallas_call | solution.py:30
  22.4 1.6 %collective-permute-done.16.other = bf16[16,1152]{1,0:T(8,128)(2,1)S(1)} collective-permute-done((bf16[16,1152]{1,0:T(8,128)(2,1)S(1)}, bf16[16,1152]{1,0:T(8,128)(2,1)S(1)}, u32[]{:S(2)}, u32[]{:S(2)}) %collective-permute-start.16) | collective-permute-done | bytes 36896 | tf_op jit(solution)/shard_map/ppermute | solution.py:21
  24.0 0.1 merge.4.mine
  24.1 2.6 %collective-permute-start.17 = (bf16[16,1152]{1,0:T(8,128)(2,1)S(1)}, bf16[16,1152]{1,0:T(8,128)(2,1)S(1)}, u32[]{:S(2)}, u32[]{:S(2)}) collective-permute-start(bf16[16,1152]{1,0:T(8,128)(2,1)S(1)} %merge.4.mine), channel_id=1, source_target_pairs={{0,4},{1,5},{2,6},{3,7},{4,0},{5,1},{6,2},{7,3},{8,12},{9,13},{10,... | collective-permute-start | bytes 110600 | tf_op jit(solution)/shard_map/ppermute | solution.py:21
  26.8 0.0 collective-permute-done.15.refs_7_
  26.8 1.6 %premises.5.grad = f32[128,1024]{1,0:T(8,128)S(1)} custom-call(bf16[128,1024]{1,0:T(8,128)(2,1)S(1)} %copy-done.1, bf16[128,1024]{1,0:T(8,128)(2,1)S(1)} %collective-permute-done.9.refs_1_, bf16[128,1024]{1,0:T(8,128)(2,1)S(1)} %collective-permute-done.10.refs_1_.refs_2_, bf16[128,1024]{1,0:T(8,128)(2,1)S(1)} %collective-permute-done.11.refs_3_, ...), custom_call_target="tpu_custom_call" | custom-call | bytes 4194304 | tf_op jit(solution)/shard_map/premises/pallas_call | solution.py:30
  28.4 0.6 %collective-permute-done.17.other = bf16[16,1152]{1,0:T(8,128)(2,1)S(1)} collective-permute-done((bf16[16,1152]{1,0:T(8,128)(2,1)S(1)}, bf16[16,1152]{1,0:T(8,128)(2,1)S(1)}, u32[]{:S(2)}, u32[]{:S(2)}) %collective-permute-start.17) | collective-permute-done | bytes 36896 | tf_op jit(solution)/shard_map/ppermute | solution.py:21
  29.0 0.1 merge.5
  29.1 1.5 %collective-permute-start.18 = (f32[8,128]{1,0:T(8,128)S(1)}, f32[8,128]{1,0:T(8,128)S(1)}, u32[]{:S(2)}, u32[]{:S(2)}) collective-permute-start(f32[8,128]{1,0:T(8,128)S(1)} %get-tuple-element.66.part), channel_id=1, source_target_pairs={{0,8},{8,0},{16,24},{24,16},{1,9},{9,1},{17,25},{25,17},{2,10},{10... | collective-permute-start | bytes 12296 | tf_op jit(solution)/shard_map/ppermute | solution.py:21
  30.5 0.8 %collective-permute-done.18.other = f32[8,128]{1,0:T(8,128)S(1)} collective-permute-done((f32[8,128]{1,0:T(8,128)S(1)}, f32[8,128]{1,0:T(8,128)S(1)}, u32[]{:S(2)}, u32[]{:S(2)}) %collective-permute-start.18) | collective-permute-done | bytes 4128 | tf_op jit(solution)/shard_map/ppermute | solution.py:21
  31.4 0.9 %finish.1 = (bf16[128,1024]{1,0:T(8,128)(2,1)}, bf16[128,1024]{1,0:T(8,128)(2,1)}, f32[1,1]{1,0:T(1,128)}) custom-call(bf16[128,1024]{1,0:T(8,128)(2,1)S(1)} %states.3.grad_states, f32[128,1024]{1,0:T(8,128)S(1)} %premises.5.grad, bf16[16,1024]{1,0:T(8,128)(2,1)S(1)} %get-tuple-element.60.home, s32[8,128]{1,0:T(8,128)S(1)} %get-tuple-element.48.meta.refs_7_.refs_9_, ...), custom_call_target="tpu_custom_call" | custom-call | tf_op jit(solution)/shard_map/finish/pallas_call | solution.py:30
  (2 shorter events, 0.0 us)
Async XLA Ops:
  1.3 1.0 %copy-start = (bf16[128,1024]{1,0:T(8,128)(2,1)S(1)}, bf16[128,1024]{1,0:T(8,128)(2,1)}, u32[]{:S(2)}) copy-start(bf16[128,1024]{1,0:T(8,128)(2,1)} %refs_0_.5) | copy-start | bytes 786436
  2.2 3.1 %copy-start.2 = (bf16[128,1024]{1,0:T(8,128)(2,1)S(1)}, bf16[128,1024]{1,0:T(8,128)(2,1)}, u32[]{:S(2)}) copy-start(bf16[128,1024]{1,0:T(8,128)(2,1)} %refs_4_.3) | copy-start | bytes 786436
  2.3 11.5 %collective-permute-start.10 = (bf16[128,1024]{1,0:T(8,128)(2,1)S(1)}, bf16[128,1024]{1,0:T(8,128)(2,1)S(1)}, u32[]{:S(2)}, u32[]{:S(2)}) collective-permute-start(bf16[128,1024]{1,0:T(8,128)(2,1)S(1)} %mark.1.refs_0_), channel_id=1, source_target_pairs={{0,16},{8,24},{16,0},{24,8},{1,17},{9,25},{17,1},{25,9},{2,18},{10... | collective-permute-start | bytes 786440 | tf_op jit(solution)/shard_map/ppermute | solution.py:21
  5.3 8.5 %collective-permute-start.8 = (bf16[128,1024]{1,0:T(8,128)(2,1)S(1)}, bf16[128,1024]{1,0:T(8,128)(2,1)S(1)}, u32[]{:S(2)}, u32[]{:S(2)}) collective-permute-start(bf16[128,1024]{1,0:T(8,128)(2,1)S(1)} %copy-done.2), channel_id=1, source_target_pairs={{0,8},{8,0},{16,24},{24,16},{1,9},{9,1},{17,25},{25,17},{2,10},{10... | collective-permute-start | bytes 786440 | tf_op jit(solution)/shard_map/ppermute | solution.py:21
  5.3 8.5 %collective-permute-start.9 = (bf16[128,1024]{1,0:T(8,128)(2,1)S(1)}, bf16[128,1024]{1,0:T(8,128)(2,1)S(1)}, u32[]{:S(2)}, u32[]{:S(2)}) collective-permute-start(bf16[128,1024]{1,0:T(8,128)(2,1)S(1)} %mark.1.refs_0_), channel_id=1, source_target_pairs={{0,8},{8,0},{16,24},{24,16},{1,9},{9,1},{17,25},{25,17},{2,10},{10... | collective-permute-start | bytes 786440 | tf_op jit(solution)/shard_map/ppermute | solution.py:21
  5.8 14.1 %collective-permute-start.13 = (bf16[128,1024]{1,0:T(8,128)(2,1)S(1)}, bf16[128,1024]{1,0:T(8,128)(2,1)S(1)}, u32[]{:S(2)}, u32[]{:S(2)}) collective-permute-start(bf16[128,1024]{1,0:T(8,128)(2,1)S(1)} %copy-done.2), channel_id=1, source_target_pairs={{0,16},{8,24},{16,0},{24,8},{1,17},{9,25},{17,1},{25,9},{2,18},{10... | collective-permute-start | bytes 786440 | tf_op jit(solution)/shard_map/ppermute | solution.py:21
  7.3 0.7 %copy-start.3 = (s32[1,1,16]{2,1,0:T(1,128)S(1)}, s32[1,1,16]{2,1,0:T(1,128)}, u32[]{:S(2)}) copy-start(s32[1,1,16]{2,1,0:T(1,128)} %param.20) | copy-start | bytes 196
  7.3 0.7 %copy-start.4 = (s32[128]{0:T(128)S(1)}, s32[128]{0:T(128)}, u32[]{:S(2)}) copy-start(s32[128]{0:T(128)} %param.21) | copy-start | bytes 1540
  8.2 4.9 %copy-start.1 = (bf16[128,1024]{1,0:T(8,128)(2,1)S(1)}, bf16[128,1024]{1,0:T(8,128)(2,1)}, u32[]{:S(2)}) copy-start(bf16[128,1024]{1,0:T(8,128)(2,1)} %refs_0_.5) | copy-start | bytes 786436
  8.3 4.9 %collective-permute-start.3 = (bf16[16,1024]{1,0:T(8,128)(2,1)S(1)}, bf16[16,1024]{1,0:T(8,128)(2,1)S(1)}, u32[]{:S(2)}, u32[]{:S(2)}) collective-permute-start(bf16[16,1024]{1,0:T(8,128)(2,1)S(1)} %param.4), channel_id=1, source_target_pairs={{0,4},{1,5},{2,6},{3,7},{4,0},{5,1},{6,2},{7,3},{8,12},{9,13},{10,... | collective-permute-start | bytes 98312 | tf_op jit(solution)/shard_map/cond/branch_4_fun/ppermute | solution.py:21
  14.4 1.2 %collective-permute-start.12 = (f32[8,256]{1,0:T(8,128)S(1)}, f32[8,256]{1,0:T(8,128)S(1)}, u32[]{:S(2)}, u32[]{:S(2)}) collective-permute-start(f32[8,256]{1,0:T(8,128)S(1)} %early.1.stats.refs_9_.refs_11_), channel_id=1, source_target_pairs={{0,8},{8,0},{16,24},{24,16},{1,9},{9,1},{17,25},{25,17},{2,10},{10... | collective-permute-start | bytes 24584 | tf_op jit(solution)/shard_map/ppermute | solution.py:21
  14.4 7.2 %collective-permute-start.11 = (bf16[128,1024]{1,0:T(8,128)(2,1)S(1)}, bf16[128,1024]{1,0:T(8,128)(2,1)S(1)}, u32[]{:S(2)}, u32[]{:S(2)}) collective-permute-start(bf16[128,1024]{1,0:T(8,128)(2,1)S(1)} %collective-permute-done.10.refs_1_.refs_2_), channel_id=1, source_target_pairs={{0,8},{8,0},{16,24},{24,16},{1,9},{9,1},{17,25},{25,17},{2,10},{10... | collective-permute-start | bytes 786440 | tf_op jit(solution)/shard_map/ppermute | solution.py:21
  15.8 4.0 %collective-permute-start.14 = (bf16[16,1152]{1,0:T(8,128)(2,1)S(1)}, bf16[16,1152]{1,0:T(8,128)(2,1)S(1)}, u32[]{:S(2)}, u32[]{:S(2)}) collective-permute-start(bf16[16,1152]{1,0:T(8,128)(2,1)S(1)} %get-tuple-element.56.mine), channel_id=1, source_target_pairs={{0,1},{1,0},{2,3},{3,2},{4,5},{5,4},{6,7},{7,6},{8,9},{9,8},{10,11... | collective-permute-start | bytes 110600 | tf_op jit(solution)/shard_map/ppermute | solution.py:21
  19.9 6.8 %collective-permute-start.15 = (bf16[128,1024]{1,0:T(8,128)(2,1)S(1)}, bf16[128,1024]{1,0:T(8,128)(2,1)S(1)}, u32[]{:S(2)}, u32[]{:S(2)}) collective-permute-start(bf16[128,1024]{1,0:T(8,128)(2,1)S(1)} %collective-permute-done.13.refs_6_), channel_id=1, source_target_pairs={{0,8},{8,0},{16,24},{24,16},{1,9},{9,1},{17,25},{25,17},{2,10},{10... | collective-permute-start | bytes 786440 | tf_op jit(solution)/shard_map/ppermute | solution.py:21
  20.0 4.0 %collective-permute-start.16 = (bf16[16,1152]{1,0:T(8,128)(2,1)S(1)}, bf16[16,1152]{1,0:T(8,128)(2,1)S(1)}, u32[]{:S(2)}, u32[]{:S(2)}) collective-permute-start(bf16[16,1152]{1,0:T(8,128)(2,1)S(1)} %merge.3.mine), channel_id=1, source_target_pairs={{0,2},{1,3},{2,0},{3,1},{4,6},{5,7},{6,4},{7,5},{8,10},{9,11},{10,... | collective-permute-start | bytes 110600 | tf_op jit(solution)/shard_map/ppermute | solution.py:21
  24.1 4.9 %collective-permute-start.17 = (bf16[16,1152]{1,0:T(8,128)(2,1)S(1)}, bf16[16,1152]{1,0:T(8,128)(2,1)S(1)}, u32[]{:S(2)}, u32[]{:S(2)}) collective-permute-start(bf16[16,1152]{1,0:T(8,128)(2,1)S(1)} %merge.4.mine), channel_id=1, source_target_pairs={{0,4},{1,5},{2,6},{3,7},{4,0},{5,1},{6,2},{7,3},{8,12},{9,13},{10,... | collective-permute-start | bytes 110600 | tf_op jit(solution)/shard_map/ppermute | solution.py:21
  29.1 2.3 %collective-permute-start.18 = (f32[8,128]{1,0:T(8,128)S(1)}, f32[8,128]{1,0:T(8,128)S(1)}, u32[]{:S(2)}, u32[]{:S(2)}) collective-permute-start(f32[8,128]{1,0:T(8,128)S(1)} %get-tuple-element.66.part), channel_id=1, source_target_pairs={{0,8},{8,0},{16,24},{24,16},{1,9},{9,1},{17,25},{25,17},{2,10},{10... | collective-permute-start | bytes 12296 | tf_op jit(solution)/shard_map/ppermute | solution.py:21

commit v3 on v2

--- a/solution.py
+++ b/solution.py
@@ -34,7 +34,7 @@
         out_specs=out_specs or jax.tree.map(lambda _: VMEM, outs),
         scratch_shapes=scratch,
         compiler_params=pltpu.CompilerParams(vmem_limit_bytes=vmem),
-        cost_estimate=pl.CostEstimate(flops=0, bytes_accessed=cost, transcendentals=0),
+        cost_estimate=pl.CostEstimate(flops=cost, bytes_accessed=0, transcendentals=0),
         name=name,
     )(*args)
 
@@ -125,7 +125,7 @@
     offered[...] = dot(place, premises[...], ((0,), (0,))).astype(BF16)
 
 
-def hard_kernel(states, premises, pool, meta, qval, back, soft):
+def hard_kernel(states, premises, pool, meta, qval, soft):
     rows, offer = states.shape[0], pool.shape[0]
     pick = pick_of(offer, meta[0:1, :])
     hard = dot(pick.astype(BF16), pool[...], ((0,), (0,)))
@@ -138,7 +138,11 @@
     plus = jnp.maximum(gap, 0.0) + jnp.log(1.0 + jnp.exp(-jnp.abs(gap)))
     qval[...] = jnp.broadcast_to(q, qval.shape)
     soft[...] = jnp.broadcast_to(total(jnp.where(valid, plus - pos, 0.0)), soft.shape)
-    weight = jnp.broadcast_to(q, (rows, rows)).T[:offer] * pick
+
+
+def back_kernel(states, qval, meta, back):
+    offer = back.shape[0]
+    weight = qval[...].T[:offer] * pick_of(offer, meta[0:1, :])
     split = jnp.concatenate(parts(weight), axis=0)
     summed = dot(split, states[...], ((1,), (0,)))
     summed = summed[:offer] + summed[offer : 2 * offer] + summed[2 * offer :]
@@ -244,36 +248,36 @@
 
 
 def premises_kernel(size, *refs):
-    keys, states = refs[:size], refs[size : 2 * size]
-    lse, meta, qval, stats, stats_sib, out = refs[2 * size :]
-    rows = states[0].shape[0]
-    grad = None
-    for b in range(0, size, 2):
-        both = jnp.concatenate([states[b][...], states[b + 1][...]], axis=0)
-        mine = score(keys[0][...], both, count_of(meta))
-        if b == 0:
-            total_lse = lse[0:1, :]
-        else:
-            blocks = [mine] + [
-                score(keys[m][...], both, limit_of(stats, stats_sib, m))
-                for m in range(1, size)
-            ]
-            top = tops(blocks)
-            total_lse = top + jnp.log(masses(blocks, top))
-        row_ok = valid_lanes(stats, stats_sib, b, rows)
-        prob = jnp.where(row_ok, jnp.exp(mine - total_lse), 0.0).astype(BF16)
-        piece = dot(prob, both, ((1,), (0,)))
-        grad = piece if grad is None else grad + piece
-    vq = jnp.where(column(rows) < count_of(meta), 1.0, 0.0) + qval[:, 0:1]
-    out[...] = grad - SCALE * vq * states[0][...].astype(F32)
-
-
-def finish_kernel(count, grad_states, grad, home, meta, part, other, out_states, out, loss):
+    keys = refs[:size]
+    own, sib, lse, qval, stats, stats_sib, near = refs[size : size + 7]
+    far = refs[size + 7 :]
+    rows = own.shape[0]
+    both = jnp.concatenate([own[...], sib[...]], axis=0)
+    row_ok = valid_lanes(stats, stats_sib, 0, rows)
+    held = jnp.concatenate([key[...] for key in keys], axis=0)
+    scores = SCALE * dot(held, both, ((1,), (1,)))
+    ok = jnp.logical_and(is_valid(held), row_ok)
+    prob = jnp.where(ok, jnp.exp(scores - lse[0:1, :]), 0.0).astype(BF16)
+    grad = dot(prob, both, ((1,), (0,)))
+    vq = jnp.where(is_valid(keys[0]), 1.0, 0.0) + qval[:, 0:1]
+    near[...] = grad[:rows] - SCALE * vq * own[...].astype(F32)
+    for i, out in enumerate(far):
+        out[...] = grad[(i + 1) * rows : (i + 2) * rows].astype(BF16)
+
+
+def finish_kernel(size, grad_states, grad, home, meta, *refs):
+    far, (out_states, out) = refs[:size], refs[size:]
     place = place_of(grad.shape[0], meta[1:2, 0 : home.shape[0]])
-    out[...] = (grad[...] + dot(place, home[...], ((1,), (0,)))).astype(BF16)
+    summed = grad[...] + dot(place, home[...], ((1,), (0,)))
+    for block in far:
+        summed = summed + block[...].astype(F32)
+    out[...] = summed.astype(BF16)
     out_states[...] = grad_states[...]
+
+
+def loss_kernel(count, part, other, out):
     odd = jnp.full((1, 1), lax.axis_index("loop") & 1, jnp.int32) == 1
-    loss[...] = jnp.where(odd, part[0:1, 0:1], other[0:1, 0:1]) / count
+    out[...] = jnp.where(odd, part[0:1, 0:1], other[0:1, 0:1]) / count
 
 
 def across_chips(held, bits):
@@ -321,17 +325,17 @@
         vmem=40 << 20,
     )
     keys = across_chips({0: marked}, loop_bits)
-    states_sib = swap(after(states, marked), "loop", 1)
+    states_sib = swap(states, "loop", 1)
 
     def route(m):
         return lambda block: block if m == 0 else swap(block, "groups", m)
 
     pool = lax.switch(partner_mask[0], [route(m) for m in range(group_size)], offered)
 
-    qval, back, soft = call(
+    qval, soft = call(
         hard_kernel,
         "hard",
-        (shape((rows, LANES), F32), shape((offer, width)), shape((8, LANES), F32)),
+        (shape((rows, rows), F32), shape((8, LANES), F32)),
         states,
         premises,
         pool,
@@ -340,10 +344,7 @@
     even = range(0, loop_size, 2)
     for m in even:
         if m:
-            keys[m] = after(keys[m], back)
-    states_sib, keys_sib = lax.optimization_barrier(
-        (states_sib, swap(marked, "loop", 1))
-    )
+            keys[m] = after(keys[m], soft)
     stats = call(
         functools.partial(early_kernel, len(even)),
         "early",
@@ -354,6 +355,10 @@
         *(keys[m] for m in even),
     )
     stats_sib = swap(stats, "loop", 1)
+    back = call(
+        back_kernel, "back", shape((offer, width)), after(states, stats), qval, meta
+    )
+    stats_sib = after(stats_sib, back)
     lse, message = call(
         near_kernel,
         "near",
@@ -363,15 +368,14 @@
         back,
     )
     for m in even:
-        keys[m] = after(keys[m], stats)
-    keys[1] = keys_sib
+        keys[m] = after(keys[m], message)
     keys = from_sibling(keys)
-    keys[0] = premises
     grad_states = call(
         functools.partial(states_kernel, loop_size),
         "states",
         shape((rows, width)),
-        *keys,
+        premises,
+        *keys[1:],
         states,
         lse,
         pool,
@@ -379,17 +383,34 @@
         qval,
         stats,
         stats_sib,
-        cost=1 << 22,
-    )
-    all_states = across_chips({0: after(states, marked)}, loop_bits)
+        cost=int(1.7e10),
+    )
     for level in range(group_bits):
         last = level == group_bits - 1
         outs = (shape((offer, width)), shape((8, LANES), F32))
+        if level == 1:
+            grad, *far = call(
+                functools.partial(premises_kernel, len(even)),
+                "premises",
+                (shape((rows, width), F32),) + (shape((rows, width)),) * (len(even) - 1),
+                *(keys[m] for m in even),
+                states,
+                states_sib,
+                after(lse, message),
+                qval,
+                stats,
+                stats_sib,
+                cost=int(1.7e10),
+            )
         other = swap(message, "groups", 1 << level)
+        if level == 2:
+            other = after(other, grad_states)
         if level == 1:
-            other = after(other, grad_states)
-        if level == 2:
-            other = after(other, grad)
+            other = after(other, grad, *far)
+            far = [
+                swap(block, "loop", m)
+                for m, block in zip(even[1:], far)
+            ]
         message = call(
             functools.partial(merge_kernel, level, last),
             "merge",
@@ -398,25 +419,6 @@
             other,
             meta,
         )
-        if level == 0:
-            for m in even:
-                if m:
-                    all_states[m] = after(all_states[m], message)
-            all_states[1] = states_sib
-            all_states = from_sibling(all_states)
-            grad = call(
-                functools.partial(premises_kernel, loop_size),
-                "premises",
-                shape((rows, width), F32),
-                *keys,
-                *all_states,
-                lse,
-                meta,
-                qval,
-                stats,
-                stats_sib,
-                cost=1 << 22,
-            )
     home, part = message
     odd = lax.axis_index("loop") & 1
 
@@ -426,16 +428,23 @@
         return block
 
     part = lax.cond(odd == 1, across, lambda block: block, part)
-    grad_states, grad_premises, loss = call(
-        functools.partial(finish_kernel, loop_size * group_size * rows),
+    grad_states, grad_premises = call(
+        functools.partial(finish_kernel, len(far)),
         "finish",
-        (shape((rows, width)), shape((rows, width)), shape((1, 1), F32)),
+        (shape((rows, width)), shape((rows, width))),
         grad_states,
         grad,
         home,
         meta,
+        *far,
+    )
+    other = after(swap(part, "loop", 1), grad_premises)
+    loss = call(
+        functools.partial(loss_kernel, loop_size * group_size * rows),
+        "loss",
+        shape((1, 1), F32),
         part,
-        swap(part, "loop", 1),
+        other,
     )
     return loss[0, 0], grad_states, grad_premises
 

time: 32.9 us -> 29.5 us (0.90); the launches traced: 32.3 us -> 29.3 us
  starting transfers between devices: 14.9 us -> 13.3 us
  waiting for transfers between devices: 8.44 us -> 7.39 us
    ppermute x12 -> x11, starting transfers between devices: 14.9 us -> 13.3 us  [swap(): return lax.ppermute(block, axis, [(i, i ^ mask) for i in range(count)])]
    ppermute x12 -> x11, waiting for transfers between devices: 8.44 us -> 7.39 us  [swap(): return lax.ppermute(block, axis, [(i, i ^ mask) for i in range(count)])]
    pallas_call x11 -> x13, Pallas kernels: 5.2 us -> 4.96 us  [call(): pl.pallas_call(kernel, out_shape=outs, in_specs=[ins.get(i, VMEM) for i i...]
  transfers between devices with their start and end apart: 12 -> 11, of which waited for: 6 -> 6; matrix products, arithmetic and copies ran while one was open for 0% -> 0% of each run, Pallas kernels for 13% -> 12%
where the time goes in v3:
time: 29.5 us; the launch traced here: 29.3 us
  starting transfers between devices  13.3 us (45%)
  waiting for transfers between devices  7.39 us (25%)
  Pallas kernels  4.96 us (17%)
  between operations  2.03 us (7%)
  local copies, waits for them, and re-layouts  1.62 us (5%)
    ppermute x11, starting transfers between devices, swap(): return lax.ppermute(block, axis, [(i, i ^ mask) for i in range(count)])  13.3 us
    ppermute x11, waiting for transfers between devices, swap(): return lax.ppermute(block, axis, [(i, i ^ mask) for i in range(count)])  7.39 us
    pallas_call x13, Pallas kernels, call(): pl.pallas_call(kernel, out_shape=outs, in_specs=[ins.get(i, VMEM) for i i...  4.96 us
    unnamed x10, local copies, waits for them, and re-layouts  1.61 us
  transfers between devices with their start and end apart: 11, of which 6 were waited for; matrix products, arithmetic and copies ran while one was open for 0% of the time, Pallas kernels for 12%

profile of v3, /device:TPU:0, one launch (start us, length us, event | category | flops | bytes accessed | tf_op | source)
XLA Modules:
  0.0 29.3 jit_solution(8197263955191564080)
XLA Ops:
  1.3 0.0 copy-start
  1.3 0.9 %copy-done = bf16[128,1024]{1,0:T(8,128)(2,1)S(1)} copy-done((bf16[128,1024]{1,0:T(8,128)(2,1)S(1)}, bf16[128,1024]{1,0:T(8,128)(2,1)}, u32[]{:S(2)}) %copy-start) | copy-done | bytes 262168
  2.2 0.0 copy-start.2
  2.2 0.1 mark.1.refs_0_
  2.3 3.0 %collective-permute-start.9 = (bf16[128,1024]{1,0:T(8,128)(2,1)S(1)}, bf16[128,1024]{1,0:T(8,128)(2,1)S(1)}, u32[]{:S(2)}, u32[]{:S(2)}) collective-permute-start(bf16[128,1024]{1,0:T(8,128)(2,1)S(1)} %mark.1.refs_0_), channel_id=1, source_target_pairs={{0,16},{8,24},{16,0},{24,8},{1,17},{9,25},{17,1},{25,9},{2,18},{10... | collective-permute-start | bytes 786440 | tf_op jit(solution)/shard_map/ppermute | solution.py:21
  5.3 0.0 copy-done.2
  5.3 0.0 collective-permute-start.8
  6.0 0.0 copy-start.3
  6.0 0.0 copy-start.4
  6.0 0.6 %copy-done.3 = s32[1,1,16]{2,1,0:T(1,128)S(1)} copy-done((s32[1,1,16]{2,1,0:T(1,128)S(1)}, s32[1,1,16]{2,1,0:T(1,128)}, u32[]{:S(2)}) %copy-start.3) | copy-done | bytes 88
  6.6 0.0 copy-done.4
  6.6 0.3 front.1
  6.9 0.0 copy-start.1
  6.9 4.9 %conditional.2 = (bf16[16,1024]{1,0:T(8,128)(2,1)S(1)}) conditional(s32[]{:T(128)} %bitcast, bf16[16,1024]{1,0:T(8,128)(2,1)S(1)} %get-tuple-element.46, bf16[16,1024]{1,0:T(8,128)(2,1)S(1)} %get-tuple-element.46, bf16[16,1024]{1,0:T(8,128)(2,1)S(1)} %get-tuple-element.46, ...), branch_computations={%region_0.0_spmd, %region_1.0_spmd, %region_2.0_spmd, %region_3.0_... | conditional | bytes 196656 | solution.py:333
  7.0 2.7 %collective-permute-start.3 = (bf16[16,1024]{1,0:T(8,128)(2,1)S(1)}, bf16[16,1024]{1,0:T(8,128)(2,1)S(1)}, u32[]{:S(2)}, u32[]{:S(2)}) collective-permute-start(bf16[16,1024]{1,0:T(8,128)(2,1)S(1)} %param.4), channel_id=1, source_target_pairs={{0,4},{1,5},{2,6},{3,7},{4,0},{5,1},{6,2},{7,3},{8,12},{9,13},{10,... | collective-permute-start | bytes 98312 | tf_op jit(solution)/shard_map/cond/branch_4_fun/ppermute | solution.py:21
  9.6 2.2 %collective-permute-done.3 = bf16[16,1024]{1,0:T(8,128)(2,1)S(1)} collective-permute-done((bf16[16,1024]{1,0:T(8,128)(2,1)S(1)}, bf16[16,1024]{1,0:T(8,128)(2,1)S(1)}, u32[]{:S(2)}, u32[]{:S(2)}) %collective-permute-start.3) | collective-permute-done | bytes 32800 | tf_op jit(solution)/shard_map/cond/branch_4_fun/ppermute | solution.py:21
  11.8 0.0 copy-done.1
  11.8 0.4 %hard.1 = (f32[128,128]{1,0:T(8,128)S(1)}, f32[8,128]{1,0:T(8,128)S(1)}) custom-call(bf16[128,1024]{1,0:T(8,128)(2,1)S(1)} %copy-done.2, bf16[128,1024]{1,0:T(8,128)(2,1)S(1)} %copy-done.1, bf16[16,1024]{1,0:T(8,128)(2,1)S(1)} %get-tuple-element.67.pool.refs_6_, s32[8,128]{1,0:T(8,128)S(1)} %get-tuple-element.47.meta.refs_7_), custom_call_target="tpu_custom_call" | custom-call | tf_op jit(solution)/shard_map/hard/pallas_call | solution.py:30
  12.3 0.0 collective-permute-done.9.refs_1_.refs_2_
  12.3 0.0 collective-permute-done.8.sib.refs_3_
  12.3 0.6 %early.1.stats.refs_6_.refs_9_ = f32[8,256]{1,0:T(8,128)S(1)} custom-call(bf16[128,1024]{1,0:T(8,128)(2,1)S(1)} %copy-done.2, bf16[128,1024]{1,0:T(8,128)(2,1)S(1)} %collective-permute-done.8.sib.refs_3_, f32[8,128]{1,0:T(8,128)S(1)} %get-tuple-element.48.soft, bf16[128,1024]{1,0:T(8,128)(2,1)S(1)} %mark.1.refs_0_, ...), custom_call_target="tpu_custom_call" | custom-call | tf_op jit(solution)/shard_map/early/pallas_call | solution.py:30
  12.8 0.1 collective-permute-start.10
  12.9 0.2 back.1
  13.1 1.0 %collective-permute-done.10.stats_sib.refs_7_.refs_10_ = f32[8,256]{1,0:T(8,128)S(1)} collective-permute-done((f32[8,256]{1,0:T(8,128)S(1)}, f32[8,256]{1,0:T(8,128)S(1)}, u32[]{:S(2)}, u32[]{:S(2)}) %collective-permute-start.10) | collective-permute-done | bytes 8224 | tf_op jit(solution)/shard_map/ppermute | solution.py:21
  14.1 0.2 near.1
  14.3 1.6 %collective-permute-start.11 = (bf16[16,1152]{1,0:T(8,128)(2,1)S(1)}, bf16[16,1152]{1,0:T(8,128)(2,1)S(1)}, u32[]{:S(2)}, u32[]{:S(2)}) collective-permute-start(bf16[16,1152]{1,0:T(8,128)(2,1)S(1)} %get-tuple-element.53.mine), channel_id=1, source_target_pairs={{0,1},{1,0},{2,3},{3,2},{4,5},{5,4},{6,7},{7,6},{8,9},{9,8},{10,11... | collective-permute-start | bytes 110600 | tf_op jit(solution)/shard_map/ppermute | solution.py:21
  15.9 0.0 collective-permute-start.15
  15.9 0.5 %collective-permute-start.14 = (bf16[128,1024]{1,0:T(8,128)(2,1)S(1)}, bf16[128,1024]{1,0:T(8,128)(2,1)S(1)}, u32[]{:S(2)}, u32[]{:S(2)}) collective-permute-start(bf16[128,1024]{1,0:T(8,128)(2,1)S(1)} %mark.1.refs_0_), channel_id=1, source_target_pairs={{0,8},{8,0},{16,24},{24,16},{1,9},{9,1},{17,25},{25,17},{2,10},{10... | collective-permute-start | bytes 786440 | tf_op jit(solution)/shard_map/ppermute | solution.py:21
  16.4 1.9 %collective-permute-done.11.other = bf16[16,1152]{1,0:T(8,128)(2,1)S(1)} collective-permute-done((bf16[16,1152]{1,0:T(8,128)(2,1)S(1)}, bf16[16,1152]{1,0:T(8,128)(2,1)S(1)}, u32[]{:S(2)}, u32[]{:S(2)}) %collective-permute-start.11) | collective-permute-done | bytes 36896 | tf_op jit(solution)/shard_map/ppermute | solution.py:21
  18.3 0.1 merge.3.mine
  18.4 1.6 %collective-permute-start.12 = (bf16[16,1152]{1,0:T(8,128)(2,1)S(1)}, bf16[16,1152]{1,0:T(8,128)(2,1)S(1)}, u32[]{:S(2)}, u32[]{:S(2)}) collective-permute-start(bf16[16,1152]{1,0:T(8,128)(2,1)S(1)} %merge.3.mine), channel_id=1, source_target_pairs={{0,2},{1,3},{2,0},{3,1},{4,6},{5,7},{6,4},{7,5},{8,10},{9,11},{10,... | collective-permute-start | bytes 110600 | tf_op jit(solution)/shard_map/ppermute | solution.py:21
  20.0 0.8 %premises.5 = (f32[128,1024]{1,0:T(8,128)S(1)}, bf16[128,1024]{1,0:T(8,128)(2,1)S(1)}) custom-call(bf16[128,1024]{1,0:T(8,128)(2,1)S(1)} %mark.1.refs_0_, bf16[128,1024]{1,0:T(8,128)(2,1)S(1)} %collective-permute-done.9.refs_1_.refs_2_, bf16[128,1024]{1,0:T(8,128)(2,1)S(1)} %copy-done.2, bf16[128,1024]{1,0:T(8,128)(2,1)S(1)} %collective-permute-done.8.sib.refs_3_, ...), custom_call_target="tpu_custom_call" | custom-call | flops 16999999488 | tf_op jit(solution)/shard_map/premises/pallas_call | solution.py:30
  20.8 1.1 %collective-permute-start.17 = (bf16[128,1024]{1,0:T(8,128)(2,1)S(1)}, bf16[128,1024]{1,0:T(8,128)(2,1)S(1)}, u32[]{:S(2)}, u32[]{:S(2)}) collective-permute-start(bf16[128,1024]{1,0:T(8,128)(2,1)S(1)} %get-tuple-element.59), channel_id=1, source_target_pairs={{0,16},{8,24},{16,0},{24,8},{1,17},{9,25},{17,1},{25,9},{2,18},{10... | collective-permute-start | bytes 786440 | tf_op jit(solution)/shard_map/ppermute | solution.py:21
  21.9 0.5 %collective-permute-done.12.other = bf16[16,1152]{1,0:T(8,128)(2,1)S(1)} collective-permute-done((bf16[16,1152]{1,0:T(8,128)(2,1)S(1)}, bf16[16,1152]{1,0:T(8,128)(2,1)S(1)}, u32[]{:S(2)}, u32[]{:S(2)}) %collective-permute-start.12) | collective-permute-done | bytes 36896 | tf_op jit(solution)/shard_map/ppermute | solution.py:21
  22.4 0.1 merge.4.mine
  22.5 2.7 %collective-permute-start.13 = (bf16[16,1152]{1,0:T(8,128)(2,1)S(1)}, bf16[16,1152]{1,0:T(8,128)(2,1)S(1)}, u32[]{:S(2)}, u32[]{:S(2)}) collective-permute-start(bf16[16,1152]{1,0:T(8,128)(2,1)S(1)} %merge.4.mine), channel_id=1, source_target_pairs={{0,4},{1,5},{2,6},{3,7},{4,0},{5,1},{6,2},{7,3},{8,12},{9,13},{10,... | collective-permute-start | bytes 110600 | tf_op jit(solution)/shard_map/ppermute | solution.py:21
  25.1 0.0 collective-permute-done.15.refs_3_
  25.1 0.0 collective-permute-done.14.refs_1_
  25.1 0.8 %states.4.grad_states = bf16[128,1024]{1,0:T(8,128)(2,1)S(1)} custom-call(bf16[128,1024]{1,0:T(8,128)(2,1)S(1)} %copy-done.1, bf16[128,1024]{1,0:T(8,128)(2,1)S(1)} %collective-permute-done.14.refs_1_, bf16[128,1024]{1,0:T(8,128)(2,1)S(1)} %collective-permute-done.9.refs_1_.refs_2_, bf16[128,1024]{1,0:T(8,128)(2,1)S(1)} %collective-permute-done.15.refs_3_, ...), custom_call_target="tpu_custom_call" | custom-call | flops 16999999488 | tf_op jit(solution)/shard_map/states/pallas_call | solution.py:30
  25.9 1.5 %collective-permute-done.13.other = bf16[16,1152]{1,0:T(8,128)(2,1)S(1)} collective-permute-done((bf16[16,1152]{1,0:T(8,128)(2,1)S(1)}, bf16[16,1152]{1,0:T(8,128)(2,1)S(1)}, u32[]{:S(2)}, u32[]{:S(2)}) %collective-permute-start.13) | collective-permute-done | bytes 36896 | tf_op jit(solution)/shard_map/ppermute | solution.py:21
  27.4 0.1 merge.5
  27.5 0.1 collective-permute-start.16
  27.5 0.3 %collective-permute-done.17.refs_0_ = bf16[128,1024]{1,0:T(8,128)(2,1)S(1)} collective-permute-done((bf16[128,1024]{1,0:T(8,128)(2,1)S(1)}, bf16[128,1024]{1,0:T(8,128)(2,1)S(1)}, u32[]{:S(2)}, u32[]{:S(2)}) %collective-permute-start.17) | collective-permute-done | bytes 262176 | tf_op jit(solution)/shard_map/ppermute | solution.py:21
  27.9 0.9 %finish.1 = (bf16[128,1024]{1,0:T(8,128)(2,1)}, bf16[128,1024]{1,0:T(8,128)(2,1)}) custom-call(bf16[128,1024]{1,0:T(8,128)(2,1)S(1)} %states.4.grad_states, f32[128,1024]{1,0:T(8,128)S(1)} %get-tuple-element.58.grad, bf16[16,1024]{1,0:T(8,128)(2,1)S(1)} %get-tuple-element.63.home, s32[8,128]{1,0:T(8,128)S(1)} %get-tuple-element.47.meta.refs_7_, ...), custom_call_target="tpu_custom_call" | custom-call | tf_op jit(solution)/shard_map/finish/pallas_call | solution.py:30
  28.8 0.0 collective-permute-done.16.other
  28.8 0.5 %loss.1 = f32[1,1]{1,0:T(1,128)} custom-call(f32[8,128]{1,0:T(8,128)S(1)} %get-tuple-element.68.part, f32[8,128]{1,0:T(8,128)S(1)} %collective-permute-done.16.other), custom_call_target="tpu_custom_call" | custom-call | tf_op jit(solution)/shard_map/loss/pallas_call | solution.py:30
  (2 shorter events, 0.0 us)
Async XLA Ops:
  1.3 1.0 %copy-start = (bf16[128,1024]{1,0:T(8,128)(2,1)S(1)}, bf16[128,1024]{1,0:T(8,128)(2,1)}, u32[]{:S(2)}) copy-start(bf16[128,1024]{1,0:T(8,128)(2,1)} %refs_0_.3) | copy-start | bytes 786436
  2.2 3.1 %copy-start.2 = (bf16[128,1024]{1,0:T(8,128)(2,1)S(1)}, bf16[128,1024]{1,0:T(8,128)(2,1)}, u32[]{:S(2)}) copy-start(bf16[128,1024]{1,0:T(8,128)(2,1)} %refs_4_.2) | copy-start | bytes 786436
  2.3 10.0 %collective-permute-start.9 = (bf16[128,1024]{1,0:T(8,128)(2,1)S(1)}, bf16[128,1024]{1,0:T(8,128)(2,1)S(1)}, u32[]{:S(2)}, u32[]{:S(2)}) collective-permute-start(bf16[128,1024]{1,0:T(8,128)(2,1)S(1)} %mark.1.refs_0_), channel_id=1, source_target_pairs={{0,16},{8,24},{16,0},{24,8},{1,17},{9,25},{17,1},{25,9},{2,18},{10... | collective-permute-start | bytes 786440 | tf_op jit(solution)/shard_map/ppermute | solution.py:21
  5.3 7.0 %collective-permute-start.8 = (bf16[128,1024]{1,0:T(8,128)(2,1)S(1)}, bf16[128,1024]{1,0:T(8,128)(2,1)S(1)}, u32[]{:S(2)}, u32[]{:S(2)}) collective-permute-start(bf16[128,1024]{1,0:T(8,128)(2,1)S(1)} %copy-done.2), channel_id=1, source_target_pairs={{0,8},{8,0},{16,24},{24,16},{1,9},{9,1},{17,25},{25,17},{2,10},{10... | collective-permute-start | bytes 786440 | tf_op jit(solution)/shard_map/ppermute | solution.py:21
  6.0 0.7 %copy-start.3 = (s32[1,1,16]{2,1,0:T(1,128)S(1)}, s32[1,1,16]{2,1,0:T(1,128)}, u32[]{:S(2)}) copy-start(s32[1,1,16]{2,1,0:T(1,128)} %param.20) | copy-start | bytes 196
  6.0 0.7 %copy-start.4 = (s32[128]{0:T(128)S(1)}, s32[128]{0:T(128)}, u32[]{:S(2)}) copy-start(s32[128]{0:T(128)} %param.21) | copy-start | bytes 1540
  6.9 4.9 %copy-start.1 = (bf16[128,1024]{1,0:T(8,128)(2,1)S(1)}, bf16[128,1024]{1,0:T(8,128)(2,1)}, u32[]{:S(2)}) copy-start(bf16[128,1024]{1,0:T(8,128)(2,1)} %refs_0_.3) | copy-start | bytes 786436
  7.0 4.9 %collective-permute-start.3 = (bf16[16,1024]{1,0:T(8,128)(2,1)S(1)}, bf16[16,1024]{1,0:T(8,128)(2,1)S(1)}, u32[]{:S(2)}, u32[]{:S(2)}) collective-permute-start(bf16[16,1024]{1,0:T(8,128)(2,1)S(1)} %param.4), channel_id=1, source_target_pairs={{0,4},{1,5},{2,6},{3,7},{4,0},{5,1},{6,2},{7,3},{8,12},{9,13},{10,... | collective-permute-start | bytes 98312 | tf_op jit(solution)/shard_map/cond/branch_4_fun/ppermute | solution.py:21
  12.8 1.2 %collective-permute-start.10 = (f32[8,256]{1,0:T(8,128)S(1)}, f32[8,256]{1,0:T(8,128)S(1)}, u32[]{:S(2)}, u32[]{:S(2)}) collective-permute-start(f32[8,256]{1,0:T(8,128)S(1)} %early.1.stats.refs_6_.refs_9_), channel_id=1, source_target_pairs={{0,8},{8,0},{16,24},{24,16},{1,9},{9,1},{17,25},{25,17},{2,10},{10... | collective-permute-start | bytes 24584 | tf_op jit(solution)/shard_map/ppermute | solution.py:21
  14.3 4.0 %collective-permute-start.11 = (bf16[16,1152]{1,0:T(8,128)(2,1)S(1)}, bf16[16,1152]{1,0:T(8,128)(2,1)S(1)}, u32[]{:S(2)}, u32[]{:S(2)}) collective-permute-start(bf16[16,1152]{1,0:T(8,128)(2,1)S(1)} %get-tuple-element.53.mine), channel_id=1, source_target_pairs={{0,1},{1,0},{2,3},{3,2},{4,5},{5,4},{6,7},{7,6},{8,9},{9,8},{10,11... | collective-permute-start | bytes 110600 | tf_op jit(solution)/shard_map/ppermute | solution.py:21
  15.9 9.3 %collective-permute-start.15 = (bf16[128,1024]{1,0:T(8,128)(2,1)S(1)}, bf16[128,1024]{1,0:T(8,128)(2,1)S(1)}, u32[]{:S(2)}, u32[]{:S(2)}) collective-permute-start(bf16[128,1024]{1,0:T(8,128)(2,1)S(1)} %collective-permute-done.9.refs_1_.refs_2_), channel_id=1, source_target_pairs={{0,8},{8,0},{16,24},{24,16},{1,9},{9,1},{17,25},{25,17},{2,10},{10... | collective-permute-start | bytes 786440 | tf_op jit(solution)/shard_map/ppermute | solution.py:21
  15.9 9.3 %collective-permute-start.14 = (bf16[128,1024]{1,0:T(8,128)(2,1)S(1)}, bf16[128,1024]{1,0:T(8,128)(2,1)S(1)}, u32[]{:S(2)}, u32[]{:S(2)}) collective-permute-start(bf16[128,1024]{1,0:T(8,128)(2,1)S(1)} %mark.1.refs_0_), channel_id=1, source_target_pairs={{0,8},{8,0},{16,24},{24,16},{1,9},{9,1},{17,25},{25,17},{2,10},{10... | collective-permute-start | bytes 786440 | tf_op jit(solution)/shard_map/ppermute | solution.py:21
  18.4 4.0 %collective-permute-start.12 = (bf16[16,1152]{1,0:T(8,128)(2,1)S(1)}, bf16[16,1152]{1,0:T(8,128)(2,1)S(1)}, u32[]{:S(2)}, u32[]{:S(2)}) collective-permute-start(bf16[16,1152]{1,0:T(8,128)(2,1)S(1)} %merge.3.mine), channel_id=1, source_target_pairs={{0,2},{1,3},{2,0},{3,1},{4,6},{5,7},{6,4},{7,5},{8,10},{9,11},{10,... | collective-permute-start | bytes 110600 | tf_op jit(solution)/shard_map/ppermute | solution.py:21
  20.8 7.1 %collective-permute-start.17 = (bf16[128,1024]{1,0:T(8,128)(2,1)S(1)}, bf16[128,1024]{1,0:T(8,128)(2,1)S(1)}, u32[]{:S(2)}, u32[]{:S(2)}) collective-permute-start(bf16[128,1024]{1,0:T(8,128)(2,1)S(1)} %get-tuple-element.59), channel_id=1, source_target_pairs={{0,16},{8,24},{16,0},{24,8},{1,17},{9,25},{17,1},{25,9},{2,18},{10... | collective-permute-start | bytes 786440 | tf_op jit(solution)/shard_map/ppermute | solution.py:21
  22.5 4.9 %collective-permute-start.13 = (bf16[16,1152]{1,0:T(8,128)(2,1)S(1)}, bf16[16,1152]{1,0:T(8,128)(2,1)S(1)}, u32[]{:S(2)}, u32[]{:S(2)}) collective-permute-start(bf16[16,1152]{1,0:T(8,128)(2,1)S(1)} %merge.4.mine), channel_id=1, source_target_pairs={{0,4},{1,5},{2,6},{3,7},{4,0},{5,1},{6,2},{7,3},{8,12},{9,13},{10,... | collective-permute-start | bytes 110600 | tf_op jit(solution)/shard_map/ppermute | solution.py:21
  27.5 1.3 %collective-permute-start.16 = (f32[8,128]{1,0:T(8,128)S(1)}, f32[8,128]{1,0:T(8,128)S(1)}, u32[]{:S(2)}, u32[]{:S(2)}) collective-permute-start(f32[8,128]{1,0:T(8,128)S(1)} %get-tuple-element.68.part), channel_id=1, source_target_pairs={{0,8},{8,0},{16,24},{24,16},{1,9},{9,1},{17,25},{25,17},{2,10},{10... | collective-permute-start | bytes 12296 | tf_op jit(solution)/shard_map/ppermute | solution.py:21

commit v4 on v3

--- a/solution.py
+++ b/solution.py
@@ -84,16 +84,23 @@
     return message[:, :width], jnp.sum(spread, axis=0, keepdims=True)[:, 0:1]
 
 
-def mark_kernel(premises, count, marked, held, sem):
-    copy = pltpu.make_async_copy(premises, held, sem)
-    copy.start()
-    copy.wait()
+def mark_kernel(premises, states, count, marked, both, held, sems):
     rows = premises.shape[0]
+    copies = [
+        pltpu.make_async_copy(premises, held, sems.at[0]),
+        pltpu.make_async_copy(states, both.at[:rows, :], sems.at[1]),
+    ]
+    for copy in copies:
+        copy.start()
+    copies[0].wait()
     row = lax.broadcasted_iota(jnp.int32, (rows, LANES), 0)
     lane = lax.broadcasted_iota(jnp.int32, (rows, LANES), 1)
     invalid = jnp.logical_and(row >= count[0, 0], lane == 0)
-    marked[:, LANES:] = held[:, LANES:]
-    marked[:, :LANES] = jnp.where(invalid, jnp.inf, held[:, :LANES].astype(F32)).astype(BF16)
+    first = jnp.where(invalid, jnp.inf, held[:, :LANES].astype(F32)).astype(BF16)
+    for target in (marked, both.at[rows:, :]):
+        target[:, LANES:] = held[:, LANES:]
+        target[:, :LANES] = first
+    copies[1].wait()
 
 
 def is_valid(key):
@@ -125,61 +132,58 @@
     offered[...] = dot(place, premises[...], ((0,), (0,))).astype(BF16)
 
 
-def hard_kernel(states, premises, pool, meta, qval, soft):
-    rows, offer = states.shape[0], pool.shape[0]
+def back_kernel(states, qval, meta, back):
+    offer = back.shape[0]
+    weight = qval[:offer, :] * pick_of(offer, meta[0:1, :])
+    split = jnp.concatenate(parts(weight), axis=0)
+    summed = dot(split, states[...], ((1,), (0,)))
+    summed = summed[:offer] + summed[offer : 2 * offer] + summed[2 * offer :]
+    back[...] = (SCALE * summed).astype(BF16)
+
+
+def line(width):
+    return lax.broadcasted_iota(jnp.int32, (1, width), 1).astype(F32)
+
+
+def mask_keys(scores, ok):
+    return jnp.where(ok, scores, -jnp.inf)
+
+
+def score(key, block, limit):
+    return mask_keys(SCALE * dot(key, block, ((1,), (1,))), column(key.shape[0]) < limit)
+
+
+def tops(blocks):
+    return jnp.max(functools.reduce(jnp.maximum, blocks), axis=0, keepdims=True)
+
+
+def masses(blocks, top):
+    weights = functools.reduce(jnp.add, [jnp.exp(block - top) for block in blocks])
+    return jnp.sum(weights, axis=0, keepdims=True)
+
+
+def early_kernel(size, own, sib, pool, meta, *refs):
+    keys, (stats, qval) = refs[:size], refs[size:]
+    rows, offer = own.shape[0], pool.shape[0]
+    both = jnp.concatenate([own[...], sib[:rows, :]], axis=0)
+    oks = [is_valid(key) for key in keys]
+    blocks = [SCALE * dot(key[...], both, ((1,), (1,))) for key in keys]
+    slot = lax.broadcasted_iota(jnp.int32, (rows, rows), 0)
+    mine = slot == lax.broadcasted_iota(jnp.int32, (rows, rows), 1)
+    pos = jnp.sum(jnp.where(mine, blocks[0][:, :rows], 0.0), axis=0, keepdims=True)
+    blocks = [mask_keys(block, ok) for block, ok in zip(blocks, oks)]
+    top = tops(blocks)
+    stats[0:1, :] = top
+    stats[1:2, :] = masses(blocks, top)
     pick = pick_of(offer, meta[0:1, :])
-    hard = dot(pick.astype(BF16), pool[...], ((0,), (0,)))
-    states_f = states[...].astype(F32)
-    tval = SCALE * jnp.sum(states_f * hard, axis=1, keepdims=True)
-    pos = SCALE * jnp.sum(states_f * premises[...].astype(F32), axis=1, keepdims=True)
-    valid = column(rows) < count_of(meta)
+    tval = SCALE * dot(pool[...], own[...], ((1,), (1,)))
+    tval = jnp.sum(pick * tval, axis=0, keepdims=True)
+    valid = line(rows) < count_of(meta)
     gap = tval - pos
     q = jnp.where(valid, 1.0 / (1.0 + jnp.exp(-gap)), 0.0)
     plus = jnp.maximum(gap, 0.0) + jnp.log(1.0 + jnp.exp(-jnp.abs(gap)))
     qval[...] = jnp.broadcast_to(q, qval.shape)
-    soft[...] = jnp.broadcast_to(total(jnp.where(valid, plus - pos, 0.0)), soft.shape)
-
-
-def back_kernel(states, qval, meta, back):
-    offer = back.shape[0]
-    weight = qval[...].T[:offer] * pick_of(offer, meta[0:1, :])
-    split = jnp.concatenate(parts(weight), axis=0)
-    summed = dot(split, states[...], ((1,), (0,)))
-    summed = summed[:offer] + summed[offer : 2 * offer] + summed[2 * offer :]
-    back[...] = (SCALE * summed).astype(BF16)
-
-
-def line(width):
-    return lax.broadcasted_iota(jnp.int32, (1, width), 1).astype(F32)
-
-
-def mask_keys(scores, ok):
-    return jnp.where(ok, scores, -jnp.inf)
-
-
-def score(key, block, limit):
-    return mask_keys(SCALE * dot(key, block, ((1,), (1,))), column(key.shape[0]) < limit)
-
-
-def tops(blocks):
-    return jnp.max(functools.reduce(jnp.maximum, blocks), axis=0, keepdims=True)
-
-
-def masses(blocks, top):
-    weights = functools.reduce(jnp.add, [jnp.exp(block - top) for block in blocks])
-    return jnp.sum(weights, axis=0, keepdims=True)
-
-
-def early_kernel(size, own, sib, soft, *refs):
-    keys, stats = refs[:size], refs[size]
-    rows = own.shape[0]
-    both = jnp.concatenate([own[...], sib[...]], axis=0)
-    oks = [is_valid(key) for key in keys]
-    blocks = [mask_keys(SCALE * dot(key[...], both, ((1,), (1,))), ok) for key, ok in zip(keys, oks)]
-    top = tops(blocks)
-    stats[0:1, :] = top
-    stats[1:2, :] = masses(blocks, top)
-    info = jnp.broadcast_to(soft[0:1, 0:1], (1, stats.shape[1]))
+    info = jnp.broadcast_to(total(jnp.where(valid, plus - pos, 0.0)), (1, stats.shape[1]))
     for i, ok in enumerate(oks):
         info = jnp.where(line(stats.shape[1]) == 1 + i, total(jnp.where(ok, 1.0, 0.0)), info)
     stats[2:3, :] = info
@@ -231,7 +235,7 @@
     valid = slot < count_of(meta)
     limits = [limit_of(stats, stats_sib, m) for m in range(size)]
     cleared = [keys[0][...]] + [
-        jnp.where(slot < limit, key[...].astype(F32), 0.0).astype(BF16)
+        jnp.where(slot < limit, key[key.shape[0] - rows :, :].astype(F32), 0.0).astype(BF16)
         for key, limit in zip(keys[1:], limits[1:])
     ]
     cleared = jnp.concatenate(cleared, axis=0)
@@ -241,7 +245,7 @@
     prob = jnp.where(jnp.logical_and(valid, ok), jnp.exp(scores - lse_column), 0.0)
     grad = dot(prob.astype(BF16), cleared, ((1,), (0,)))
     hard = dot(pick_of(offer, meta[0:1, :]).astype(BF16), pool[...], ((0,), (0,)))
-    q = qval[:, 0:1]
+    q = qval[...].T[:, 0:1]
     vq = jnp.where(valid, 1.0, 0.0) + q
     grad = grad + q * hard - vq * keys[0][...].astype(F32)
     out[...] = (SCALE * grad).astype(BF16)
@@ -252,14 +256,14 @@
     own, sib, lse, qval, stats, stats_sib, near = refs[size : size + 7]
     far = refs[size + 7 :]
     rows = own.shape[0]
-    both = jnp.concatenate([own[...], sib[...]], axis=0)
+    both = jnp.concatenate([own[...], sib[:rows, :]], axis=0)
     row_ok = valid_lanes(stats, stats_sib, 0, rows)
     held = jnp.concatenate([key[...] for key in keys], axis=0)
     scores = SCALE * dot(held, both, ((1,), (1,)))
     ok = jnp.logical_and(is_valid(held), row_ok)
     prob = jnp.where(ok, jnp.exp(scores - lse[0:1, :]), 0.0).astype(BF16)
     grad = dot(prob, both, ((1,), (0,)))
-    vq = jnp.where(is_valid(keys[0]), 1.0, 0.0) + qval[:, 0:1]
+    vq = jnp.where(is_valid(keys[0]), 1.0, 0.0) + qval[...].T[:, 0:1]
     near[...] = grad[:rows] - SCALE * vq * own[...].astype(F32)
     for i, out in enumerate(far):
         out[...] = grad[(i + 1) * rows : (i + 2) * rows].astype(BF16)
@@ -304,15 +308,15 @@
         return lax.optimization_barrier((value, *earlier))[0] if earlier else value
 
     sources = (premises, send_rows[0], hard_idx[None, :], partner_mask[None, :], counts)
-    marked = call(
+    marked, both = call(
         mark_kernel,
         "mark",
-        shape((rows, width)),
+        (shape((rows, width)), shape((2 * rows, width))),
         premises,
+        states,
         counts,
-        ins={0: HBM, 1: SMEM},
-        scratch=[pltpu.VMEM((rows, width), BF16), pltpu.SemaphoreType.DMA(())],
-        vmem=40 << 20,
+        ins={0: HBM, 1: HBM, 2: SMEM},
+        scratch=[pltpu.VMEM((rows, width), BF16), pltpu.SemaphoreType.DMA((2,))],
     )
     offered, meta = call(
         functools.partial(front_kernel, len(sources)),
@@ -325,33 +329,26 @@
         vmem=40 << 20,
     )
     keys = across_chips({0: marked}, loop_bits)
-    states_sib = swap(states, "loop", 1)
+    both_sib = swap(both, "loop", 1)
 
     def route(m):
         return lambda block: block if m == 0 else swap(block, "groups", m)
 
     pool = lax.switch(partner_mask[0], [route(m) for m in range(group_size)], offered)
 
-    qval, soft = call(
-        hard_kernel,
-        "hard",
-        (shape((rows, rows), F32), shape((8, LANES), F32)),
+    even = range(0, loop_size, 2)
+    forward = dict(keys)
+    for m in even:
+        if m:
+            keys[m] = after(keys[m], pool)
+    stats, qval = call(
+        functools.partial(early_kernel, len(even)),
+        "early",
+        (shape((8, 2 * rows), F32), shape((rows, rows), F32)),
         states,
-        premises,
+        both_sib,
         pool,
         meta,
-    )
-    even = range(0, loop_size, 2)
-    for m in even:
-        if m:
-            keys[m] = after(keys[m], soft)
-    stats = call(
-        functools.partial(early_kernel, len(even)),
-        "early",
-        shape((8, 2 * rows), F32),
-        states,
-        states_sib,
-        soft,
         *(keys[m] for m in even),
     )
     stats_sib = swap(stats, "loop", 1)
@@ -367,84 +364,104 @@
         stats_sib,
         back,
     )
-    for m in even:
-        keys[m] = after(keys[m], message)
-    keys = from_sibling(keys)
-    grad_states = call(
-        functools.partial(states_kernel, loop_size),
-        "states",
-        shape((rows, width)),
-        premises,
-        *keys[1:],
-        states,
-        lse,
-        pool,
-        meta,
-        qval,
-        stats,
-        stats_sib,
-        cost=int(1.7e10),
-    )
-    for level in range(group_bits):
-        last = level == group_bits - 1
-        outs = (shape((offer, width)), shape((8, LANES), F32))
-        if level == 1:
-            grad, *far = call(
-                functools.partial(premises_kernel, len(even)),
-                "premises",
-                (shape((rows, width), F32),) + (shape((rows, width)),) * (len(even) - 1),
-                *(keys[m] for m in even),
-                states,
-                states_sib,
-                after(lse, message),
-                qval,
-                stats,
-                stats_sib,
-                cost=int(1.7e10),
+    held = [keys[m] for m in even]
+    for m in even[1:]:
+        keys[m | 1] = swap(after(forward[m], pool), "loop", 1)
+    keys[1] = both_sib
+    keys = [keys[m] for m in range(loop_size)]
+
+    def states_part():
+        return call(
+            functools.partial(states_kernel, loop_size),
+            "states",
+            shape((rows, width)),
+            premises,
+            *keys[1:],
+            states,
+            lse,
+            pool,
+            meta,
+            qval,
+            stats,
+            stats_sib,
+            cost=int(1.7e10),
+        )
+
+    def premises_part(lse):
+        grad, *far = call(
+            functools.partial(premises_kernel, len(even)),
+            "premises",
+            (shape((rows, width), F32),) + (shape((rows, width)),) * (len(even) - 1),
+            *held,
+            states,
+            both_sib,
+            lse,
+            qval,
+            stats,
+            stats_sib,
+            cost=int(1.7e10),
+        )
+        return grad, far
+
+    def send(far):
+        return [swap(block, "loop", m) for m, block in zip(even[1:], far)]
+
+    def finish(grad_states, grad, home, sent):
+        return call(
+            functools.partial(finish_kernel, len(sent)),
+            "finish",
+            (shape((rows, width)), shape((rows, width))),
+            grad_states,
+            grad,
+            home,
+            meta,
+            *sent,
+        )
+
+    def odd_core():
+        held = message
+        for level in range(group_bits):
+            last = level == group_bits - 1
+            if level == 0:
+                grad, far = premises_part(after(lse, held))
+            other = swap(held, "groups", 1 << level)
+            if level == 0:
+                other = after(other, grad, *far)
+                sent = send(far)
+            if level == 1:
+                grad_states = states_part()
+                other = after(other, grad_states)
+            held = call(
+                functools.partial(merge_kernel, level, last),
+                "merge",
+                (shape((offer, width)), shape((8, LANES), F32)) if last else shape(held.shape),
+                held,
+                other,
+                meta,
             )
-        other = swap(message, "groups", 1 << level)
-        if level == 2:
-            other = after(other, grad_states)
-        if level == 1:
-            other = after(other, grad, *far)
-            far = [
-                swap(block, "loop", m)
-                for m, block in zip(even[1:], far)
-            ]
-        message = call(
-            functools.partial(merge_kernel, level, last),
-            "merge",
-            outs if last else shape(message.shape),
-            message,
-            other,
-            meta,
+        home, part = held
+        grads = finish(grad_states, grad, home, sent)
+        for bit in range(1, loop_bits):
+            other = swap(part, "loop", 1 << bit)
+            part = part + (after(other, *grads) if bit == 1 else other)
+        return part, *grads
+
+    def even_core():
+        grad, far = premises_part(lse)
+        sent = send(far)
+        home = lax.switch(
+            partner_mask[0], [route(m) for m in range(group_size)], after(back, grad)
         )
-    home, part = message
+        return jnp.zeros((8, LANES), F32), *finish(states_part(), grad, home, sent)
+
     odd = lax.axis_index("loop") & 1
-
-    def across(block):
-        for bit in range(1, loop_bits):
-            block = block + swap(block, "loop", 1 << bit)
-        return block
-
-    part = lax.cond(odd == 1, across, lambda block: block, part)
-    grad_states, grad_premises = call(
-        functools.partial(finish_kernel, len(far)),
-        "finish",
-        (shape((rows, width)), shape((rows, width))),
-        grad_states,
-        grad,
-        home,
-        meta,
-        *far,
-    )
-    other = after(swap(part, "loop", 1), grad_premises)
+    part, grad_states, grad_premises = lax.cond(odd == 1, odd_core, even_core)
     loss = call(
         functools.partial(loss_kernel, loop_size * group_size * rows),
         "loss",
         shape((1, 1), F32),
         part,
-        other,
+        swap(part, "loop", 1),
     )
     return loss[0, 0], grad_states, grad_premises
 

time: 29.5 us -> 29.8 us (1.010)
  starting transfers between devices: 13.3 us -> 14.4 us
  local copies, waits for them, and re-layouts: 1.62 us -> 0.67 us
  waiting for transfers between devices: 7.39 us -> 6.48 us
  loops' own time: 0.03 us -> 0.75 us
  Pallas kernels: 4.96 us -> 5.32 us
    ppermute x11 -> x8, starting transfers between devices: 13.3 us -> 14.4 us  [swap(): return lax.ppermute(block, axis, [(i, i ^ mask) for i in range(count)])]
    unnamed x10 -> x8, local copies, waits for them, and re-layouts: 1.61 us -> 0.66 us
    ppermute x11 -> x8, waiting for transfers between devices: 7.39 us -> 6.48 us  [swap(): return lax.ppermute(block, axis, [(i, i ^ mask) for i in range(count)])]
    another operation x1 -> x2, loops' own time: 0.01 us -> 0.71 us  [the longest x1 0.68 us: body(): part, grad_states, grad_premises = lax.cond(odd == 1, odd_core, even_core)]
    pallas_call x13 -> x9, Pallas kernels: 4.96 us -> 5.32 us  [call(): pl.pallas_call(kernel, out_shape=outs, in_specs=[ins.get(i, VMEM) for i i...]
  transfers between devices with their start and end apart: 11 -> 8, of which waited for: 6 -> 6; matrix products, arithmetic and copies ran while one was open for 0% -> 0% of each run, Pallas kernels for 12% -> 7%
where the time goes in v4:
time: 29.8 us; the launch traced here: 29.6 us
  starting transfers between devices  14.4 us (48%)
  waiting for transfers between devices  6.48 us (22%)
  Pallas kernels  5.32 us (18%)
  between operations  2.01 us (7%)
  loops' own time  0.75 us (3%)
  local copies, waits for them, and re-layouts  0.67 us (2%)
    ppermute x8, starting transfers between devices, swap(): return lax.ppermute(block, axis, [(i, i ^ mask) for i in range(count)])  14.4 us
    ppermute x8, waiting for transfers between devices, swap(): return lax.ppermute(block, axis, [(i, i ^ mask) for i in range(count)])  6.48 us
    pallas_call x9, Pallas kernels, call(): pl.pallas_call(kernel, out_shape=outs, in_specs=[ins.get(i, VMEM) for i i...  5.32 us
    another operation x1, loops' own time, body(): part, grad_states, grad_premises = lax.cond(odd == 1, odd_core, even_core)  0.68 us
    unnamed x8, local copies, waits for them, and re-layouts  0.66 us
  transfers between devices with their start and end apart: 8, of which 6 were waited for; matrix products, arithmetic and copies ran while one was open for 0% of the time, Pallas kernels for 7%

profile of v4, /device:TPU:0, one launch (start us, length us, event | category | flops | bytes accessed | tf_op | source)
XLA Modules:
  0.0 29.6 jit_solution(6845106345656923374)
XLA Ops:
  1.3 0.0 copy-start.3
  1.3 1.1 %mark.1 = (bf16[128,1024]{1,0:T(8,128)(2,1)S(1)}, bf16[256,1024]{1,0:T(8,128)(2,1)S(1)}) custom-call(bf16[128,1024]{1,0:T(8,128)(2,1)} %refs_0_.1, bf16[128,1024]{1,0:T(8,128)(2,1)} %states.6, s32[1,1]{1,0:T(1,128)S(6)} %copy.31.count.refs_4_), custom_call_target="tpu_custom_call" | custom-call | tf_op jit(solution)/shard_map/mark/pallas_call | solution.py:30
  2.4 0.5 %collective-permute-start.20 = (bf16[256,1024]{1,0:T(8,128)(2,1)S(1)}, bf16[256,1024]{1,0:T(8,128)(2,1)S(1)}, u32[]{:S(2)}, u32[]{:S(2)}) collective-permute-start(bf16[256,1024]{1,0:T(8,128)(2,1)S(1)} %get-tuple-element.147), channel_id=1, source_target_pairs={{0,8},{8,0},{16,24},{24,16},{1,9},{9,1},{17,25},{25,17},{2,10},{10... | collective-permute-start | bytes 1572872 | tf_op jit(solution)/shard_map/ppermute | solution.py:21
  2.9 2.6 %collective-permute-start.21 = (bf16[128,1024]{1,0:T(8,128)(2,1)S(1)}, bf16[128,1024]{1,0:T(8,128)(2,1)S(1)}, u32[]{:S(2)}, u32[]{:S(2)}) collective-permute-start(bf16[128,1024]{1,0:T(8,128)(2,1)S(1)} %get-tuple-element.148.refs_0_), channel_id=1, source_target_pairs={{0,16},{8,24},{16,0},{24,8},{1,17},{9,25},{17,1},{25,9},{2,18},{10... | collective-permute-start | bytes 786440 | tf_op jit(solution)/shard_map/ppermute | solution.py:21
  6.1 0.0 copy-start
  6.1 0.0 copy-start.1
  6.1 0.0 copy-done.3
  6.2 0.6 %copy-done = s32[1,1,16]{2,1,0:T(1,128)S(1)} copy-done((s32[1,1,16]{2,1,0:T(1,128)S(1)}, s32[1,1,16]{2,1,0:T(1,128)}, u32[]{:S(2)}) %copy-start) | copy-done | bytes 88
  6.8 0.0 copy-done.1
  6.8 0.3 front.1
  7.1 0.0 copy-start.2
  7.1 4.9 %conditional.3 = (bf16[16,1024]{1,0:T(8,128)(2,1)S(1)}) conditional(s32[]{:T(128)} %bitcast.1, bf16[16,1024]{1,0:T(8,128)(2,1)S(1)} %get-tuple-element.149, bf16[16,1024]{1,0:T(8,128)(2,1)S(1)} %get-tuple-element.149, bf16[16,1024]{1,0:T(8,128)(2,1)S(1)} %get-tuple-element.149, ...), branch_computations={%region_0.0_spmd, %region_1.0_spmd, %region_2.0_spmd, %region_3.0_... | conditional | bytes 196656 | solution.py:337
  7.1 2.7 %collective-permute-start.3 = (bf16[16,1024]{1,0:T(8,128)(2,1)S(1)}, bf16[16,1024]{1,0:T(8,128)(2,1)S(1)}, u32[]{:S(2)}, u32[]{:S(2)}) collective-permute-start(bf16[16,1024]{1,0:T(8,128)(2,1)S(1)} %param.4), channel_id=1, source_target_pairs={{0,4},{1,5},{2,6},{3,7},{4,0},{5,1},{6,2},{7,3},{8,12},{9,13},{10,... | collective-permute-start | bytes 98312 | tf_op jit(solution)/shard_map/cond/branch_4_fun/ppermute | solution.py:21
  9.8 2.2 %collective-permute-done.3 = bf16[16,1024]{1,0:T(8,128)(2,1)S(1)} collective-permute-done((bf16[16,1024]{1,0:T(8,128)(2,1)S(1)}, bf16[16,1024]{1,0:T(8,128)(2,1)S(1)}, u32[]{:S(2)}, u32[]{:S(2)}) %collective-permute-start.3) | collective-permute-done | bytes 32800 | tf_op jit(solution)/shard_map/cond/branch_4_fun/ppermute | solution.py:21
  12.0 0.4 %collective-permute-done.21.refs_1_ = bf16[128,1024]{1,0:T(8,128)(2,1)S(1)} collective-permute-done((bf16[128,1024]{1,0:T(8,128)(2,1)S(1)}, bf16[128,1024]{1,0:T(8,128)(2,1)S(1)}, u32[]{:S(2)}, u32[]{:S(2)}) %collective-permute-start.21) | collective-permute-done | bytes 262176 | tf_op jit(solution)/shard_map/ppermute | solution.py:21
  12.4 0.0 collective-permute-start.22
  12.4 0.0 collective-permute-done.20.sib
  12.4 0.0 copy-done.2
  12.4 0.6 %early.1 = (f32[8,256]{1,0:T(8,128)S(1)}, f32[128,128]{1,0:T(8,128)S(1)}) custom-call(bf16[128,1024]{1,0:T(8,128)(2,1)S(1)} %copy-done.2, bf16[256,1024]{1,0:T(8,128)(2,1)S(1)} %collective-permute-done.20.sib, bf16[16,1024]{1,0:T(8,128)(2,1)S(1)} %get-tuple-element.168.pool, s32[8,128]{1,0:T(8,128)S(1)} %get-tuple-element.151.meta, ...), custom_call_target="tpu_custom_call" | custom-call | tf_op jit(solution)/shard_map/early/pallas_call | solution.py:30
  13.0 0.6 %collective-permute-start.23 = (f32[8,256]{1,0:T(8,128)S(1)}, f32[8,256]{1,0:T(8,128)S(1)}, u32[]{:S(2)}, u32[]{:S(2)}) collective-permute-start(f32[8,256]{1,0:T(8,128)S(1)} %get-tuple-element.152.stats), channel_id=1, source_target_pairs={{0,8},{8,0},{16,24},{24,16},{1,9},{9,1},{17,25},{25,17},{2,10},{10... | collective-permute-start | bytes 24584 | tf_op jit(solution)/shard_map/ppermute | solution.py:21
  13.6 0.1 back.1
  13.7 0.7 %collective-permute-done.23.stats_sib = f32[8,256]{1,0:T(8,128)S(1)} collective-permute-done((f32[8,256]{1,0:T(8,128)S(1)}, f32[8,256]{1,0:T(8,128)S(1)}, u32[]{:S(2)}, u32[]{:S(2)}) %collective-permute-start.23) | collective-permute-done | bytes 8224 | tf_op jit(solution)/shard_map/ppermute | solution.py:21
  14.4 0.2 near.1
  14.6 0.0 collective-permute-done.22
  14.6 10.0 %conditional.4 = (f32[8,128]{1,0:T(8,128)S(1)}, bf16[128,1024]{1,0:T(8,128)(2,1)}, bf16[128,1024]{1,0:T(8,128)(2,1)}) conditional(s32[]{:T(128)} %convert_element_type.3, (bf16[128,1024]{1,0:T(8,128)(2,1)S(1)}, bf16[256,1024]{1,0:T(8,128)(2,1)S(1)}, bf16[128,1024]{1,0:T(8,128)(2,1)S(1)}, bf16[128,1024]{1,0:T(8,128)(2,1)S(1)}, ...), branch_computations={%region_8.0_spmd, %region_17.0_spmd} | conditional | flops 33999998976 | bytes 1519840 | solution.py:458
  14.6 0.8 %premises.3 = (f32[128,1024]{1,0:T(8,128)S(1)}, bf16[128,1024]{1,0:T(8,128)(2,1)S(1)}) custom-call(bf16[128,1024]{1,0:T(8,128)(2,1)S(1)} %get-tuple-element.99.refs_0_, bf16[128,1024]{1,0:T(8,128)(2,1)S(1)} %get-tuple-element.90.refs_2_.refs_1_, bf16[128,1024]{1,0:T(8,128)(2,1)S(1)} %get-tuple-element.92.refs_4_.refs_2_, ...), custom_call_target="tpu_custom_call" | custom-call | flops 16999999488 | tf_op jit(solution)/shard_map/cond/branch_0_fun/premises/pallas_call | solution.py:30
  15.4 1.8 %collective-permute-start.14 = (bf16[128,1024]{1,0:T(8,128)(2,1)S(1)}, bf16[128,1024]{1,0:T(8,128)(2,1)S(1)}, u32[]{:S(2)}, u32[]{:S(2)}) collective-permute-start(bf16[128,1024]{1,0:T(8,128)(2,1)S(1)} %get-tuple-element.104), channel_id=1, source_target_pairs={{0,16},{8,24},{16,0},{24,8},{1,17},{9,25},{17,1},{25,9},{2,18},{10... | collective-permute-start | bytes 786440 | tf_op jit(solution)/shard_map/cond/branch_0_fun/ppermute | solution.py:21
  17.2 0.8 %states.3.grad_states = bf16[128,1024]{1,0:T(8,128)(2,1)S(1)} custom-call(bf16[128,1024]{1,0:T(8,128)(2,1)S(1)} %get-tuple-element.88.refs_0_, bf16[256,1024]{1,0:T(8,128)(2,1)S(1)} %get-tuple-element.89.refs_1_.refs_3_, bf16[128,1024]{1,0:T(8,128)(2,1)S(1)} %get-tuple-element.90.refs_2_.refs_1_, bf16[128,1024]{1,0:T(8,128)(2,1)S(1)} %get-tuple-element.91.refs_3_, ...), custom_call_target="tpu_custom_call" | custom-call | flops 16999999488 | tf_op jit(solution)/shard_map/cond/branch_0_fun/states/pallas_call | solution.py:30
  18.6 4.9 %conditional = (bf16[16,1024]{1,0:T(8,128)(2,1)S(1)}) conditional(s32[]{:T(128)} %bitcast, bf16[16,1024]{1,0:T(8,128)(2,1)S(1)} %get-tuple-element.103, bf16[16,1024]{1,0:T(8,128)(2,1)S(1)} %get-tuple-element.103, bf16[16,1024]{1,0:T(8,128)(2,1)S(1)} %get-tuple-element.103, ...), branch_computations={%region_9.0_spmd, %region_10.0_spmd, %region_11.0_spmd, %region_12... | conditional | bytes 196656 | solution.py:452
  18.7 2.7 %collective-permute-start.10 = (bf16[16,1024]{1,0:T(8,128)(2,1)S(1)}, bf16[16,1024]{1,0:T(8,128)(2,1)S(1)}, u32[]{:S(2)}, u32[]{:S(2)}) collective-permute-start(bf16[16,1024]{1,0:T(8,128)(2,1)S(1)} %param.12), channel_id=1, source_target_pairs={{0,4},{1,5},{2,6},{3,7},{4,0},{5,1},{6,2},{7,3},{8,12},{9,13},{10,... | collective-permute-start | bytes 98312 | tf_op jit(solution)/shard_map/cond/branch_0_fun/cond/branch_4_fun/ppermute | solution.py:21
  21.3 2.2 %collective-permute-done.10 = bf16[16,1024]{1,0:T(8,128)(2,1)S(1)} collective-permute-done((bf16[16,1024]{1,0:T(8,128)(2,1)S(1)}, bf16[16,1024]{1,0:T(8,128)(2,1)S(1)}, u32[]{:S(2)}, u32[]{:S(2)}) %collective-permute-start.10) | collective-permute-done | bytes 32800 | tf_op jit(solution)/shard_map/cond/branch_0_fun/cond/branch_4_fun/ppermute | solution.py:21
  23.6 0.2 collective-permute-done.14.refs_0_
  23.7 0.9 %finish.2 = (bf16[128,1024]{1,0:T(8,128)(2,1)}, bf16[128,1024]{1,0:T(8,128)(2,1)}) custom-call(bf16[128,1024]{1,0:T(8,128)(2,1)S(1)} %states.3.grad_states, f32[128,1024]{1,0:T(8,128)S(1)} %get-tuple-element.100.grad, bf16[16,1024]{1,0:T(8,128)(2,1)S(1)} %get-tuple-element.167.home, s32[8,128]{1,0:T(8,128)S(1)} %get-tuple-element.95.refs_7_.meta, ...), custom_call_target="tpu_custom_call" | custom-call | tf_op jit(solution)/shard_map/cond/branch_0_fun/finish/pallas_call | solution.py:30
  24.7 3.6 %collective-permute-start.24 = (f32[8,128]{1,0:T(8,128)S(1)}, f32[8,128]{1,0:T(8,128)S(1)}, u32[]{:S(2)}, u32[]{:S(2)}) collective-permute-start(f32[8,128]{1,0:T(8,128)S(1)} %get-tuple-element.158.part), channel_id=1, source_target_pairs={{0,8},{8,0},{16,24},{24,16},{1,9},{9,1},{17,25},{25,17},{2,10},{10... | collective-permute-start | bytes 12296 | tf_op jit(solution)/shard_map/ppermute | solution.py:21
  28.3 0.8 %collective-permute-done.24.other = f32[8,128]{1,0:T(8,128)S(1)} collective-permute-done((f32[8,128]{1,0:T(8,128)S(1)}, f32[8,128]{1,0:T(8,128)S(1)}, u32[]{:S(2)}, u32[]{:S(2)}) %collective-permute-start.24) | collective-permute-done | bytes 4128 | tf_op jit(solution)/shard_map/ppermute | solution.py:21
  29.1 0.5 %loss.1 = f32[1,1]{1,0:T(1,128)} custom-call(f32[8,128]{1,0:T(8,128)S(1)} %get-tuple-element.158.part, f32[8,128]{1,0:T(8,128)S(1)} %collective-permute-done.24.other), custom_call_target="tpu_custom_call" | custom-call | tf_op jit(solution)/shard_map/loss/pallas_call | solution.py:30
  (3 shorter events, 0.0 us)
Async XLA Ops:
  1.3 4.9 %copy-start.3 = (bf16[128,1024]{1,0:T(8,128)(2,1)S(1)}, bf16[128,1024]{1,0:T(8,128)(2,1)}, u32[]{:S(2)}) copy-start(bf16[128,1024]{1,0:T(8,128)(2,1)} %refs_0_.1) | copy-start | bytes 786436
  2.4 10.0 %collective-permute-start.20 = (bf16[256,1024]{1,0:T(8,128)(2,1)S(1)}, bf16[256,1024]{1,0:T(8,128)(2,1)S(1)}, u32[]{:S(2)}, u32[]{:S(2)}) collective-permute-start(bf16[256,1024]{1,0:T(8,128)(2,1)S(1)} %get-tuple-element.147), channel_id=1, source_target_pairs={{0,8},{8,0},{16,24},{24,16},{1,9},{9,1},{17,25},{25,17},{2,10},{10... | collective-permute-start | bytes 1572872 | tf_op jit(solution)/shard_map/ppermute | solution.py:21
  2.9 9.5 %collective-permute-start.21 = (bf16[128,1024]{1,0:T(8,128)(2,1)S(1)}, bf16[128,1024]{1,0:T(8,128)(2,1)S(1)}, u32[]{:S(2)}, u32[]{:S(2)}) collective-permute-start(bf16[128,1024]{1,0:T(8,128)(2,1)S(1)} %get-tuple-element.148.refs_0_), channel_id=1, source_target_pairs={{0,16},{8,24},{16,0},{24,8},{1,17},{9,25},{17,1},{25,9},{2,18},{10... | collective-permute-start | bytes 786440 | tf_op jit(solution)/shard_map/ppermute | solution.py:21
  6.1 0.7 %copy-start = (s32[1,1,16]{2,1,0:T(1,128)S(1)}, s32[1,1,16]{2,1,0:T(1,128)}, u32[]{:S(2)}) copy-start(s32[1,1,16]{2,1,0:T(1,128)} %param.28) | copy-start | bytes 196
  6.1 0.7 %copy-start.1 = (s32[128]{0:T(128)S(1)}, s32[128]{0:T(128)}, u32[]{:S(2)}) copy-start(s32[128]{0:T(128)} %param.29) | copy-start | bytes 1540
  7.1 5.3 %copy-start.2 = (bf16[128,1024]{1,0:T(8,128)(2,1)S(1)}, bf16[128,1024]{1,0:T(8,128)(2,1)}, u32[]{:S(2)}) copy-start(bf16[128,1024]{1,0:T(8,128)(2,1)} %states.6) | copy-start | bytes 786436
  7.1 4.9 %collective-permute-start.3 = (bf16[16,1024]{1,0:T(8,128)(2,1)S(1)}, bf16[16,1024]{1,0:T(8,128)(2,1)S(1)}, u32[]{:S(2)}, u32[]{:S(2)}) collective-permute-start(bf16[16,1024]{1,0:T(8,128)(2,1)S(1)} %param.4), channel_id=1, source_target_pairs={{0,4},{1,5},{2,6},{3,7},{4,0},{5,1},{6,2},{7,3},{8,12},{9,13},{10,... | collective-permute-start | bytes 98312 | tf_op jit(solution)/shard_map/cond/branch_4_fun/ppermute | solution.py:21
  12.4 2.2 %collective-permute-start.22 = (bf16[128,1024]{1,0:T(8,128)(2,1)S(1)}, bf16[128,1024]{1,0:T(8,128)(2,1)S(1)}, u32[]{:S(2)}, u32[]{:S(2)}) collective-permute-start(bf16[128,1024]{1,0:T(8,128)(2,1)S(1)} %collective-permute-done.21.refs_1_), channel_id=1, source_target_pairs={{0,8},{8,0},{16,24},{24,16},{1,9},{9,1},{17,25},{25,17},{2,10},{10... | collective-permute-start | bytes 786440 | tf_op jit(solution)/shard_map/ppermute | solution.py:21
  13.0 1.4 %collective-permute-start.23 = (f32[8,256]{1,0:T(8,128)S(1)}, f32[8,256]{1,0:T(8,128)S(1)}, u32[]{:S(2)}, u32[]{:S(2)}) collective-permute-start(f32[8,256]{1,0:T(8,128)S(1)} %get-tuple-element.152.stats), channel_id=1, source_target_pairs={{0,8},{8,0},{16,24},{24,16},{1,9},{9,1},{17,25},{25,17},{2,10},{10... | collective-permute-start | bytes 24584 | tf_op jit(solution)/shard_map/ppermute | solution.py:21
  15.4 8.3 %collective-permute-start.14 = (bf16[128,1024]{1,0:T(8,128)(2,1)S(1)}, bf16[128,1024]{1,0:T(8,128)(2,1)S(1)}, u32[]{:S(2)}, u32[]{:S(2)}) collective-permute-start(bf16[128,1024]{1,0:T(8,128)(2,1)S(1)} %get-tuple-element.104), channel_id=1, source_target_pairs={{0,16},{8,24},{16,0},{24,8},{1,17},{9,25},{17,1},{25,9},{2,18},{10... | collective-permute-start | bytes 786440 | tf_op jit(solution)/shard_map/cond/branch_0_fun/ppermute | solution.py:21
  18.7 4.9 %collective-permute-start.10 = (bf16[16,1024]{1,0:T(8,128)(2,1)S(1)}, bf16[16,1024]{1,0:T(8,128)(2,1)S(1)}, u32[]{:S(2)}, u32[]{:S(2)}) collective-permute-start(bf16[16,1024]{1,0:T(8,128)(2,1)S(1)} %param.12), channel_id=1, source_target_pairs={{0,4},{1,5},{2,6},{3,7},{4,0},{5,1},{6,2},{7,3},{8,12},{9,13},{10,... | collective-permute-start | bytes 98312 | tf_op jit(solution)/shard_map/cond/branch_0_fun/cond/branch_4_fun/ppermute | solution.py:21
  24.7 4.4 %collective-permute-start.24 = (f32[8,128]{1,0:T(8,128)S(1)}, f32[8,128]{1,0:T(8,128)S(1)}, u32[]{:S(2)}, u32[]{:S(2)}) collective-permute-start(f32[8,128]{1,0:T(8,128)S(1)} %get-tuple-element.158.part), channel_id=1, source_target_pairs={{0,8},{8,0},{16,24},{24,16},{1,9},{9,1},{17,25},{25,17},{2,10},{10... | collective-permute-start | bytes 12296 | tf_op jit(solution)/shard_map/ppermute | solution.py:21

commit v5 on v4

--- a/solution.py
+++ b/solution.py
@@ -84,23 +84,23 @@
     return message[:, :width], jnp.sum(spread, axis=0, keepdims=True)[:, 0:1]
 
 
-def mark_kernel(premises, states, count, marked, both, held, sems):
+def mark_kernel(premises, count, marked, sems):
     rows = premises.shape[0]
+    size = rows // 1
+    pieces = [pl.ds(i * size, size) for i in range(1)]
     copies = [
-        pltpu.make_async_copy(premises, held, sems.at[0]),
-        pltpu.make_async_copy(states, both.at[:rows, :], sems.at[1]),
+        pltpu.make_async_copy(premises.at[piece, :], marked.at[piece, :], sems.at[i])
+        for i, piece in enumerate(pieces)
     ]
     for copy in copies:
         copy.start()
-    copies[0].wait()
-    row = lax.broadcasted_iota(jnp.int32, (rows, LANES), 0)
-    lane = lax.broadcasted_iota(jnp.int32, (rows, LANES), 1)
-    invalid = jnp.logical_and(row >= count[0, 0], lane == 0)
-    first = jnp.where(invalid, jnp.inf, held[:, :LANES].astype(F32)).astype(BF16)
-    for target in (marked, both.at[rows:, :]):
-        target[:, LANES:] = held[:, LANES:]
-        target[:, :LANES] = first
-    copies[1].wait()
+    for i, copy in enumerate(copies):
+        copy.wait()
+        row = lax.broadcasted_iota(jnp.int32, (size, LANES), 0) + i * size
+        lane = lax.broadcasted_iota(jnp.int32, (size, LANES), 1)
+        invalid = jnp.logical_and(row >= count[0, 0], lane == 0)
+        first = marked[pieces[i], :LANES].astype(F32)
+        marked[pieces[i], :LANES] = jnp.where(invalid, jnp.inf, first).astype(BF16)
 
 
 def is_valid(key):
@@ -165,7 +165,7 @@
 def early_kernel(size, own, sib, pool, meta, *refs):
     keys, (stats, qval) = refs[:size], refs[size:]
     rows, offer = own.shape[0], pool.shape[0]
-    both = jnp.concatenate([own[...], sib[:rows, :]], axis=0)
+    both = jnp.concatenate([own[...], sib[...]], axis=0)
     oks = [is_valid(key) for key in keys]
     blocks = [SCALE * dot(key[...], both, ((1,), (1,))) for key in keys]
     slot = lax.broadcasted_iota(jnp.int32, (rows, rows), 0)
@@ -235,7 +235,7 @@
     valid = slot < count_of(meta)
     limits = [limit_of(stats, stats_sib, m) for m in range(size)]
     cleared = [keys[0][...]] + [
-        jnp.where(slot < limit, key[key.shape[0] - rows :, :].astype(F32), 0.0).astype(BF16)
+        jnp.where(slot < limit, key[...].astype(F32), 0.0).astype(BF16)
         for key, limit in zip(keys[1:], limits[1:])
     ]
     cleared = jnp.concatenate(cleared, axis=0)
@@ -256,7 +256,7 @@
     own, sib, lse, qval, stats, stats_sib, near = refs[size : size + 7]
     far = refs[size + 7 :]
     rows = own.shape[0]
-    both = jnp.concatenate([own[...], sib[:rows, :]], axis=0)
+    both = jnp.concatenate([own[...], sib[...]], axis=0)
     row_ok = valid_lanes(stats, stats_sib, 0, rows)
     held = jnp.concatenate([key[...] for key in keys], axis=0)
     scores = SCALE * dot(held, both, ((1,), (1,)))
@@ -308,15 +308,15 @@
         return lax.optimization_barrier((value, *earlier))[0] if earlier else value
 
     sources = (premises, send_rows[0], hard_idx[None, :], partner_mask[None, :], counts)
-    marked, both = call(
+    marked = call(
         mark_kernel,
         "mark",
-        (shape((rows, width)), shape((2 * rows, width))),
+        shape((rows, width)),
         premises,
-        states,
         counts,
-        ins={0: HBM, 1: HBM, 2: SMEM},
-        scratch=[pltpu.VMEM((rows, width), BF16), pltpu.SemaphoreType.DMA((2,))],
+        ins={0: HBM, 1: SMEM},
+        scratch=[pltpu.SemaphoreType.DMA((1,))],
+        vmem=40 << 20,
     )
     offered, meta = call(
         functools.partial(front_kernel, len(sources)),
@@ -329,7 +329,7 @@
         vmem=40 << 20,
     )
     keys = across_chips({0: marked}, loop_bits)
-    both_sib = swap(both, "loop", 1)
+    states_sib = swap(states, "loop", 1)
 
     def route(m):
         return lambda block: block if m == 0 else swap(block, "groups", m)
@@ -346,7 +346,7 @@
         "early",
         (shape((8, 2 * rows), F32), shape((rows, rows), F32)),
         states,
-        both_sib,
+        states_sib,
         pool,
         meta,
         *(keys[m] for m in even),
@@ -365,9 +365,8 @@
         back,
     )
     held = [keys[m] for m in even]
-    for m in even[1:]:
+    for m in even:
         keys[m | 1] = swap(after(forward[m], pool), "loop", 1)
-    keys[1] = both_sib
     keys = [keys[m] for m in range(loop_size)]
 
     def states_part():
@@ -394,7 +393,7 @@
             (shape((rows, width), F32),) + (shape((rows, width)),) * (len(even) - 1),
             *held,
             states,
-            both_sib,
+            states_sib,
             lse,
             qval,
             stats,
@@ -428,7 +427,7 @@
             if level == 0:
                 other = after(other, grad, *far)
                 sent = send(far)
-            if level == 1:
+            if level == 2:
                 grad_states = states_part()
                 other = after(other, grad_states)
             held = call(

time: 29.8 us -> 29.4 us (0.987); the launches traced: 29.6 us -> 29.6 us
  waiting for transfers between devices: 6.48 us -> 6.83 us
  starting transfers between devices: 14.4 us -> 14.1 us
    ppermute x8 -> x9, waiting for transfers between devices: 6.48 us -> 6.83 us  [swap(): return lax.ppermute(block, axis, [(i, i ^ mask) for i in range(count)])]
    ppermute x8 -> x9, starting transfers between devices: 14.4 us -> 14.1 us  [swap(): return lax.ppermute(block, axis, [(i, i ^ mask) for i in range(count)])]
  transfers between devices with their start and end apart: 8 -> 9, of which waited for: 6 -> 5; matrix products, arithmetic and copies ran while one was open for 0% -> 0% of each run, Pallas kernels for 7% -> 7%
where the time goes in v5:
time: 29.4 us; the launch traced here: 29.6 us
  starting transfers between devices  14.1 us (48%)
  waiting for transfers between devices  6.83 us (23%)
  Pallas kernels  5.26 us (18%)
  between operations  2.02 us (7%)
  loops' own time  0.75 us (3%)
  local copies, waits for them, and re-layouts  0.66 us (2%)
    ppermute x9, starting transfers between devices, swap(): return lax.ppermute(block, axis, [(i, i ^ mask) for i in range(count)])  14.1 us
    ppermute x9, waiting for transfers between devices, swap(): return lax.ppermute(block, axis, [(i, i ^ mask) for i in range(count)])  6.83 us
    pallas_call x9, Pallas kernels, call(): pl.pallas_call(kernel, out_shape=outs, in_specs=[ins.get(i, VMEM) for i i...  5.26 us
    another operation x1, loops' own time, body(): part, grad_states, grad_premises = lax.cond(odd == 1, odd_core, even_core)  0.68 us
    unnamed x8, local copies, waits for them, and re-layouts  0.66 us
  transfers between devices with their start and end apart: 9, of which 5 were waited for; matrix products, arithmetic and copies ran while one was open for 0% of the time, Pallas kernels for 7%

profile of v5, /device:TPU:0, one launch (start us, length us, event | category | flops | bytes accessed | tf_op | source)
XLA Modules:
  0.0 29.6 jit_solution(1619882452973170192)
XLA Ops:
  1.3 0.0 copy-start.3
  1.3 0.0 copy-start.2
  1.3 1.0 %mark.1.refs_0_ = bf16[128,1024]{1,0:T(8,128)(2,1)S(1)} custom-call(bf16[128,1024]{1,0:T(8,128)(2,1)} %refs_0_.1, s32[1,1]{1,0:T(1,128)S(6)} %copy.31.count.refs_4_), custom_call_target="tpu_custom_call" | custom-call | tf_op jit(solution)/shard_map/mark/pallas_call | solution.py:30
  2.3 3.0 %collective-permute-start.21 = (bf16[128,1024]{1,0:T(8,128)(2,1)S(1)}, bf16[128,1024]{1,0:T(8,128)(2,1)S(1)}, u32[]{:S(2)}, u32[]{:S(2)}) collective-permute-start(bf16[128,1024]{1,0:T(8,128)(2,1)S(1)} %mark.1.refs_0_), channel_id=1, source_target_pairs={{0,16},{8,24},{16,0},{24,8},{1,17},{9,25},{17,1},{25,9},{2,18},{10... | collective-permute-start | bytes 786440 | tf_op jit(solution)/shard_map/ppermute | solution.py:21
  5.3 0.0 copy-done.3
  5.4 0.0 collective-permute-start.23
  6.0 0.0 copy-start
  6.0 0.0 copy-start.1
  6.0 0.0 copy-done.2
  6.0 0.6 %copy-done = s32[1,1,16]{2,1,0:T(1,128)S(1)} copy-done((s32[1,1,16]{2,1,0:T(1,128)S(1)}, s32[1,1,16]{2,1,0:T(1,128)}, u32[]{:S(2)}) %copy-start) | copy-done | bytes 88
  6.7 0.0 copy-done.1
  6.7 0.3 front.1
  7.0 4.9 %conditional.3 = (bf16[16,1024]{1,0:T(8,128)(2,1)S(1)}) conditional(s32[]{:T(128)} %bitcast.1, bf16[16,1024]{1,0:T(8,128)(2,1)S(1)} %get-tuple-element.152, bf16[16,1024]{1,0:T(8,128)(2,1)S(1)} %get-tuple-element.152, bf16[16,1024]{1,0:T(8,128)(2,1)S(1)} %get-tuple-element.152, ...), branch_computations={%region_0.0_spmd, %region_1.0_spmd, %region_2.0_spmd, %region_3.0_... | conditional | bytes 196656 | solution.py:337
  7.0 2.7 %collective-permute-start.3 = (bf16[16,1024]{1,0:T(8,128)(2,1)S(1)}, bf16[16,1024]{1,0:T(8,128)(2,1)S(1)}, u32[]{:S(2)}, u32[]{:S(2)}) collective-permute-start(bf16[16,1024]{1,0:T(8,128)(2,1)S(1)} %param.4), channel_id=1, source_target_pairs={{0,4},{1,5},{2,6},{3,7},{4,0},{5,1},{6,2},{7,3},{8,12},{9,13},{10,... | collective-permute-start | bytes 98312 | tf_op jit(solution)/shard_map/cond/branch_4_fun/ppermute | solution.py:21
  9.6 2.2 %collective-permute-done.3 = bf16[16,1024]{1,0:T(8,128)(2,1)S(1)} collective-permute-done((bf16[16,1024]{1,0:T(8,128)(2,1)S(1)}, bf16[16,1024]{1,0:T(8,128)(2,1)S(1)}, u32[]{:S(2)}, u32[]{:S(2)}) %collective-permute-start.3) | collective-permute-done | bytes 32800 | tf_op jit(solution)/shard_map/cond/branch_4_fun/ppermute | solution.py:21
  11.9 1.3 %collective-permute-start.20 = (bf16[128,1024]{1,0:T(8,128)(2,1)S(1)}, bf16[128,1024]{1,0:T(8,128)(2,1)S(1)}, u32[]{:S(2)}, u32[]{:S(2)}) collective-permute-start(bf16[128,1024]{1,0:T(8,128)(2,1)S(1)} %mark.1.refs_0_), channel_id=1, source_target_pairs={{0,8},{8,0},{16,24},{24,16},{1,9},{9,1},{17,25},{25,17},{2,10},{10... | collective-permute-start | bytes 786440 | tf_op jit(solution)/shard_map/ppermute | solution.py:21
  13.2 0.0 collective-permute-done.21.refs_1_
  13.2 0.1 collective-permute-start.22
  13.2 0.0 collective-permute-done.23.sib
  13.2 0.6 %early.1 = (f32[8,256]{1,0:T(8,128)S(1)}, f32[128,128]{1,0:T(8,128)S(1)}) custom-call(bf16[128,1024]{1,0:T(8,128)(2,1)S(1)} %copy-done.3, bf16[128,1024]{1,0:T(8,128)(2,1)S(1)} %collective-permute-done.23.sib, bf16[16,1024]{1,0:T(8,128)(2,1)S(1)} %get-tuple-element.172.pool, s32[8,128]{1,0:T(8,128)S(1)} %get-tuple-element.155.meta, ...), custom_call_target="tpu_custom_call" | custom-call | tf_op jit(solution)/shard_map/early/pallas_call | solution.py:30
  13.9 0.5 %collective-permute-start.24 = (f32[8,256]{1,0:T(8,128)S(1)}, f32[8,256]{1,0:T(8,128)S(1)}, u32[]{:S(2)}, u32[]{:S(2)}) collective-permute-start(f32[8,256]{1,0:T(8,128)S(1)} %get-tuple-element.156.stats), channel_id=1, source_target_pairs={{0,8},{8,0},{16,24},{24,16},{1,9},{9,1},{17,25},{25,17},{2,10},{10... | collective-permute-start | bytes 24584 | tf_op jit(solution)/shard_map/ppermute | solution.py:21
  14.4 0.1 back.1
  14.5 0.7 %collective-permute-done.24.stats_sib = f32[8,256]{1,0:T(8,128)S(1)} collective-permute-done((f32[8,256]{1,0:T(8,128)S(1)}, f32[8,256]{1,0:T(8,128)S(1)}, u32[]{:S(2)}, u32[]{:S(2)}) %collective-permute-start.24) | collective-permute-done | bytes 8224 | tf_op jit(solution)/shard_map/ppermute | solution.py:21
  15.2 0.2 near.1
  15.4 0.0 collective-permute-done.20
  15.4 0.0 collective-permute-done.22
  15.4 9.2 %conditional.4 = (f32[8,128]{1,0:T(8,128)S(1)}, bf16[128,1024]{1,0:T(8,128)(2,1)}, bf16[128,1024]{1,0:T(8,128)(2,1)}) conditional(s32[]{:T(128)} %convert_element_type.3, (bf16[128,1024]{1,0:T(8,128)(2,1)S(1)}, bf16[128,1024]{1,0:T(8,128)(2,1)S(1)}, bf16[128,1024]{1,0:T(8,128)(2,1)S(1)}, bf16[128,1024]{1,0:T(8,128)(2,1)S(1)}, ...), branch_computations={%region_8.0_spmd, %region_17.0_spmd} | conditional | flops 33999998976 | bytes 1519840 | solution.py:457
  15.4 0.8 %premises.3 = (f32[128,1024]{1,0:T(8,128)S(1)}, bf16[128,1024]{1,0:T(8,128)(2,1)S(1)}) custom-call(bf16[128,1024]{1,0:T(8,128)(2,1)S(1)} %get-tuple-element.103.refs_0_, bf16[128,1024]{1,0:T(8,128)(2,1)S(1)} %get-tuple-element.94.refs_2_.refs_1_, bf16[128,1024]{1,0:T(8,128)(2,1)S(1)} %get-tuple-element.96.refs_4_.refs_2_, ...), custom_call_target="tpu_custom_call" | custom-call | flops 16999999488 | tf_op jit(solution)/shard_map/cond/branch_0_fun/premises/pallas_call | solution.py:30
  16.2 0.3 collective-permute-start.14
  16.5 0.7 %states.2.grad_states = bf16[128,1024]{1,0:T(8,128)(2,1)S(1)} custom-call(bf16[128,1024]{1,0:T(8,128)(2,1)S(1)} %get-tuple-element.92.refs_0_, bf16[128,1024]{1,0:T(8,128)(2,1)S(1)} %get-tuple-element.93.refs_1_, bf16[128,1024]{1,0:T(8,128)(2,1)S(1)} %get-tuple-element.94.refs_2_.refs_1_, bf16[128,1024]{1,0:T(8,128)(2,1)S(1)} %get-tuple-element.95.refs_3_, ...), custom_call_target="tpu_custom_call" | custom-call | flops 16999999488 | tf_op jit(solution)/shard_map/cond/branch_0_fun/states/pallas_call | solution.py:30
  17.9 4.9 %conditional = (bf16[16,1024]{1,0:T(8,128)(2,1)S(1)}) conditional(s32[]{:T(128)} %bitcast, bf16[16,1024]{1,0:T(8,128)(2,1)S(1)} %get-tuple-element.108, bf16[16,1024]{1,0:T(8,128)(2,1)S(1)} %get-tuple-element.108, bf16[16,1024]{1,0:T(8,128)(2,1)S(1)} %get-tuple-element.108, ...), branch_computations={%region_9.0_spmd, %region_10.0_spmd, %region_11.0_spmd, %region_12... | conditional | bytes 196656 | solution.py:451
  18.0 2.7 %collective-permute-start.10 = (bf16[16,1024]{1,0:T(8,128)(2,1)S(1)}, bf16[16,1024]{1,0:T(8,128)(2,1)S(1)}, u32[]{:S(2)}, u32[]{:S(2)}) collective-permute-start(bf16[16,1024]{1,0:T(8,128)(2,1)S(1)} %param.12), channel_id=1, source_target_pairs={{0,4},{1,5},{2,6},{3,7},{4,0},{5,1},{6,2},{7,3},{8,12},{9,13},{10,... | collective-permute-start | bytes 98312 | tf_op jit(solution)/shard_map/cond/branch_0_fun/cond/branch_4_fun/ppermute | solution.py:21
  20.6 2.2 %collective-permute-done.10 = bf16[16,1024]{1,0:T(8,128)(2,1)S(1)} collective-permute-done((bf16[16,1024]{1,0:T(8,128)(2,1)S(1)}, bf16[16,1024]{1,0:T(8,128)(2,1)S(1)}, u32[]{:S(2)}, u32[]{:S(2)}) %collective-permute-start.10) | collective-permute-done | bytes 32800 | tf_op jit(solution)/shard_map/cond/branch_0_fun/cond/branch_4_fun/ppermute | solution.py:21
  22.8 0.9 %collective-permute-done.14.refs_0_ = bf16[128,1024]{1,0:T(8,128)(2,1)S(1)} collective-permute-done((bf16[128,1024]{1,0:T(8,128)(2,1)S(1)}, bf16[128,1024]{1,0:T(8,128)(2,1)S(1)}, u32[]{:S(2)}, u32[]{:S(2)}) %collective-permute-start.14) | collective-permute-done | bytes 262176 | tf_op jit(solution)/shard_map/cond/branch_0_fun/ppermute | solution.py:21
  23.7 0.9 %finish.2 = (bf16[128,1024]{1,0:T(8,128)(2,1)}, bf16[128,1024]{1,0:T(8,128)(2,1)}) custom-call(bf16[128,1024]{1,0:T(8,128)(2,1)S(1)} %states.2.grad_states, f32[128,1024]{1,0:T(8,128)S(1)} %get-tuple-element.105.grad, bf16[16,1024]{1,0:T(8,128)(2,1)S(1)} %get-tuple-element.171.home, s32[8,128]{1,0:T(8,128)S(1)} %get-tuple-element.99.refs_7_.meta, ...), custom_call_target="tpu_custom_call" | custom-call | tf_op jit(solution)/shard_map/cond/branch_0_fun/finish/pallas_call | solution.py:30
  24.6 3.7 %collective-permute-start.25 = (f32[8,128]{1,0:T(8,128)S(1)}, f32[8,128]{1,0:T(8,128)S(1)}, u32[]{:S(2)}, u32[]{:S(2)}) collective-permute-start(f32[8,128]{1,0:T(8,128)S(1)} %get-tuple-element.162.part), channel_id=1, source_target_pairs={{0,8},{8,0},{16,24},{24,16},{1,9},{9,1},{17,25},{25,17},{2,10},{10... | collective-permute-start | bytes 12296 | tf_op jit(solution)/shard_map/ppermute | solution.py:21
  28.3 0.8 %collective-permute-done.25.other = f32[8,128]{1,0:T(8,128)S(1)} collective-permute-done((f32[8,128]{1,0:T(8,128)S(1)}, f32[8,128]{1,0:T(8,128)S(1)}, u32[]{:S(2)}, u32[]{:S(2)}) %collective-permute-start.25) | collective-permute-done | bytes 4128 | tf_op jit(solution)/shard_map/ppermute | solution.py:21
  29.1 0.5 %loss.1 = f32[1,1]{1,0:T(1,128)} custom-call(f32[8,128]{1,0:T(8,128)S(1)} %get-tuple-element.162.part, f32[8,128]{1,0:T(8,128)S(1)} %collective-permute-done.25.other), custom_call_target="tpu_custom_call" | custom-call | tf_op jit(solution)/shard_map/loss/pallas_call | solution.py:30
  (3 shorter events, 0.0 us)
Async XLA Ops:
  1.3 4.1 %copy-start.3 = (bf16[128,1024]{1,0:T(8,128)(2,1)S(1)}, bf16[128,1024]{1,0:T(8,128)(2,1)}, u32[]{:S(2)}) copy-start(bf16[128,1024]{1,0:T(8,128)(2,1)} %states.4) | copy-start | bytes 786436
  1.3 4.7 %copy-start.2 = (bf16[128,1024]{1,0:T(8,128)(2,1)S(1)}, bf16[128,1024]{1,0:T(8,128)(2,1)}, u32[]{:S(2)}) copy-start(bf16[128,1024]{1,0:T(8,128)(2,1)} %refs_0_.1) | copy-start | bytes 786436
  2.3 10.8 %collective-permute-start.21 = (bf16[128,1024]{1,0:T(8,128)(2,1)S(1)}, bf16[128,1024]{1,0:T(8,128)(2,1)S(1)}, u32[]{:S(2)}, u32[]{:S(2)}) collective-permute-start(bf16[128,1024]{1,0:T(8,128)(2,1)S(1)} %mark.1.refs_0_), channel_id=1, source_target_pairs={{0,16},{8,24},{16,0},{24,8},{1,17},{9,25},{17,1},{25,9},{2,18},{10... | collective-permute-start | bytes 786440 | tf_op jit(solution)/shard_map/ppermute | solution.py:21
  5.4 7.9 %collective-permute-start.23 = (bf16[128,1024]{1,0:T(8,128)(2,1)S(1)}, bf16[128,1024]{1,0:T(8,128)(2,1)S(1)}, u32[]{:S(2)}, u32[]{:S(2)}) collective-permute-start(bf16[128,1024]{1,0:T(8,128)(2,1)S(1)} %copy-done.3), channel_id=1, source_target_pairs={{0,8},{8,0},{16,24},{24,16},{1,9},{9,1},{17,25},{25,17},{2,10},{10... | collective-permute-start | bytes 786440 | tf_op jit(solution)/shard_map/ppermute | solution.py:21
  6.0 0.7 %copy-start = (s32[1,1,16]{2,1,0:T(1,128)S(1)}, s32[1,1,16]{2,1,0:T(1,128)}, u32[]{:S(2)}) copy-start(s32[1,1,16]{2,1,0:T(1,128)} %param.28) | copy-start | bytes 196
  6.0 0.7 %copy-start.1 = (s32[128]{0:T(128)S(1)}, s32[128]{0:T(128)}, u32[]{:S(2)}) copy-start(s32[128]{0:T(128)} %param.29) | copy-start | bytes 1540
  7.0 4.9 %collective-permute-start.3 = (bf16[16,1024]{1,0:T(8,128)(2,1)S(1)}, bf16[16,1024]{1,0:T(8,128)(2,1)S(1)}, u32[]{:S(2)}, u32[]{:S(2)}) collective-permute-start(bf16[16,1024]{1,0:T(8,128)(2,1)S(1)} %param.4), channel_id=1, source_target_pairs={{0,4},{1,5},{2,6},{3,7},{4,0},{5,1},{6,2},{7,3},{8,12},{9,13},{10,... | collective-permute-start | bytes 98312 | tf_op jit(solution)/shard_map/cond/branch_4_fun/ppermute | solution.py:21
  11.9 3.5 %collective-permute-start.20 = (bf16[128,1024]{1,0:T(8,128)(2,1)S(1)}, bf16[128,1024]{1,0:T(8,128)(2,1)S(1)}, u32[]{:S(2)}, u32[]{:S(2)}) collective-permute-start(bf16[128,1024]{1,0:T(8,128)(2,1)S(1)} %mark.1.refs_0_), channel_id=1, source_target_pairs={{0,8},{8,0},{16,24},{24,16},{1,9},{9,1},{17,25},{25,17},{2,10},{10... | collective-permute-start | bytes 786440 | tf_op jit(solution)/shard_map/ppermute | solution.py:21
  13.2 2.2 %collective-permute-start.22 = (bf16[128,1024]{1,0:T(8,128)(2,1)S(1)}, bf16[128,1024]{1,0:T(8,128)(2,1)S(1)}, u32[]{:S(2)}, u32[]{:S(2)}) collective-permute-start(bf16[128,1024]{1,0:T(8,128)(2,1)S(1)} %collective-permute-done.21.refs_1_), channel_id=1, source_target_pairs={{0,8},{8,0},{16,24},{24,16},{1,9},{9,1},{17,25},{25,17},{2,10},{10... | collective-permute-start | bytes 786440 | tf_op jit(solution)/shard_map/ppermute | solution.py:21
  13.9 1.3 %collective-permute-start.24 = (f32[8,256]{1,0:T(8,128)S(1)}, f32[8,256]{1,0:T(8,128)S(1)}, u32[]{:S(2)}, u32[]{:S(2)}) collective-permute-start(f32[8,256]{1,0:T(8,128)S(1)} %get-tuple-element.156.stats), channel_id=1, source_target_pairs={{0,8},{8,0},{16,24},{24,16},{1,9},{9,1},{17,25},{25,17},{2,10},{10... | collective-permute-start | bytes 24584 | tf_op jit(solution)/shard_map/ppermute | solution.py:21
  16.2 7.5 %collective-permute-start.14 = (bf16[128,1024]{1,0:T(8,128)(2,1)S(1)}, bf16[128,1024]{1,0:T(8,128)(2,1)S(1)}, u32[]{:S(2)}, u32[]{:S(2)}) collective-permute-start(bf16[128,1024]{1,0:T(8,128)(2,1)S(1)} %get-tuple-element.109), channel_id=1, source_target_pairs={{0,16},{8,24},{16,0},{24,8},{1,17},{9,25},{17,1},{25,9},{2,18},{10... | collective-permute-start | bytes 786440 | tf_op jit(solution)/shard_map/cond/branch_0_fun/ppermute | solution.py:21
  18.0 4.9 %collective-permute-start.10 = (bf16[16,1024]{1,0:T(8,128)(2,1)S(1)}, bf16[16,1024]{1,0:T(8,128)(2,1)S(1)}, u32[]{:S(2)}, u32[]{:S(2)}) collective-permute-start(bf16[16,1024]{1,0:T(8,128)(2,1)S(1)} %param.12), channel_id=1, source_target_pairs={{0,4},{1,5},{2,6},{3,7},{4,0},{5,1},{6,2},{7,3},{8,12},{9,13},{10,... | collective-permute-start | bytes 98312 | tf_op jit(solution)/shard_map/cond/branch_0_fun/cond/branch_4_fun/ppermute | solution.py:21
  24.6 4.5 %collective-permute-start.25 = (f32[8,128]{1,0:T(8,128)S(1)}, f32[8,128]{1,0:T(8,128)S(1)}, u32[]{:S(2)}, u32[]{:S(2)}) collective-permute-start(f32[8,128]{1,0:T(8,128)S(1)} %get-tuple-element.162.part), channel_id=1, source_target_pairs={{0,8},{8,0},{16,24},{24,16},{1,9},{9,1},{17,25},{25,17},{2,10},{10... | collective-permute-start | bytes 12296 | tf_op jit(solution)/shard_map/ppermute | solution.py:21

commit v6 on v5

--- a/solution.py
+++ b/solution.py
@@ -103,6 +103,12 @@
         marked[pieces[i], :LANES] = jnp.where(invalid, jnp.inf, first).astype(BF16)
 
 
+def pair_kernel(states, marked, both):
+    rows = states.shape[0]
+    both[:rows, :] = states[...]
+    both[rows:, :] = marked[...]
+
+
 def is_valid(key):
     return key[:, 0:1].astype(F32) < jnp.inf
 
@@ -165,7 +171,7 @@
 def early_kernel(size, own, sib, pool, meta, *refs):
     keys, (stats, qval) = refs[:size], refs[size:]
     rows, offer = own.shape[0], pool.shape[0]
-    both = jnp.concatenate([own[...], sib[...]], axis=0)
+    both = jnp.concatenate([own[...], sib[: own.shape[0], :]], axis=0)
     oks = [is_valid(key) for key in keys]
     blocks = [SCALE * dot(key[...], both, ((1,), (1,))) for key in keys]
     slot = lax.broadcasted_iota(jnp.int32, (rows, rows), 0)
@@ -235,7 +241,7 @@
     valid = slot < count_of(meta)
     limits = [limit_of(stats, stats_sib, m) for m in range(size)]
     cleared = [keys[0][...]] + [
-        jnp.where(slot < limit, key[...].astype(F32), 0.0).astype(BF16)
+        jnp.where(slot < limit, key[key.shape[0] - rows :, :].astype(F32), 0.0).astype(BF16)
         for key, limit in zip(keys[1:], limits[1:])
     ]
     cleared = jnp.concatenate(cleared, axis=0)
@@ -256,7 +262,7 @@
     own, sib, lse, qval, stats, stats_sib, near = refs[size : size + 7]
     far = refs[size + 7 :]
     rows = own.shape[0]
-    both = jnp.concatenate([own[...], sib[...]], axis=0)
+    both = jnp.concatenate([own[...], sib[: own.shape[0], :]], axis=0)
     row_ok = valid_lanes(stats, stats_sib, 0, rows)
     held = jnp.concatenate([key[...] for key in keys], axis=0)
     scores = SCALE * dot(held, both, ((1,), (1,)))
@@ -329,7 +335,10 @@
         vmem=40 << 20,
     )
     keys = across_chips({0: marked}, loop_bits)
-    states_sib = swap(states, "loop", 1)
+    both = call(
+        pair_kernel, "pair", shape((2 * rows, width)), states, marked, cost=int(1.7e10)
+    )
+    both_sib = swap(both, "loop", 1)
 
     def route(m):
         return lambda block: block if m == 0 else swap(block, "groups", m)
@@ -346,7 +355,7 @@
         "early",
         (shape((8, 2 * rows), F32), shape((rows, rows), F32)),
         states,
-        states_sib,
+        both_sib,
         pool,
         meta,
         *(keys[m] for m in even),
@@ -365,8 +374,9 @@
         back,
     )
     held = [keys[m] for m in even]
-    for m in even:
+    for m in even[1:]:
         keys[m | 1] = swap(after(forward[m], pool), "loop", 1)
+    keys[1] = both_sib
     keys = [keys[m] for m in range(loop_size)]
 
     def states_part():
@@ -393,7 +403,7 @@
             (shape((rows, width), F32),) + (shape((rows, width)),) * (len(even) - 1),
             *held,
             states,
-            states_sib,
+            both_sib,
             lse,
             qval,
             stats,
@@ -419,15 +429,16 @@
 
     def odd_core():
         held = message
-        for level in range(group_bits):
-            last = level == group_bits - 1
-            if level == 0:
+        order = [*range(group_bits - 2), group_bits - 1, group_bits - 2]
+        for step, level in enumerate(order):
+            last = step == group_bits - 1
+            if step == 0:
                 grad, far = premises_part(after(lse, held))
             other = swap(held, "groups", 1 << level)
-            if level == 0:
+            if step == 0:
                 other = after(other, grad, *far)
                 sent = send(far)
-            if level == 2:
+            if step == 2:
                 grad_states = states_part()
                 other = after(other, grad_states)
             held = call(

time: 29.4 us -> 29 us (0.986); the launches traced: 29.6 us -> 28.9 us
  starting transfers between devices: 14.1 us -> 13.5 us
    ppermute x9 -> x8, starting transfers between devices: 14.1 us -> 13.5 us  [swap(): return lax.ppermute(block, axis, [(i, i ^ mask) for i in range(count)])]
    ppermute x9 -> x8, waiting for transfers between devices: 6.83 us -> 6.7 us  [swap(): return lax.ppermute(block, axis, [(i, i ^ mask) for i in range(count)])]
    pallas_call x9 -> x10, Pallas kernels: 5.26 us -> 5.28 us  [call(): pl.pallas_call(kernel, out_shape=outs, in_specs=[ins.get(i, VMEM) for i i...]
  transfers between devices with their start and end apart: 9 -> 8, of which waited for: 5 -> 5; matrix products, arithmetic and copies ran while one was open for 0% -> 0% of each run, Pallas kernels for 7% -> 7%
where the time goes in v6:
time: 29 us; the launch traced here: 28.9 us
  starting transfers between devices  13.5 us (47%)
  waiting for transfers between devices  6.7 us (23%)
  Pallas kernels  5.28 us (18%)
  between operations  2.02 us (7%)
  loops' own time  0.75 us (3%)
  local copies, waits for them, and re-layouts  0.67 us (2%)
    ppermute x8, starting transfers between devices, swap(): return lax.ppermute(block, axis, [(i, i ^ mask) for i in range(count)])  13.5 us
    ppermute x8, waiting for transfers between devices, swap(): return lax.ppermute(block, axis, [(i, i ^ mask) for i in range(count)])  6.7 us
    pallas_call x10, Pallas kernels, call(): pl.pallas_call(kernel, out_shape=outs, in_specs=[ins.get(i, VMEM) for i i...  5.28 us
    another operation x1, loops' own time, body(): part, grad_states, grad_premises = lax.cond(odd == 1, odd_core, even_core)  0.68 us
    unnamed x8, local copies, waits for them, and re-layouts  0.66 us
  transfers between devices with their start and end apart: 8, of which 5 were waited for; matrix products, arithmetic and copies ran while one was open for 0% of the time, Pallas kernels for 7%

profile of v6, /device:TPU:0, one launch (start us, length us, event | category | flops | bytes accessed | tf_op | source)
XLA Modules:
  0.0 28.9 jit_solution(16991197462385466104)
XLA Ops:
  1.3 0.0 copy-start.3
  1.3 1.0 %mark.1.marked.refs_0_ = bf16[128,1024]{1,0:T(8,128)(2,1)S(1)} custom-call(bf16[128,1024]{1,0:T(8,128)(2,1)} %refs_0_.1, s32[1,1]{1,0:T(1,128)S(6)} %copy.31.count.refs_4_), custom_call_target="tpu_custom_call" | custom-call | tf_op jit(solution)/shard_map/mark/pallas_call | solution.py:30
  2.3 0.0 copy-done.3
  2.3 0.0 copy-start.2
  2.4 0.5 %collective-permute-start.20 = (bf16[256,1024]{1,0:T(8,128)(2,1)S(1)}, bf16[256,1024]{1,0:T(8,128)(2,1)S(1)}, u32[]{:S(2)}, u32[]{:S(2)}) collective-permute-start(bf16[256,1024]{1,0:T(8,128)(2,1)S(1)} %pair.1), channel_id=1, source_target_pairs={{0,8},{8,0},{16,24},{24,16},{1,9},{9,1},{17,25},{25,17},{2,10},{10... | collective-permute-start | bytes 1572872 | tf_op jit(solution)/shard_map/ppermute | solution.py:21
  2.9 2.6 %collective-permute-start.21 = (bf16[128,1024]{1,0:T(8,128)(2,1)S(1)}, bf16[128,1024]{1,0:T(8,128)(2,1)S(1)}, u32[]{:S(2)}, u32[]{:S(2)}) collective-permute-start(bf16[128,1024]{1,0:T(8,128)(2,1)S(1)} %mark.1.marked.refs_0_), channel_id=1, source_target_pairs={{0,16},{8,24},{16,0},{24,8},{1,17},{9,25},{17,1},{25,9},{2,18},{10... | collective-permute-start | bytes 786440 | tf_op jit(solution)/shard_map/ppermute | solution.py:21
  6.1 0.0 copy-start
  6.1 0.0 copy-start.1
  6.1 0.0 copy-done.2
  6.2 0.6 %copy-done = s32[1,1,16]{2,1,0:T(1,128)S(1)} copy-done((s32[1,1,16]{2,1,0:T(1,128)S(1)}, s32[1,1,16]{2,1,0:T(1,128)}, u32[]{:S(2)}) %copy-start) | copy-done | bytes 88
  6.8 0.0 copy-done.1
  6.8 0.3 front.1
  7.1 5.0 %conditional.3 = (bf16[16,1024]{1,0:T(8,128)(2,1)S(1)}) conditional(s32[]{:T(128)} %bitcast.1, bf16[16,1024]{1,0:T(8,128)(2,1)S(1)} %get-tuple-element.145, bf16[16,1024]{1,0:T(8,128)(2,1)S(1)} %get-tuple-element.145, bf16[16,1024]{1,0:T(8,128)(2,1)S(1)} %get-tuple-element.145, ...), branch_computations={%region_0.0_spmd, %region_1.0_spmd, %region_2.0_spmd, %region_3.0_... | conditional | bytes 196656 | solution.py:346
  7.1 2.7 %collective-permute-start.3 = (bf16[16,1024]{1,0:T(8,128)(2,1)S(1)}, bf16[16,1024]{1,0:T(8,128)(2,1)S(1)}, u32[]{:S(2)}, u32[]{:S(2)}) collective-permute-start(bf16[16,1024]{1,0:T(8,128)(2,1)S(1)} %param.4), channel_id=1, source_target_pairs={{0,4},{1,5},{2,6},{3,7},{4,0},{5,1},{6,2},{7,3},{8,12},{9,13},{10,... | collective-permute-start | bytes 98312 | tf_op jit(solution)/shard_map/cond/branch_4_fun/ppermute | solution.py:21
  9.8 2.3 %collective-permute-done.3 = bf16[16,1024]{1,0:T(8,128)(2,1)S(1)} collective-permute-done((bf16[16,1024]{1,0:T(8,128)(2,1)S(1)}, bf16[16,1024]{1,0:T(8,128)(2,1)S(1)}, u32[]{:S(2)}, u32[]{:S(2)}) %collective-permute-start.3) | collective-permute-done | bytes 32800 | tf_op jit(solution)/shard_map/cond/branch_4_fun/ppermute | solution.py:21
  12.0 0.3 %collective-permute-done.21.refs_1_ = bf16[128,1024]{1,0:T(8,128)(2,1)S(1)} collective-permute-done((bf16[128,1024]{1,0:T(8,128)(2,1)S(1)}, bf16[128,1024]{1,0:T(8,128)(2,1)S(1)}, u32[]{:S(2)}, u32[]{:S(2)}) %collective-permute-start.21) | collective-permute-done | bytes 262176 | tf_op jit(solution)/shard_map/ppermute | solution.py:21
  12.4 0.7 %collective-permute-start.22 = (bf16[128,1024]{1,0:T(8,128)(2,1)S(1)}, bf16[128,1024]{1,0:T(8,128)(2,1)S(1)}, u32[]{:S(2)}, u32[]{:S(2)}) collective-permute-start(bf16[128,1024]{1,0:T(8,128)(2,1)S(1)} %collective-permute-done.21.refs_1_), channel_id=1, source_target_pairs={{0,8},{8,0},{16,24},{24,16},{1,9},{9,1},{17,25},{25,17},{2,10},{10... | collective-permute-start | bytes 786440 | tf_op jit(solution)/shard_map/ppermute | solution.py:21
  13.1 0.0 collective-permute-done.20.sib
  13.1 0.6 %early.1 = (f32[8,256]{1,0:T(8,128)S(1)}, f32[128,128]{1,0:T(8,128)S(1)}) custom-call(bf16[128,1024]{1,0:T(8,128)(2,1)S(1)} %copy-done.3, bf16[256,1024]{1,0:T(8,128)(2,1)S(1)} %collective-permute-done.20.sib, bf16[16,1024]{1,0:T(8,128)(2,1)S(1)} %get-tuple-element.164.pool, s32[8,128]{1,0:T(8,128)S(1)} %get-tuple-element.147.meta, ...), custom_call_target="tpu_custom_call" | custom-call | tf_op jit(solution)/shard_map/early/pallas_call | solution.py:30
  13.7 0.1 collective-permute-start.23
  13.8 0.1 back.1
  14.0 1.0 %collective-permute-done.23.stats_sib = f32[8,256]{1,0:T(8,128)S(1)} collective-permute-done((f32[8,256]{1,0:T(8,128)S(1)}, f32[8,256]{1,0:T(8,128)S(1)}, u32[]{:S(2)}, u32[]{:S(2)}) %collective-permute-start.23) | collective-permute-done | bytes 8224 | tf_op jit(solution)/shard_map/ppermute | solution.py:21
  15.0 0.2 near.1
  15.2 0.0 collective-permute-done.22
  15.2 9.4 %conditional.4 = (f32[8,128]{1,0:T(8,128)S(1)}, bf16[128,1024]{1,0:T(8,128)(2,1)}, bf16[128,1024]{1,0:T(8,128)(2,1)}) conditional(s32[]{:T(128)} %convert_element_type.3, (bf16[128,1024]{1,0:T(8,128)(2,1)S(1)}, bf16[256,1024]{1,0:T(8,128)(2,1)S(1)}, bf16[128,1024]{1,0:T(8,128)(2,1)S(1)}, bf16[128,1024]{1,0:T(8,128)(2,1)S(1)}, ...), branch_computations={%region_8.0_spmd, %region_17.0_spmd} | conditional | flops 33999998976 | bytes 1519840 | solution.py:468
  15.2 0.8 %premises.3 = (f32[128,1024]{1,0:T(8,128)S(1)}, bf16[128,1024]{1,0:T(8,128)(2,1)S(1)}) custom-call(bf16[128,1024]{1,0:T(8,128)(2,1)S(1)} %get-tuple-element.99.refs_0_, bf16[128,1024]{1,0:T(8,128)(2,1)S(1)} %get-tuple-element.90.refs_2_.refs_1_, bf16[128,1024]{1,0:T(8,128)(2,1)S(1)} %get-tuple-element.92.refs_4_.refs_2_, ...), custom_call_target="tpu_custom_call" | custom-call | flops 16999999488 | tf_op jit(solution)/shard_map/cond/branch_0_fun/premises/pallas_call | solution.py:30
  16.0 1.2 %collective-permute-start.14 = (bf16[128,1024]{1,0:T(8,128)(2,1)S(1)}, bf16[128,1024]{1,0:T(8,128)(2,1)S(1)}, u32[]{:S(2)}, u32[]{:S(2)}) collective-permute-start(bf16[128,1024]{1,0:T(8,128)(2,1)S(1)} %get-tuple-element.104), channel_id=1, source_target_pairs={{0,16},{8,24},{16,0},{24,8},{1,17},{9,25},{17,1},{25,9},{2,18},{10... | collective-permute-start | bytes 786440 | tf_op jit(solution)/shard_map/cond/branch_0_fun/ppermute | solution.py:21
  17.2 0.8 %states.3.grad_states = bf16[128,1024]{1,0:T(8,128)(2,1)S(1)} custom-call(bf16[128,1024]{1,0:T(8,128)(2,1)S(1)} %get-tuple-element.88.refs_0_, bf16[256,1024]{1,0:T(8,128)(2,1)S(1)} %get-tuple-element.89.refs_1_.refs_3_, bf16[128,1024]{1,0:T(8,128)(2,1)S(1)} %get-tuple-element.90.refs_2_.refs_1_, bf16[128,1024]{1,0:T(8,128)(2,1)S(1)} %get-tuple-element.91.refs_3_, ...), custom_call_target="tpu_custom_call" | custom-call | flops 16999999488 | tf_op jit(solution)/shard_map/cond/branch_0_fun/states/pallas_call | solution.py:30
  18.6 4.9 %conditional = (bf16[16,1024]{1,0:T(8,128)(2,1)S(1)}) conditional(s32[]{:T(128)} %bitcast, bf16[16,1024]{1,0:T(8,128)(2,1)S(1)} %get-tuple-element.103, bf16[16,1024]{1,0:T(8,128)(2,1)S(1)} %get-tuple-element.103, bf16[16,1024]{1,0:T(8,128)(2,1)S(1)} %get-tuple-element.103, ...), branch_computations={%region_9.0_spmd, %region_10.0_spmd, %region_11.0_spmd, %region_12... | conditional | bytes 196656 | solution.py:462
  18.7 2.7 %collective-permute-start.10 = (bf16[16,1024]{1,0:T(8,128)(2,1)S(1)}, bf16[16,1024]{1,0:T(8,128)(2,1)S(1)}, u32[]{:S(2)}, u32[]{:S(2)}) collective-permute-start(bf16[16,1024]{1,0:T(8,128)(2,1)S(1)} %param.12), channel_id=1, source_target_pairs={{0,4},{1,5},{2,6},{3,7},{4,0},{5,1},{6,2},{7,3},{8,12},{9,13},{10,... | collective-permute-start | bytes 98312 | tf_op jit(solution)/shard_map/cond/branch_0_fun/cond/branch_4_fun/ppermute | solution.py:21
  21.3 2.3 %collective-permute-done.10 = bf16[16,1024]{1,0:T(8,128)(2,1)S(1)} collective-permute-done((bf16[16,1024]{1,0:T(8,128)(2,1)S(1)}, bf16[16,1024]{1,0:T(8,128)(2,1)S(1)}, u32[]{:S(2)}, u32[]{:S(2)}) %collective-permute-start.10) | collective-permute-done | bytes 32800 | tf_op jit(solution)/shard_map/cond/branch_0_fun/cond/branch_4_fun/ppermute | solution.py:21
  23.6 0.0 collective-permute-done.14.refs_0_
  23.6 0.9 %finish.2 = (bf16[128,1024]{1,0:T(8,128)(2,1)}, bf16[128,1024]{1,0:T(8,128)(2,1)}) custom-call(bf16[128,1024]{1,0:T(8,128)(2,1)S(1)} %states.3.grad_states, f32[128,1024]{1,0:T(8,128)S(1)} %get-tuple-element.100.grad, bf16[16,1024]{1,0:T(8,128)(2,1)S(1)} %get-tuple-element.163.home, s32[8,128]{1,0:T(8,128)S(1)} %get-tuple-element.95.refs_7_.meta, ...), custom_call_target="tpu_custom_call" | custom-call | tf_op jit(solution)/shard_map/cond/branch_0_fun/finish/pallas_call | solution.py:30
  24.5 3.1 %collective-permute-start.24 = (f32[8,128]{1,0:T(8,128)S(1)}, f32[8,128]{1,0:T(8,128)S(1)}, u32[]{:S(2)}, u32[]{:S(2)}) collective-permute-start(f32[8,128]{1,0:T(8,128)S(1)} %get-tuple-element.154.part), channel_id=1, source_target_pairs={{0,8},{8,0},{16,24},{24,16},{1,9},{9,1},{17,25},{25,17},{2,10},{10... | collective-permute-start | bytes 12296 | tf_op jit(solution)/shard_map/ppermute | solution.py:21
  27.6 0.8 %collective-permute-done.24.other = f32[8,128]{1,0:T(8,128)S(1)} collective-permute-done((f32[8,128]{1,0:T(8,128)S(1)}, f32[8,128]{1,0:T(8,128)S(1)}, u32[]{:S(2)}, u32[]{:S(2)}) %collective-permute-start.24) | collective-permute-done | bytes 4128 | tf_op jit(solution)/shard_map/ppermute | solution.py:21
  28.4 0.5 %loss.1 = f32[1,1]{1,0:T(1,128)} custom-call(f32[8,128]{1,0:T(8,128)S(1)} %get-tuple-element.154.part, f32[8,128]{1,0:T(8,128)S(1)} %collective-permute-done.24.other), custom_call_target="tpu_custom_call" | custom-call | tf_op jit(solution)/shard_map/loss/pallas_call | solution.py:30
  (4 shorter events, 0.0 us)
Async XLA Ops:
  1.3 1.0 %copy-start.3 = (bf16[128,1024]{1,0:T(8,128)(2,1)S(1)}, bf16[128,1024]{1,0:T(8,128)(2,1)}, u32[]{:S(2)}) copy-start(bf16[128,1024]{1,0:T(8,128)(2,1)} %states.6) | copy-start | bytes 786436
  2.3 3.8 %copy-start.2 = (bf16[128,1024]{1,0:T(8,128)(2,1)S(1)}, bf16[128,1024]{1,0:T(8,128)(2,1)}, u32[]{:S(2)}) copy-start(bf16[128,1024]{1,0:T(8,128)(2,1)} %refs_0_.1) | copy-start | bytes 786436
  2.4 10.7 %collective-permute-start.20 = (bf16[256,1024]{1,0:T(8,128)(2,1)S(1)}, bf16[256,1024]{1,0:T(8,128)(2,1)S(1)}, u32[]{:S(2)}, u32[]{:S(2)}) collective-permute-start(bf16[256,1024]{1,0:T(8,128)(2,1)S(1)} %pair.1), channel_id=1, source_target_pairs={{0,8},{8,0},{16,24},{24,16},{1,9},{9,1},{17,25},{25,17},{2,10},{10... | collective-permute-start | bytes 1572872 | tf_op jit(solution)/shard_map/ppermute | solution.py:21
  2.9 9.5 %collective-permute-start.21 = (bf16[128,1024]{1,0:T(8,128)(2,1)S(1)}, bf16[128,1024]{1,0:T(8,128)(2,1)S(1)}, u32[]{:S(2)}, u32[]{:S(2)}) collective-permute-start(bf16[128,1024]{1,0:T(8,128)(2,1)S(1)} %mark.1.marked.refs_0_), channel_id=1, source_target_pairs={{0,16},{8,24},{16,0},{24,8},{1,17},{9,25},{17,1},{25,9},{2,18},{10... | collective-permute-start | bytes 786440 | tf_op jit(solution)/shard_map/ppermute | solution.py:21
  6.1 0.7 %copy-start = (s32[1,1,16]{2,1,0:T(1,128)S(1)}, s32[1,1,16]{2,1,0:T(1,128)}, u32[]{:S(2)}) copy-start(s32[1,1,16]{2,1,0:T(1,128)} %param.28) | copy-start | bytes 196
  6.1 0.7 %copy-start.1 = (s32[128]{0:T(128)S(1)}, s32[128]{0:T(128)}, u32[]{:S(2)}) copy-start(s32[128]{0:T(128)} %param.29) | copy-start | bytes 1540
  7.1 4.9 %collective-permute-start.3 = (bf16[16,1024]{1,0:T(8,128)(2,1)S(1)}, bf16[16,1024]{1,0:T(8,128)(2,1)S(1)}, u32[]{:S(2)}, u32[]{:S(2)}) collective-permute-start(bf16[16,1024]{1,0:T(8,128)(2,1)S(1)} %param.4), channel_id=1, source_target_pairs={{0,4},{1,5},{2,6},{3,7},{4,0},{5,1},{6,2},{7,3},{8,12},{9,13},{10,... | collective-permute-start | bytes 98312 | tf_op jit(solution)/shard_map/cond/branch_4_fun/ppermute | solution.py:21
  12.4 2.8 %collective-permute-start.22 = (bf16[128,1024]{1,0:T(8,128)(2,1)S(1)}, bf16[128,1024]{1,0:T(8,128)(2,1)S(1)}, u32[]{:S(2)}, u32[]{:S(2)}) collective-permute-start(bf16[128,1024]{1,0:T(8,128)(2,1)S(1)} %collective-permute-done.21.refs_1_), channel_id=1, source_target_pairs={{0,8},{8,0},{16,24},{24,16},{1,9},{9,1},{17,25},{25,17},{2,10},{10... | collective-permute-start | bytes 786440 | tf_op jit(solution)/shard_map/ppermute | solution.py:21
  13.7 1.2 %collective-permute-start.23 = (f32[8,256]{1,0:T(8,128)S(1)}, f32[8,256]{1,0:T(8,128)S(1)}, u32[]{:S(2)}, u32[]{:S(2)}) collective-permute-start(f32[8,256]{1,0:T(8,128)S(1)} %get-tuple-element.148.stats), channel_id=1, source_target_pairs={{0,8},{8,0},{16,24},{24,16},{1,9},{9,1},{17,25},{25,17},{2,10},{10... | collective-permute-start | bytes 24584 | tf_op jit(solution)/shard_map/ppermute | solution.py:21
  16.0 7.6 %collective-permute-start.14 = (bf16[128,1024]{1,0:T(8,128)(2,1)S(1)}, bf16[128,1024]{1,0:T(8,128)(2,1)S(1)}, u32[]{:S(2)}, u32[]{:S(2)}) collective-permute-start(bf16[128,1024]{1,0:T(8,128)(2,1)S(1)} %get-tuple-element.104), channel_id=1, source_target_pairs={{0,16},{8,24},{16,0},{24,8},{1,17},{9,25},{17,1},{25,9},{2,18},{10... | collective-permute-start | bytes 786440 | tf_op jit(solution)/shard_map/cond/branch_0_fun/ppermute | solution.py:21
  18.7 4.9 %collective-permute-start.10 = (bf16[16,1024]{1,0:T(8,128)(2,1)S(1)}, bf16[16,1024]{1,0:T(8,128)(2,1)S(1)}, u32[]{:S(2)}, u32[]{:S(2)}) collective-permute-start(bf16[16,1024]{1,0:T(8,128)(2,1)S(1)} %param.12), channel_id=1, source_target_pairs={{0,4},{1,5},{2,6},{3,7},{4,0},{5,1},{6,2},{7,3},{8,12},{9,13},{10,... | collective-permute-start | bytes 98312 | tf_op jit(solution)/shard_map/cond/branch_0_fun/cond/branch_4_fun/ppermute | solution.py:21
  24.5 3.9 %collective-permute-start.24 = (f32[8,128]{1,0:T(8,128)S(1)}, f32[8,128]{1,0:T(8,128)S(1)}, u32[]{:S(2)}, u32[]{:S(2)}) collective-permute-start(f32[8,128]{1,0:T(8,128)S(1)} %get-tuple-element.154.part), channel_id=1, source_target_pairs={{0,8},{8,0},{16,24},{24,16},{1,9},{9,1},{17,25},{25,17},{2,10},{10... | collective-permute-start | bytes 12296 | tf_op jit(solution)/shard_map/ppermute | solution.py:21
